TPU v7x, 256 devices: a whole 4x4x8 slice. The times are simulated.
256 devices in a mesh: depth: 8 (over x_lo, y), row: 16 (over z, x_hi), col: 2 (over core).
Axes of the slice: x: 4 (x_hi: 2, x_lo: 2; x = x_hi * 2 + x_lo), y: 4, z: 8, core: 2. Of those that a mesh axis runs over, the one named last changes fastest.
Arguments:
- phase: float32 [4096, 4096], P(('row', 'col')), may hold values from -3.140625 to 3.140625
- depths: int32 [8], P('depth'), may hold values from 0 to 63
- targets: float32 [8, 4096, 4096], P('depth', ('row', 'col')), may hold values from 0.1 to 3
Outputs:
- gradient: float32 [4096, 4096], P(('row', 'col'))
All inputs are finite; a program needn't handle non-finite values.
Results may differ from a plain program's by a relative error of at most 0.0003.
Values sent between devices are 32-bit elements; how exact they have to be, the bound alone decides.
No kernel may reach another device: no remote copies, remote signals or barrier semaphores. Data moves between devices by JAX's collectives and lax.ppermute only.
A program may use at most 128 MiB of HBM per device.

v0:
```python
import math

import jax
import jax.numpy as jnp
from jax import lax
from jax.sharding import PartitionSpec as P


def angles(count_left, count_right, modulus, direction_sign):
    left_idx = jnp.arange(count_left, dtype=jnp.int32)[:, None]
    right_idx = jnp.arange(count_right, dtype=jnp.int32)[None, :]
    turned = (left_idx * right_idx % modulus).astype(jnp.float32) * (
        direction_sign * 2.0 * math.pi / modulus
    )
    return (jnp.cos(turned), jnp.sin(turned))


def block_table(table_cos, table_sin, factor):
    upper = jnp.stack([table_cos, table_sin])
    lower = jnp.stack([-table_sin, table_cos])
    return jnp.stack([upper, lower]) * factor


def stacked_dot(values, table, pattern):
    return jnp.einsum(pattern, values, table, precision=lax.Precision.HIGHEST)


def twist(values, table_cos, table_sin):
    real_part = values[0]
    imag_part = values[1]
    return jnp.stack(
        [
            real_part * table_cos - imag_part * table_sin,
            real_part * table_sin + imag_part * table_cos,
        ]
    )


def lines(values, trailing, inverse):
    old_shape = values.shape
    if trailing:
        length = old_shape[-2]
        leading = old_shape[:-2]
        extra_dims = (old_shape[-1],)
    else:
        length = old_shape[-1]
        leading = old_shape[:-1]
        extra_dims = ()
    inner_size = 128
    outer_size = length // inner_size
    values = values.reshape(leading + (outer_size, inner_size) + extra_dims)
    direction_sign = 1.0 if inverse else -1.0
    outer_cos, outer_sin = angles(outer_size, outer_size, outer_size, direction_sign)
    inner_cos, inner_sin = angles(inner_size, inner_size, inner_size, direction_sign)
    twid_cos, twid_sin = angles(outer_size, inner_size, length, direction_sign)
    if trailing:
        twid_cos = twid_cos[:, :, None]
        twid_sin = twid_sin[:, :, None]
    if inverse:
        inner_table = block_table(inner_cos, inner_sin, 1.0)
        outer_table = block_table(outer_cos, outer_sin, 1.0 / length)
        values = stacked_dot(
            values, inner_table, "t...klc,tslq->s...kqc" if trailing else "t...kl,tslq->s...kq"
        )
        values = twist(values, twid_cos, twid_sin)
        values = stacked_dot(
            values, outer_table, "t...kqc,tskp->s...pqc" if trailing else "t...kq,tskp->s...pq"
        )
    else:
        inner_table = block_table(inner_cos, inner_sin, 1.0)
        outer_table = block_table(outer_cos, outer_sin, 1.0)
        values = stacked_dot(
            values, outer_table, "t...pqc,tspk->s...kqc" if trailing else "t...pq,tspk->s...kq"
        )
        values = twist(values, twid_cos, twid_sin)
        values = stacked_dot(
            values, inner_table, "t...kqc,tsql->s...klc" if trailing else "t...kq,tsql->s...kl"
        )
    return values.reshape(old_shape)


def frequency_squares(position, length):
    freq = position // 128 + length // 128 * (position % 128)
    centered = jnp.where(freq < length // 2, freq, freq - length)
    return centered * centered % (2 * length)


def line_phase(depths, squares_now, length):
    strength = ((depths + 8) * (length // 64) + 1) % (2 * length)
    turned = (strength[:, None] * squares_now[None, :] % (2 * length)).astype(jnp.float32) * (
        -math.pi / length
    )
    return (jnp.cos(turned), jnp.sin(turned))


def transfer(depths, length, column_block, columns):
    first_sq = frequency_squares(jnp.arange(length, dtype=jnp.int32), length)
    second_sq = frequency_squares(
        column_block * columns + jnp.arange(columns, dtype=jnp.int32), length
    )
    first_cos, first_sin = line_phase(depths, first_sq, length)
    second_cos, second_sin = line_phase(depths, second_sq, length)
    first_cos = first_cos[:, :, None]
    first_sin = first_sin[:, :, None]
    second_cos = second_cos[:, None, :]
    second_sin = second_sin[:, None, :]
    return (
        first_cos * second_cos - first_sin * second_sin,
        first_cos * second_sin + first_sin * second_cos,
    )


def apply_kernel(values, kern_cos, kern_sin):
    real_part = values[0]
    imag_part = values[1]
    return jnp.stack(
        [real_part * kern_cos - imag_part * kern_sin, real_part * kern_sin + imag_part * kern_cos]
    )


def to_columns(values):
    return lax.all_to_all(values, ("row", "col"), split_axis=3, concat_axis=2, tiled=True)


def to_rows(values):
    return lax.all_to_all(values, ("row", "col"), split_axis=2, concat_axis=3, tiled=True)


def on_device(phase, depths, targets):
    rows_dev, length = phase.shape
    groups = lax.axis_size("row") * lax.axis_size("col")
    columns = length // groups
    column_block = lax.axis_index("row") * lax.axis_size("col") + lax.axis_index("col")
    planes_total = depths.shape[0] * lax.axis_size("depth")
    cos_phase = jnp.cos(phase)
    sin_phase = jnp.sin(phase)
    spectrum = lines(jnp.stack([cos_phase, sin_phase])[:, None], False, False)
    spectrum = to_columns(spectrum)
    spectrum = lines(spectrum, True, False)
    kern_cos, kern_sin = transfer(depths, length, column_block, columns)
    field = lines(apply_kernel(spectrum, kern_cos, kern_sin), True, True)
    field = to_rows(field)
    field = lines(field, False, True)
    intensity = field[0] * field[0] + field[1] * field[1]
    residual = 4.0 / planes_total * (intensity - targets)
    wave = lines(field * residual[None], False, False)
    wave = to_columns(wave)
    wave = lines(wave, True, False)
    adjoint = jnp.sum(apply_kernel(wave, kern_cos, -kern_sin), axis=1, keepdims=True)
    adjoint = lax.psum(adjoint, "depth")
    adjoint = lines(adjoint, True, True)
    adjoint = to_rows(adjoint)
    adjoint = lines(adjoint, False, True)
    gradient = adjoint[1, 0] * cos_phase - adjoint[0, 0] * sin_phase
    return gradient


def solution(mesh):
    placed = (P(("row", "col"), None), P("depth"), P("depth", ("row", "col"), None))
    return jax.shard_map(
        on_device, mesh=mesh, in_specs=placed, out_specs=P(("row", "col"), None), check_vma=False
    )
```

profile of v0, /device:TPU:4, one launch (start us, length us, event | category | flops | bytes accessed | tf_op | source)
XLA Modules:
  0.0 777.3 jit_solution(13962992368284442715)
XLA Ops:
  7.3 8.4 %fusion.167 = (f32[128,4096]{1,0:T(8,128)S(1)}, f32[128,4096]{1,0:T(8,128)S(1)}) fusion(f32[128,4096]{1,0:T(8,128)} %param.3), kind=kLoop, calls=%fused_computation.251 | loop fusion | bytes 6291456 | tf_op jit(solution)/shard_map/cos | solution.py:135
  22.4 6.1 fusion.33
  28.6 26.9 %copy.64 = f32[2,1,128,4096]{2,0,1,3:T(2,128)} copy(f32[2,1,128,4096]{2,3,0,1:T(8,128)S(1)} %bitcast.331) | data formatting | bytes 8388608 | tf_op jit(solution)/shard_map/reshape | solution.py:79
  55.5 11.7 %all-to-all-start = ((f32[2,1,128,4096]{2,0,1,3:T(2,128)}), f32[2,1,128,4096]{2,0,1,3:T(2,128)}, u32[]{:S(2)}, u32[]{:S(2)}) async-start(f32[2,1,128,4096]{2,0,1,3:T(2,128)} %copy.64), calls=%async_computation | async-start | bytes 8388608 | tf_op jit(solution)/shard_map/all_to_all | solution.py:122
  69.1 92.2 %all-to-all-done = f32[2,1,128,4096]{2,0,1,3:T(2,128)} async-done(((f32[2,1,128,4096]{2,0,1,3:T(2,128)}), f32[2,1,128,4096]{2,0,1,3:T(2,128)}, u32[]{:S(2)}, u32[]{:S(2)}) %all-to-all-start) | async-done | bytes 4194336 | tf_op jit(solution)/shard_map/all_to_all | solution.py:122
  161.3 5.6 copy.142
  166.9 5.4 fusion.70
  174.2 6.2 fusion.43
  182.3 4.1 fusion.46
  188.3 6.0 fusion.49
  196.7 15.6 %copy.74 = f32[2,1,4096,128]{3,0,1,2:T(2,128)S(1)} copy(f32[2,1,4096,128]{3,2,0,1:T(8,128)S(1)} %bitcast.337) | data formatting | bytes 8388608 | tf_op jit(solution)/shard_map/reshape;t...kqc,tskp->s...pqc/transpose | solution.py:79
  212.4 103.8 %all_to_all.60 = f32[2,1,4096,128]{3,0,1,2:T(2,128)S(1)} all-to-all(f32[2,1,4096,128]{3,0,1,2:T(2,128)S(1)} %copy.74), channel_id=1, replica_groups=mesh['depth'=8,'row'=16,'col'=2] {'row','col'}, dimensions={2} | all-to-all | bytes 8388608 | tf_op jit(solution)/shard_map/all_to_all | solution.py:126
  316.1 4.2 fusion.73
  324.0 5.5 copy.79
  329.5 5.4 fusion.52
  346.5 3.9 fusion.55
  351.5 6.1 fusion.20
  357.6 16.7 %copy.82 = f32[2,1,128,4096]{2,0,1,3:T(2,128)} copy(f32[2,1,128,4096]{2,3,0,1:T(8,128)S(1)} %bitcast.332) | data formatting | bytes 8388608 | tf_op jit(solution)/shard_map/reshape | solution.py:79
  374.3 5.1 all-to-all-start.2
  379.5 93.9 %all-to-all-done.2 = f32[2,1,128,4096]{2,0,1,3:T(2,128)} async-done(((f32[2,1,128,4096]{2,0,1,3:T(2,128)}), f32[2,1,128,4096]{2,0,1,3:T(2,128)}, u32[]{:S(2)}, u32[]{:S(2)}) %all-to-all-start.2) | async-done | bytes 4194336 | tf_op jit(solution)/shard_map/all_to_all | solution.py:122
  473.5 5.6 copy.145
  479.1 5.4 fusion.76
  486.5 5.9 fusion.58
  497.2 109.1 %all-reduce.2.cloned.1.call-done = f32[2,32,128,128]{3,2,0,1:T(8,128)} async-done(((f32[2,32,128,128]{3,2,0,1:T(8,128)}), f32[2,32,128,128]{3,2,0,1:T(8,128)}) %all-reduce.2.cloned.1.call-update) | async-done | bytes 4194320 | tf_op jit(solution)/shard_map/psum | solution.py:150
  606.2 5.6 fusion.61
  613.7 6.0 fusion.64
  622.1 15.6 %copy.94 = f32[2,1,4096,128]{3,0,1,2:T(2,128)S(1)} copy(f32[2,1,4096,128]{3,2,0,1:T(8,128)S(1)} %bitcast.339) | data formatting | bytes 8388608 | tf_op jit(solution)/shard_map/reshape;t...kqc,tskp->s...pqc/transpose | solution.py:79
  637.8 106.5 %all_to_all.61 = f32[2,1,4096,128]{3,0,1,2:T(2,128)S(1)} all-to-all(f32[2,1,4096,128]{3,0,1,2:T(2,128)S(1)} %copy.94), channel_id=1, replica_groups=mesh['depth'=8,'row'=16,'col'=2] {'row','col'}, dimensions={2} | all-to-all | bytes 8388608 | tf_op jit(solution)/shard_map/all_to_all | solution.py:126
  744.3 4.2 fusion.79
  752.1 5.5 copy.99
  757.7 5.4 fusion.67
  764.7 5.4 fusion.83
  (60 shorter events, 49.1 us)
Async XLA Ops:
  15.7 1.3 copy-start.2
  55.5 105.7 %all-to-all-start = ((f32[2,1,128,4096]{2,0,1,3:T(2,128)}), f32[2,1,128,4096]{2,0,1,3:T(2,128)}, u32[]{:S(2)}, u32[]{:S(2)}) async-start(f32[2,1,128,4096]{2,0,1,3:T(2,128)} %copy.64), calls=%async_computation | async-start | bytes 8388608 | tf_op jit(solution)/shard_map/all_to_all | solution.py:122
  335.0 2.0 copy-start
  344.3 2.2 copy-start.1
  374.3 99.1 %all-to-all-start.2 = ((f32[2,1,128,4096]{2,0,1,3:T(2,128)}), f32[2,1,128,4096]{2,0,1,3:T(2,128)}, u32[]{:S(2)}, u32[]{:S(2)}) async-start(f32[2,1,128,4096]{2,0,1,3:T(2,128)} %copy.82), calls=%async_computation.2 | async-start | bytes 8388608 | tf_op jit(solution)/shard_map/all_to_all | solution.py:122
  379.4 226.8 %all-reduce.2.cloned.1.call-start = ((), (), s32[]{:S(2)}) async-start(), calls=%async_computation.4 | async-start | bytes 8388608 | tf_op jit(solution)/shard_map/psum | solution.py:150
  763.1 1.6 copy-start.3
Sparse Core Ops, SparseCore 0:
  497.3 108.9 all-reduce.1
where the time goes:
time: 788 us; the launch traced here: 777 us
  waiting for transfers between devices  295 us (37%)
  blocking collectives  210 us (27%)
  local copies, waits for them, and re-layouts  124 us (16%)
  matrix products  83.9 us (11%)
  other arithmetic  32.5 us (4%)
  starting transfers between devices  16.8 us (2%)
  between operations  14.9 us (2%)
    all_to_all x2, blocking collectives, to_rows(): lax.all_to_all(values, ('row', 'col'), split_axis=2, concat_axis=3, tiled...  210 us
    all_to_all x2, waiting for transfers between devices, to_columns(): lax.all_to_all(values, ('row', 'col'), split_axis=3, concat_axis=2, tiled...  186 us
    psum x1, waiting for transfers between devices, on_device(): adjoint = lax.psum(adjoint, 'depth')  109 us
    dot_general x16, matrix products, stacked_dot(): return jnp.einsum(pattern, values, table, precision=lax.Precision.HIGHEST)  83.9 us
    reshape x2, local copies, waits for them, and re-layouts, lines(): return values.reshape(old_shape)  43.6 us
    transpose x2, local copies, waits for them, and re-layouts, lines(): return values.reshape(old_shape)  31.3 us
    all_to_all x2, starting transfers between devices, to_columns(): lax.all_to_all(values, ('row', 'col'), split_axis=3, concat_axis=2, tiled...  16.7 us
  transfers between devices with their start and end apart: 3, of which 3 were waited for; matrix products, arithmetic and copies ran while one was open for 0% of the time, Pallas kernels for 0%

commit v1 on v0

v1 whole, which is shorter than its diff:
```python
import math

import jax
import jax.numpy as jnp
import numpy as np
from jax import lax
from jax.experimental import pallas as pl
from jax.experimental.pallas import tpu as pltpu
from jax.sharding import Mesh
from jax.sharding import PartitionSpec as P

SLAB = ("xl", "y", "xh", "c")
OUTER = 32
INNER = 128
BLOCK = 16
F32 = jnp.float32
BF16 = jnp.bfloat16


def fit(function, count, odd):
    points = np.cos(np.pi * (np.arange(400) + 0.5) / 400) * 0.5
    powers = np.stack([points ** (2 * k + odd) for k in range(count)], axis=1)
    return [float(c) for c in np.linalg.lstsq(powers, function(np.pi * points), rcond=None)[0]]


SIN_TERMS = fit(np.sin, 6, 1)
COS_TERMS = fit(np.cos, 6, 0)


def horner(terms, square):
    total = jnp.full_like(square, terms[-1])
    for term in terms[-2::-1]:
        total = total * square + term
    return total


def unit_wave(turns):
    turns = turns - jnp.round(turns)
    square = turns * turns
    half_sin = turns * horner(SIN_TERMS, square)
    half_cos = horner(COS_TERMS, square)
    twice = half_sin + half_sin
    return 1.0 - twice * half_sin, twice * half_cos


def spin(value, step, size, sign):
    real, imag = value
    step = step % size
    if step == 0:
        return value
    if 4 * step == size:
        return (-imag, real) if sign > 0 else (imag, -real)
    if 2 * step == size:
        return (-real, -imag)
    if 4 * step == 3 * size:
        return (imag, -real) if sign > 0 else (-imag, real)
    cos = math.cos(2 * math.pi * step / size)
    sin = sign * math.sin(2 * math.pi * step / size)
    if 8 * step % size == 0 and abs(abs(cos) - abs(sin)) < 1e-9:
        root = abs(cos)
        real, imag = real * root, imag * root
        cs = 1 if cos > 0 else -1
        ss = 1 if sin > 0 else -1
        a = real if cs > 0 else -real
        new_real = a - imag if ss > 0 else a + imag
        b = imag if cs > 0 else -imag
        new_imag = b + real if ss > 0 else b - real
        return new_real, new_imag
    return real * cos - imag * sin, real * sin + imag * cos


def small_dft(values, sign):
    size = len(values)
    if size == 1:
        return values
    even = small_dft(values[0::2], sign)
    odd = small_dft(values[1::2], sign)
    low, high = [], []
    for k in range(size // 2):
        turned = spin(odd[k], k, size, sign)
        low.append((even[k][0] + turned[0], even[k][1] + turned[1]))
        high.append((even[k][0] - turned[0], even[k][1] - turned[1]))
    return low + high


def dft32(load, store, mid_ref, sign):
    for b in range(8):
        out = small_dft([load(8 * a + b) for a in range(4)], sign)
        for p in range(4):
            real, imag = spin(out[p], b * p, 32, sign)
            mid_ref[8 * p + b, 0] = real
            mid_ref[8 * p + b, 1] = imag
    for p in range(4):
        out = small_dft([(mid_ref[8 * p + b, 0], mid_ref[8 * p + b, 1]) for b in range(8)], sign)
        for s in range(8):
            store(p + 4 * s, out[s])


def split(value):
    high = value.astype(BF16)
    return high, (value - high.astype(F32)).astype(BF16)


def dot(left, right):
    return jnp.dot(left, right, preferred_element_type=F32)


def row_block(step):
    return pl.ds(pl.multiple_of(step * BLOCK, BLOCK), BLOCK)


def tile(index):
    return slice(index * INNER, (index + 1) * INNER)


def sort_kernel(target_ref, out_ref, turned_ref):
    for k in range(OUTER):
        turned_ref[tile(k), :] = target_ref[:, tile(k)].T
    for j in range(OUTER):
        out_ref[j] = turned_ref[pl.ds(j, INNER, stride=OUTER), :].T


def rows_kernel(phase_ref, row_ref, col_ref, tw_ref, dft_ref, out_ref, wave_ref, high_ref, low_ref, mid_ref, sh_ref, sl_ref):
    high_ref[...], low_ref[...] = split(dft_ref[...])

    def block(step, carry):
        rows = row_block(step)
        row_turn = row_ref[rows, :]

        def load(k):
            turns = phase_ref[rows, tile(k)] * (0.5 / math.pi) + (row_turn + col_ref[:, tile(k)])
            cos, sin = unit_wave(turns)
            wave_ref[0, rows, tile(k)] = cos
            wave_ref[1, rows, tile(k)] = sin
            return cos, sin

        def store(k, value):
            cos, sin = tw_ref[0, k : k + 1, :], tw_ref[1, k : k + 1, :]
            real, imag = value
            for part, side in ((real * cos - imag * sin, 0), (real * sin + imag * cos, 1)):
                high, low = split(part)
                sh_ref[k, rows, tile(side)] = high
                sl_ref[k, rows, tile(side)] = low

        dft32(load, store, mid_ref, -1)
        return carry

    lax.fori_loop(0, INNER // BLOCK, block, 0)

    def multiply(step, carry):
        group = pl.ds(step * 4, 4)
        high = sh_ref[group].reshape(4 * INNER, 2 * INNER)
        low = sl_ref[group].reshape(4 * INNER, 2 * INNER)
        out = dot(high, high_ref[...]) + dot(low, high_ref[...]) + dot(high, low_ref[...])
        out = out.reshape(4, INNER, 2 * INNER)
        out_ref[group, 0] = out[:, :, :INNER]
        out_ref[group, 1] = out[:, :, INNER:]
        return carry

    lax.fori_loop(0, OUTER // 4, multiply, 0)


def columns_kernel(
    scale, in_ref, target_ref, tw_ref, there_ref, home_ref, out_ref,
    fh_ref, fl_ref, bh_ref, bl_ref, mid_ref, sh_ref, sl_ref, back_ref,
):
    fh_ref[...], fl_ref[...] = split(home_ref[...])
    bh_ref[...], bl_ref[...] = split(there_ref[...])

    def forward(step, carry):
        rows = row_block(step)

        def load(k):
            return tuple(in_ref[step * 4 + k % 4, side, tile_rows(k // 4), :] for side in (0, 1))

        def store(k, value):
            cos, sin = tw_ref[0, k, rows, :], tw_ref[1, k, rows, :]
            real, imag = value
            for part, side in ((real * cos - imag * sin, 0), (real * sin + imag * cos, 1)):
                high, low = split(part)
                sh_ref[k, side, rows, :] = high
                sl_ref[k, side, rows, :] = low

        dft32(load, store, mid_ref, -1)
        return carry

    lax.fori_loop(0, INNER // BLOCK, forward, 0)

    def pair(ref, first):
        return jnp.concatenate([ref[first + k].reshape(2 * INNER, INNER) for k in (0, 1)], axis=1)

    def multiply(step, carry):
        first = step * 2
        high, low = pair(sh_ref, first), pair(sl_ref, first)
        field = dot(fh_ref[...], high) + dot(fh_ref[...], low) + dot(fl_ref[...], high)
        real, imag = field[:INNER], field[INNER:]
        target = jnp.concatenate(
            [target_ref[pl.ds(first + k, INNER, stride=OUTER), :] for k in (0, 1)], axis=1
        )
        residual = scale * (real * real + imag * imag - target)
        high, low = split(jnp.concatenate([residual * real, residual * imag], axis=0))
        back = dot(bh_ref[...], high) + dot(bh_ref[...], low) + dot(bl_ref[...], high)
        for k in (0, 1):
            back_ref[first + k] = back[:, tile(k)].reshape(2, INNER, INNER)
        return carry

    lax.fori_loop(0, OUTER // 2, multiply, 0)

    def backward(step, carry):
        rows = row_block(step)

        def load(k):
            cos, sin = tw_ref[0, k, rows, :], tw_ref[1, k, rows, :]
            real, imag = back_ref[k, 0, rows, :], back_ref[k, 1, rows, :]
            return real * cos + imag * sin, imag * cos - real * sin

        def store(k, value):
            for side in (0, 1):
                out_ref[step * 4 + k % 4, side, tile_rows(k // 4), :] = value[side]

        dft32(load, store, mid_ref, 1)
        return carry

    lax.fori_loop(0, INNER // BLOCK, backward, 0)


def tile_rows(index):
    return slice(index * BLOCK, (index + 1) * BLOCK)


def gradient_kernel(in_ref, wave_ref, tw_ref, dft_ref, out_ref, high_ref, low_ref, mid_ref, back_ref):
    high_ref[...], low_ref[...] = split(dft_ref[...])

    def multiply(step, carry):
        group = pl.ds(step * 4, 4)
        both = jnp.concatenate([in_ref[group, 0], in_ref[group, 1]], axis=-1).reshape(4 * INNER, 2 * INNER)
        high, low = split(both)
        out = dot(high, high_ref[...]) + dot(low, high_ref[...]) + dot(high, low_ref[...])
        back_ref[group] = out.reshape(4, INNER, 2 * INNER)
        return carry

    lax.fori_loop(0, OUTER // 4, multiply, 0)

    def block(step, carry):
        rows = row_block(step)

        def load(k):
            cos, sin = tw_ref[0, k : k + 1, :], tw_ref[1, k : k + 1, :]
            real, imag = back_ref[k, rows, tile(0)], back_ref[k, rows, tile(1)]
            return real * cos + imag * sin, imag * cos - real * sin

        def store(k, value):
            out_ref[rows, tile(k)] = value[1] * wave_ref[0, rows, tile(k)] - value[0] * wave_ref[1, rows, tile(k)]

        dft32(load, store, mid_ref, 1)
        return carry

    lax.fori_loop(0, INNER // BLOCK, block, 0)


def call(kernel, out_shapes, scratch, *args):
    return pl.pallas_call(
        kernel,
        out_shape=[jax.ShapeDtypeStruct(shape, F32) for shape in out_shapes],
        in_specs=[pl.BlockSpec(memory_space=pltpu.VMEM)] * len(args),
        out_specs=[pl.BlockSpec(memory_space=pltpu.VMEM)] * len(out_shapes),
        scratch_shapes=[pltpu.VMEM(shape, dtype) for shape, dtype in scratch],
        compiler_params=pltpu.CompilerParams(vmem_limit_bytes=40 * 2**20),
    )(*args)


def inverse_odd(value, modulus):
    result = value
    for _ in range(4):
        result = result * ((2 - value * result) % modulus) % modulus
    return result


def turns_of(steps, modulus):
    return steps.astype(F32) * (1.0 / modulus)


def table(weight, length, sign):
    index = jnp.arange(INNER, dtype=jnp.int32)
    steps = (index[:, None] * index[None, :] % INNER) * (weight % INNER) % INNER
    angle = steps.astype(F32) * (sign * 2.0 * math.pi / INNER)
    cos, sin = jnp.cos(angle) / math.sqrt(length), jnp.sin(angle) / math.sqrt(length)
    return jnp.block([[cos, sin], [-sin, cos]])


def on_device(phase, depths, targets):
    rows_dev, length = phase.shape
    planes = lax.axis_size("xl") * lax.axis_size("y")
    layers = lax.axis_size("z")
    place = lax.axis_index("xl") * lax.axis_size("y") + lax.axis_index("y")
    slab_size = math.prod(lax.axis_size(axis) for axis in SLAB)
    modulus = 2 * length

    share = rows_dev // planes
    mine = lax.dynamic_slice_in_dim(phase, place * share, share, 0)
    rows_phase = lax.all_gather(mine, "z", axis=0, tiled=True)

    all_depths = lax.all_gather(depths, ("xl", "y"), axis=0, tiled=True)
    depth = lax.dynamic_index_in_dim(all_depths, lax.axis_index("z"), keepdims=False)
    (sorted_targets,) = call(
        sort_kernel,
        [(slab_size, rows_dev, INNER)],
        [((length, rows_dev), F32)],
        targets[0],
    )
    sorted_targets = lax.all_to_all(sorted_targets, SLAB, 0, 0, tiled=True)
    sorted_targets = lax.all_to_all(sorted_targets, "z", 0, 0, tiled=True).reshape(length, INNER)

    strength = ((depth + 8) * (length // 64) + 1) % modulus
    weight = inverse_odd(strength, modulus)

    pixel = jnp.arange(length, dtype=jnp.int32)
    chirp = turns_of(pixel * pixel % modulus * weight % modulus, modulus)
    slot = lax.axis_index("xh") * lax.axis_size("c") + lax.axis_index("c")
    local = jnp.arange(layers * share, dtype=jnp.int32)
    row = (local // share * (length // layers)) + slot * rows_dev + place * share + local % share
    row_chirp = turns_of(row * row % modulus * weight % modulus, modulus)
    row_chirp = jnp.broadcast_to(row_chirp[:, None], (layers * share, INNER))

    outer = jnp.arange(OUTER, dtype=jnp.int32)[:, None]
    inner = jnp.arange(INNER, dtype=jnp.int32)[None, :]
    angle = (outer * inner * weight % length).astype(F32) * (-2.0 * math.pi / length)
    twiddle = jnp.stack([jnp.cos(angle), jnp.sin(angle)])
    tall_twiddle = jnp.broadcast_to(twiddle[:, :, :, None], (2, OUTER, INNER, INNER))
    there = table(weight, length, -1.0)
    back = table(weight, length, 1.0)

    mid = ((OUTER, 2, BLOCK, INNER), F32)
    matrix = ((2 * INNER, 2 * INNER), BF16)
    chunks = (slab_size, 2, layers * share, INNER)
    spectrum, wave = call(
        rows_kernel,
        [chunks, (2, layers * share, length)],
        [matrix, matrix, mid, ((OUTER, INNER, 2 * INNER), BF16), ((OUTER, INNER, 2 * INNER), BF16)],
        rows_phase,
        row_chirp,
        chirp[None, :],
        twiddle,
        there,
    )
    spectrum = lax.all_to_all(spectrum, SLAB, 0, 0, tiled=True)
    (spectrum,) = call(
        lambda *refs: columns_kernel(4.0 / planes, *refs),
        [chunks],
        [
            matrix,
            matrix,
            matrix,
            matrix,
            mid,
            ((OUTER, 2, INNER, INNER), BF16),
            ((OUTER, 2, INNER, INNER), BF16),
            ((OUTER, 2, INNER, INNER), F32),
        ],
        spectrum,
        sorted_targets,
        tall_twiddle,
        there,
        back,
    )
    spectrum = lax.all_to_all(spectrum, SLAB, 0, 0, tiled=True)
    (part,) = call(
        gradient_kernel,
        [(layers * share, length)],
        [matrix, matrix, mid, ((OUTER, INNER, 2 * INNER), F32)],
        spectrum,
        wave,
        twiddle,
        back,
    )
    part = lax.psum_scatter(part, "z", scatter_dimension=0, tiled=True)
    part = jnp.broadcast_to(part[None], (planes, share, length))
    return lax.all_to_all(part, ("xl", "y"), 0, 0, tiled=True).reshape(rows_dev, length)


def solution(mesh):
    fine = Mesh(mesh.devices.reshape(2, 4, 8, 2, 2), ("xl", "y", "z", "xh", "c"))
    rows = ("z", "xh", "c")
    placed = (P(rows, None), P(("xl", "y")), P(("xl", "y"), rows, None))
    return jax.shard_map(on_device, mesh=fine, in_specs=placed, out_specs=P(rows, None), check_vma=False)
```

time: 788 us -> 330 us (0.42); the launches traced: 777 us -> 329 us
  waiting for transfers between devices: 295 us -> 140 us
  blocking collectives: 210 us -> 97.9 us
  local copies, waits for them, and re-layouts: 124 us -> 17.7 us
  matrix products: 83.9 us -> 0 us
  Pallas kernels: 0 us -> 33.1 us
  other arithmetic: 32.5 us -> 1.49 us
    all_to_all x2, blocking collectives: 210 us -> 85 us  [the longest x1 57.2 us: on_device(): spectrum = lax.all_to_all(spectrum, SLAB, 0, 0, tiled=True)]
    psum x1 -> x0, waiting for transfers between devices: 109 us -> none  [on_device(): adjoint = lax.psum(adjoint, 'depth')]
    all_to_all x2 -> x3, waiting for transfers between devices: 186 us -> 89.3 us  [the longest x1 51.3 us: on_device(): spectrum = lax.all_to_all(spectrum, SLAB, 0, 0, tiled=True)]
    dot_general x16 -> x0, matrix products: 83.9 us -> none  [stacked_dot(): return jnp.einsum(pattern, values, table, precision=lax.Precision.HIGHEST)]
    reshape x2 -> x0, local copies, waits for them, and re-layouts: 43.6 us -> none  [lines(): return values.reshape(old_shape)]
    reduce_scatter x0 -> x1, waiting for transfers between devices: none -> 38.3 us  [on_device(): part = lax.psum_scatter(part, 'z', scatter_dimension=0, tiled=True)]
    pallas_call x0 -> x4, Pallas kernels: none -> 33.1 us  [call(): pl.pallas_call(kernel, out_shape=[jax.ShapeDtypeStruct(shape, F32) for sh...]
    transpose x2 -> x0, local copies, waits for them, and re-layouts: 31.3 us -> none  [lines(): return values.reshape(old_shape)]
  transfers between devices with their start and end apart: 3 -> 5, of which waited for: 3 -> 5; matrix products, arithmetic and copies ran while one was open for 0% -> 1% of each run, Pallas kernels for 0% -> 2%
where the time goes in v1:
time: 330 us; the launch traced here: 329 us
  waiting for transfers between devices  140 us (42%)
  blocking collectives  97.9 us (30%)
  Pallas kernels  33.1 us (10%)
  starting transfers between devices  24.1 us (7%)
  local copies, waits for them, and re-layouts  17.7 us (5%)
  between operations  15.1 us (5%)
    all_to_all x1, blocking collectives, on_device(): spectrum = lax.all_to_all(spectrum, SLAB, 0, 0, tiled=True)  57.2 us
    all_to_all x1, waiting for transfers between devices, on_device(): spectrum = lax.all_to_all(spectrum, SLAB, 0, 0, tiled=True)  51.3 us
    reduce_scatter x1, waiting for transfers between devices, on_device(): part = lax.psum_scatter(part, 'z', scatter_dimension=0, tiled=True)  38.3 us
    pallas_call x4, Pallas kernels, call(): pl.pallas_call(kernel, out_shape=[jax.ShapeDtypeStruct(shape, F32) for sh...  33.1 us
    all_to_all x1, blocking collectives, on_device(): lax.all_to_all(part, ('xl', 'y'), 0, 0, tiled=True)  27.8 us
    all_to_all x1, waiting for transfers between devices, on_device(): sorted_targets = lax.all_to_all(sorted_targets, SLAB, 0, 0, tiled=True)  25 us
    all_to_all x1, waiting for transfers between devices, on_device(): lax.all_to_all(sorted_targets, 'z', 0, 0, tiled=True).reshape(length, INNER)  13 us
    unnamed x1, blocking collectives  12.9 us
  transfers between devices with their start and end apart: 5, of which 5 were waited for; matrix products, arithmetic and copies ran while one was open for 1% of the time, Pallas kernels for 2%

profile of v1, /device:TPU:4, one launch (start us, length us, event | category | flops | bytes accessed | tf_op | source)
XLA Modules:
  0.0 329.2 jit_solution(1194899299503142521)
XLA Ops:
  6.5 1.7 copy-done.7
  8.3 1.7 shard_map.38
  10.0 1.3 copy-done.1
  11.3 7.6 %all-to-all-start.1 = ((f32[32,128,128]{2,1,0:T(8,128)}), f32[32,128,128]{2,1,0:T(8,128)}, u32[]{:S(2)}, u32[]{:S(2)}) async-start(f32[32,128,128]{2,1,0:T(8,128)} %copy-done.1), calls=%async_computation.1 | async-start | bytes 4194304 | tf_op jit(solution)/shard_map/all_to_all | solution.py:311
  19.1 0.7 constant_dynamic-slice_fusion
  19.8 25.0 %all-to-all-done.1 = f32[32,128,128]{2,1,0:T(8,128)} async-done(((f32[32,128,128]{2,1,0:T(8,128)}), f32[32,128,128]{2,1,0:T(8,128)}, u32[]{:S(2)}, u32[]{:S(2)}) %all-to-all-start.1) | async-done | bytes 2097184 | tf_op jit(solution)/shard_map/all_to_all | solution.py:311
  44.9 8.5 %all-to-all-start.2 = ((f32[32,128,128]{2,1,0:T(8,128)}), f32[32,128,128]{2,1,0:T(8,128)}, u32[]{:S(2)}, u32[]{:S(2)}) async-start(f32[32,128,128]{2,1,0:T(8,128)} %all-to-all-done.1), calls=%async_computation.2 | async-start | bytes 4194304 | tf_op jit(solution)/shard_map/all_to_all | solution.py:312
  54.0 0.6 dynamic-slice
  54.6 0.8 dynamic-update-slice
  55.3 12.9 %all-reduce = s32[8]{0:T(128)S(1)} all-reduce(s32[8]{0:T(128)S(1)} %dynamic-update-slice), channel_id=1, replica_groups=mesh['xl'=2,'y'=4,'z'=8,'xh'=2,'c'=2] {'xl','y'}, use_global_device_ids=true, to_apply=%add | all-reduce | flops 8 | bytes 64
  68.2 0.6 dynamic_slice.8
  69.8 0.3 fusion.7
  70.1 0.3 sine_multiply_fusion.1
  70.5 12.3 %all-gather.2.cloned.1.call-done.phase_ref = f32[128,4096]{1,0:T(8,128)} async-done(((f32[16,4096]{1,0:T(8,128)}), f32[128,4096]{1,0:T(8,128)}) %all-gather.2.cloned.1.call-update) | async-done | bytes 2097168 | tf_op jit(solution)/shard_map/all_gather | solution.py:301
  82.9 1.6 copy-done.6
  84.5 7.3 %shard_map.37 = (f32[32,2,128,128]{3,2,1,0:T(8,128)S(1)}, f32[2,128,4096]{2,1,0:T(8,128)S(1)}) custom-call(f32[128,4096]{1,0:T(8,128)S(1)} %copy-done.6, f32[128,128]{1,0:T(8,128)S(1)} %broadcast_in_dim.6.row_ref, f32[1,4096]{1,0:T(1,128)S(1)} %fusion.14.col_ref, f32[2,32,128]{2,1,0:T(8,128)S(1)} %pad_maximum_fusion.tw_ref, ...), custom_call_target="tpu_custom_call" | custom-call | tf_op jit(solution)/shard_map/pallas_call | solution.py:262
  91.8 2.0 copy-done.3
  93.8 2.0 copy-done.4
  95.7 13.0 %all-to-all-done.2 = f32[32,128,128]{2,1,0:T(8,128)} async-done(((f32[32,128,128]{2,1,0:T(8,128)}), f32[32,128,128]{2,1,0:T(8,128)}, u32[]{:S(2)}, u32[]{:S(2)}) %all-to-all-start.2) | async-done | bytes 2097184 | tf_op jit(solution)/shard_map/all_to_all | solution.py:312
  108.7 7.9 %all-to-all-start = ((f32[32,2,128,128]{3,2,1,0:T(8,128)}), f32[32,2,128,128]{3,2,1,0:T(8,128)}, u32[]{:S(2)}, u32[]{:S(2)}) async-start(f32[32,2,128,128]{3,2,1,0:T(8,128)} %copy-done.3), calls=%async_computation | async-start | bytes 8388608 | tf_op jit(solution)/shard_map/all_to_all | solution.py:346
  116.7 0.3 fusion.8
  117.0 0.3 sine_multiply_fusion
  117.3 51.3 %all-to-all-done.refs_0_ = f32[32,2,128,128]{3,2,1,0:T(8,128)} async-done(((f32[32,2,128,128]{3,2,1,0:T(8,128)}), f32[32,2,128,128]{3,2,1,0:T(8,128)}, u32[]{:S(2)}, u32[]{:S(2)}) %all-to-all-start) | async-done | bytes 4194336 | tf_op jit(solution)/shard_map/all_to_all | solution.py:346
  168.6 2.6 broadcast_in_dim.7.refs_2_
  171.2 19.1 %shard_map.39 = f32[32,2,128,128]{3,2,1,0:T(8,128)S(1)} custom-call(f32[32,2,128,128]{3,2,1,0:T(8,128)} %all-to-all-done.refs_0_, f32[4096,128]{1,0:T(8,128)} %bitcast.3.refs_1_, f32[2,32,128,128]{3,2,1,0:T(8,128)} %broadcast_in_dim.7.refs_2_, f32[256,256]{1,0:T(8,128)S(1)} %maximum_maximum_fusion.dft_ref.refs_3_, ...), custom_call_target="tpu_custom_call" | custom-call | tf_op jit(solution)/shard_map/pallas_call | solution.py:262
  190.3 57.2 %all_to_all.25.in_ref = f32[32,2,128,128]{3,2,1,0:T(8,128)S(1)} all-to-all(f32[32,2,128,128]{3,2,1,0:T(8,128)S(1)} %shard_map.39), channel_id=1, replica_groups=mesh['xl'=2,'y'=4,'z'=8,'xh'=2,'c'=2] {'xl','y','xh','c'}, dimensions={0} | all-to-all | bytes 8388608 | tf_op jit(solution)/shard_map/all_to_all | solution.py:366
  247.5 5.0 %shard_map.40 = f32[128,4096]{1,0:T(8,128)S(1)} custom-call(f32[32,2,128,128]{3,2,1,0:T(8,128)S(1)} %all_to_all.25.in_ref, f32[2,128,4096]{2,1,0:T(8,128)S(1)} %copy-done.5, f32[2,32,128]{2,1,0:T(8,128)S(1)} %pad_maximum_fusion.tw_ref, f32[256,256]{1,0:T(8,128)S(1)} %maximum_maximum_fusion.1.refs_4_.dft_ref), custom_call_target="tpu_custom_call" | custom-call | tf_op jit(solution)/shard_map/pallas_call | solution.py:262
  252.5 1.3 copy-done.2
  253.8 38.3 %reduce-scatter.2.cloned.1.call-done = f32[16,4096]{1,0:T(8,128)} async-done(((f32[128,4096]{1,0:T(8,128)}), f32[16,4096]{1,0:T(8,128)}) %reduce-scatter.2.cloned.1.call-update) | async-done | bytes 262160 | tf_op jit(solution)/shard_map/reduce_scatter | solution.py:376
  292.1 1.1 broadcast_in_dim.8
  293.3 27.8 %all_to_all.26 = f32[8,16,4096]{2,1,0:T(8,128)S(1)} all-to-all(f32[8,16,4096]{2,1,0:T(8,128)S(1)} %broadcast_in_dim.8), channel_id=1, replica_groups=mesh['xl'=2,'y'=4,'z'=8,'xh'=2,'c'=2] {'xl','y'}, dimensions={0} | all-to-all | bytes 4194304 | tf_op jit(solution)/shard_map/all_to_all | solution.py:378
  321.1 1.3 copy.7
  (24 shorter events, 0.5 us)
Async XLA Ops:
  6.5 12.5 %copy-start = (f32[128,4096]{1,0:T(8,128)S(1)}, f32[128,4096]{1,0:T(8,128)}, u32[]{:S(2)}) copy-start(f32[128,4096]{1,0:T(8,128)} %param.3) | copy-start | bytes 6291460
  6.5 1.7 copy-start.7
  10.0 1.3 copy-start.1
  11.3 33.5 %all-to-all-start.1 = ((f32[32,128,128]{2,1,0:T(8,128)}), f32[32,128,128]{2,1,0:T(8,128)}, u32[]{:S(2)}, u32[]{:S(2)}) async-start(f32[32,128,128]{2,1,0:T(8,128)} %copy-done.1), calls=%async_computation.1 | async-start | bytes 4194304 | tf_op jit(solution)/shard_map/all_to_all | solution.py:311
  19.0 63.8 %all-gather.2.cloned.1.call-start = ((), (), s32[]{:S(2)}) async-start(), calls=%async_computation.6 | async-start | bytes 2359296 | tf_op jit(solution)/shard_map/all_gather | solution.py:301
  19.8 34.2 %copy-start.8 = (u32[256]{0:T(256)S(1)}, u32[256]{0:T(256)}, u32[]{:S(2)}) copy-start(u32[256]{0:T(256)} %constant.202) | copy-start | bytes 3076
  44.9 63.9 %all-to-all-start.2 = ((f32[32,128,128]{2,1,0:T(8,128)}), f32[32,128,128]{2,1,0:T(8,128)}, u32[]{:S(2)}, u32[]{:S(2)}) async-start(f32[32,128,128]{2,1,0:T(8,128)} %all-to-all-done.1), calls=%async_computation.2 | async-start | bytes 4194304 | tf_op jit(solution)/shard_map/all_to_all | solution.py:312
  82.9 1.6 copy-start.6
  91.8 2.0 copy-start.3
  93.8 2.0 copy-start.4
  108.7 59.9 %all-to-all-start = ((f32[32,2,128,128]{3,2,1,0:T(8,128)}), f32[32,2,128,128]{3,2,1,0:T(8,128)}, u32[]{:S(2)}, u32[]{:S(2)}) async-start(f32[32,2,128,128]{3,2,1,0:T(8,128)} %copy-done.3), calls=%async_computation | async-start | bytes 8388608 | tf_op jit(solution)/shard_map/all_to_all | solution.py:346
  116.6 175.5 %reduce-scatter.2.cloned.1.call-start = ((), (), s32[]{:S(2)}) async-start(), calls=%async_computation.7 | async-start | bytes 2359296 | tf_op jit(solution)/shard_map/reduce_scatter | solution.py:376
  190.3 57.3 %copy-start.5 = (f32[2,128,4096]{2,1,0:T(8,128)S(1)}, f32[2,128,4096]{2,1,0:T(8,128)}, u32[]{:S(2)}) copy-start(f32[2,128,4096]{2,1,0:T(8,128)} %copy-done.4) | copy-start | bytes 12582916
  252.5 1.3 copy-start.2
Sparse Core Ops, SparseCore 0:
  21.6 61.1 all-gather.1
  254.0 38.1 reduce-scatter.1

commit v2 on v1

--- a/solution.py
+++ b/solution.py
@@ -13,6 +13,7 @@
 OUTER = 32
 INNER = 128
 BLOCK = 16
+WIDE = 4
 F32 = jnp.float32
 BF16 = jnp.bfloat16
 
@@ -120,8 +121,16 @@
         out_ref[j] = turned_ref[pl.ds(j, INNER, stride=OUTER), :].T
 
 
-def rows_kernel(phase_ref, row_ref, col_ref, tw_ref, dft_ref, out_ref, wave_ref, high_ref, low_ref, mid_ref, sh_ref, sl_ref):
+def rows_kernel(phase_ref, row_ref, col_ref, tw_ref, dft_ref, out_hbm, wave_hbm, high_ref, low_ref, mid_ref, sh_ref, sl_ref, out_ref, wave_ref, sem):
     high_ref[...], low_ref[...] = split(dft_ref[...])
+
+    def save_wave(step):
+        rows = row_block(step)
+        return pltpu.make_async_copy(wave_ref.at[:, rows, :], wave_hbm.at[:, rows, :], sem.at[0])
+
+    def save_out(step):
+        group = pl.ds(step * 4, 4)
+        return pltpu.make_async_copy(out_ref.at[group], out_hbm.at[group], sem.at[1])
 
     def block(step, carry):
         rows = row_block(step)
@@ -143,6 +152,7 @@
                 sl_ref[k, rows, tile(side)] = low
 
         dft32(load, store, mid_ref, -1)
+        save_wave(step).start()
         return carry
 
     lax.fori_loop(0, INNER // BLOCK, block, 0)
@@ -155,17 +165,29 @@
         out = out.reshape(4, INNER, 2 * INNER)
         out_ref[group, 0] = out[:, :, :INNER]
         out_ref[group, 1] = out[:, :, INNER:]
+        save_out(step).start()
         return carry
 
     lax.fori_loop(0, OUTER // 4, multiply, 0)
+    pltpu.make_async_copy(wave_ref, wave_hbm, sem.at[0]).wait()
+    pltpu.make_async_copy(out_ref, out_hbm, sem.at[1]).wait()
 
 
 def columns_kernel(
-    scale, in_ref, target_ref, tw_ref, there_ref, home_ref, out_ref,
-    fh_ref, fl_ref, bh_ref, bl_ref, mid_ref, sh_ref, sl_ref, back_ref,
+    scale, layer_ref, in_ref, *refs
 ):
-    fh_ref[...], fl_ref[...] = split(home_ref[...])
-    bh_ref[...], bl_ref[...] = split(there_ref[...])
+    pieces, refs = refs[: len(refs) - 11], refs[len(refs) - 11 :]
+    tw_ref, there_ref, home_ref, out_ref, there_both, home_both, mid_ref, sh_ref, sl_ref, back_ref, target_ref = refs
+    for both, ref in ((there_both, home_ref), (home_both, there_ref)):
+        both[: 2 * INNER, :], both[2 * INNER :, :] = split(ref[...])
+
+    layers = len(pieces)
+    run = INNER // layers
+    for k, piece in enumerate(pieces):
+        start = lax.rem(layer_ref[0] + (layers - k), layers) * run
+        spot = pl.ds(pl.multiple_of(start, run), run)
+        for u0 in range(OUTER):
+            target_ref[u0, spot, :] = piece[pl.ds(u0, run, stride=OUTER), :]
 
     def forward(step, carry):
         rows = row_block(step)
@@ -174,7 +196,7 @@
             return tuple(in_ref[step * 4 + k % 4, side, tile_rows(k // 4), :] for side in (0, 1))
 
         def store(k, value):
-            cos, sin = tw_ref[0, k, rows, :], tw_ref[1, k, rows, :]
+            cos, sin = tw_ref[0, rows, k : k + 1], tw_ref[1, rows, k : k + 1]
             real, imag = value
             for part, side in ((real * cos - imag * sin, 0), (real * sin + imag * cos, 1)):
                 high, low = split(part)
@@ -186,31 +208,31 @@
 
     lax.fori_loop(0, INNER // BLOCK, forward, 0)
 
-    def pair(ref, first):
-        return jnp.concatenate([ref[first + k].reshape(2 * INNER, INNER) for k in (0, 1)], axis=1)
+    def wide(ref, first):
+        return jnp.concatenate([ref[first + k].reshape(2 * INNER, INNER) for k in range(WIDE)], axis=1)
+
+    def product(table_ref, high, low):
+        out = dot(table_ref[...], high)
+        return out[: 2 * INNER] + (out[2 * INNER :] + dot(table_ref[: 2 * INNER, :], low))
 
     def multiply(step, carry):
-        first = step * 2
-        high, low = pair(sh_ref, first), pair(sl_ref, first)
-        field = dot(fh_ref[...], high) + dot(fh_ref[...], low) + dot(fl_ref[...], high)
+        first = step * WIDE
+        field = product(there_both, wide(sh_ref, first), wide(sl_ref, first))
         real, imag = field[:INNER], field[INNER:]
-        target = jnp.concatenate(
-            [target_ref[pl.ds(first + k, INNER, stride=OUTER), :] for k in (0, 1)], axis=1
-        )
+        target = jnp.concatenate([target_ref[first + k] for k in range(WIDE)], axis=1)
         residual = scale * (real * real + imag * imag - target)
-        high, low = split(jnp.concatenate([residual * real, residual * imag], axis=0))
-        back = dot(bh_ref[...], high) + dot(bh_ref[...], low) + dot(bl_ref[...], high)
-        for k in (0, 1):
+        back = product(home_both, *split(jnp.concatenate([residual * real, residual * imag], axis=0)))
+        for k in range(WIDE):
             back_ref[first + k] = back[:, tile(k)].reshape(2, INNER, INNER)
         return carry
 
-    lax.fori_loop(0, OUTER // 2, multiply, 0)
+    lax.fori_loop(0, OUTER // WIDE, multiply, 0)
 
     def backward(step, carry):
         rows = row_block(step)
 
         def load(k):
-            cos, sin = tw_ref[0, k, rows, :], tw_ref[1, k, rows, :]
+            cos, sin = tw_ref[0, rows, k : k + 1], tw_ref[1, rows, k : k + 1]
             real, imag = back_ref[k, 0, rows, :], back_ref[k, 1, rows, :]
             return real * cos + imag * sin, imag * cos - real * sin
 
@@ -258,14 +280,14 @@
     lax.fori_loop(0, INNER // BLOCK, block, 0)
 
 
-def call(kernel, out_shapes, scratch, *args):
+def call(kernel, out_shapes, scratch, *args, space=pltpu.VMEM, limit=28):
     return pl.pallas_call(
         kernel,
         out_shape=[jax.ShapeDtypeStruct(shape, F32) for shape in out_shapes],
-        in_specs=[pl.BlockSpec(memory_space=pltpu.VMEM)] * len(args),
-        out_specs=[pl.BlockSpec(memory_space=pltpu.VMEM)] * len(out_shapes),
-        scratch_shapes=[pltpu.VMEM(shape, dtype) for shape, dtype in scratch],
-        compiler_params=pltpu.CompilerParams(vmem_limit_bytes=40 * 2**20),
+        in_specs=[pl.BlockSpec(memory_space=pltpu.SMEM if arg.dtype == jnp.int32 else pltpu.VMEM) for arg in args],
+        out_specs=[pl.BlockSpec(memory_space=space)] * len(out_shapes),
+        scratch_shapes=[pltpu.VMEM(*item) if isinstance(item, tuple) else item for item in scratch],
+        compiler_params=pltpu.CompilerParams(vmem_limit_bytes=limit * 2**20),
     )(*args)
 
 
@@ -298,6 +320,7 @@
 
     share = rows_dev // planes
     mine = lax.dynamic_slice_in_dim(phase, place * share, share, 0)
+    mine, targets = lax.optimization_barrier((mine, targets))
     rows_phase = lax.all_gather(mine, "z", axis=0, tiled=True)
 
     all_depths = lax.all_gather(depths, ("xl", "y"), axis=0, tiled=True)
@@ -309,7 +332,15 @@
         targets[0],
     )
     sorted_targets = lax.all_to_all(sorted_targets, SLAB, 0, 0, tiled=True)
-    sorted_targets = lax.all_to_all(sorted_targets, "z", 0, 0, tiled=True).reshape(length, INNER)
+    rows_phase, sorted_targets = lax.optimization_barrier((rows_phase, sorted_targets))
+    layer = lax.axis_index("z")
+    group = slab_size // layers
+    pieces = []
+    for k in range(layers):
+        piece = lax.dynamic_slice_in_dim(sorted_targets, (layer + k) % layers * group, group, 0)
+        if k:
+            piece = lax.ppermute(piece, "z", [(i, (i + k) % layers) for i in range(layers)])
+        pieces.append(piece.reshape(group * rows_dev, INNER))
 
     strength = ((depth + 8) * (length // 64) + 1) % modulus
     weight = inverse_odd(strength, modulus)
@@ -326,7 +357,7 @@
     inner = jnp.arange(INNER, dtype=jnp.int32)[None, :]
     angle = (outer * inner * weight % length).astype(F32) * (-2.0 * math.pi / length)
     twiddle = jnp.stack([jnp.cos(angle), jnp.sin(angle)])
-    tall_twiddle = jnp.broadcast_to(twiddle[:, :, :, None], (2, OUTER, INNER, INNER))
+    tall_twiddle = jnp.stack([jnp.cos(angle.T), jnp.sin(angle.T)])
     there = table(weight, length, -1.0)
     back = table(weight, length, 1.0)
 
@@ -336,29 +367,40 @@
     spectrum, wave = call(
         rows_kernel,
         [chunks, (2, layers * share, length)],
-        [matrix, matrix, mid, ((OUTER, INNER, 2 * INNER), BF16), ((OUTER, INNER, 2 * INNER), BF16)],
+        [
+            matrix,
+            matrix,
+            mid,
+            ((OUTER, INNER, 2 * INNER), BF16),
+            ((OUTER, INNER, 2 * INNER), BF16),
+            (chunks, F32),
+            ((2, layers * share, length), F32),
+            pltpu.SemaphoreType.DMA((2,)),
+        ],
         rows_phase,
         row_chirp,
         chirp[None, :],
         twiddle,
         there,
+        space=pltpu.HBM,
+        limit=60,
     )
     spectrum = lax.all_to_all(spectrum, SLAB, 0, 0, tiled=True)
     (spectrum,) = call(
         lambda *refs: columns_kernel(4.0 / planes, *refs),
         [chunks],
         [
-            matrix,
-            matrix,
-            matrix,
-            matrix,
+            ((4 * INNER, 2 * INNER), BF16),
+            ((4 * INNER, 2 * INNER), BF16),
             mid,
             ((OUTER, 2, INNER, INNER), BF16),
             ((OUTER, 2, INNER, INNER), BF16),
             ((OUTER, 2, INNER, INNER), F32),
+            ((OUTER, INNER, INNER), F32),
         ],
+        layer.astype(jnp.int32)[None],
         spectrum,
-        sorted_targets,
+        *pieces,
         tall_twiddle,
         there,
         back,

time: 330 us -> 296 us (0.90)
  waiting for transfers between devices: 140 us -> 84.6 us
  blocking collectives: 97.9 us -> 114 us
  starting transfers between devices: 24.1 us -> 31 us
  other arithmetic: 1.49 us -> 4.96 us
  local copies, waits for them, and re-layouts: 17.7 us -> 14.3 us
    all_to_all x1, waiting for transfers between devices: 51.3 us -> 0.01 us  [on_device(): spectrum = lax.all_to_all(spectrum, SLAB, 0, 0, tiled=True)]
    ppermute x0 -> x7, waiting for transfers between devices: none -> 41.7 us  [on_device(): lax.ppermute(piece, 'z', [(i, (i + k) % layers) for i in range(layers)])]
    all_to_all x1, waiting for transfers between devices: 25 us -> 0.01 us  [on_device(): sorted_targets = lax.all_to_all(sorted_targets, SLAB, 0, 0, tiled=True)]
    unnamed x1, blocking collectives: 12.9 us -> 30.5 us
    ppermute x0 -> x7, starting transfers between devices: none -> 15.2 us  [on_device(): lax.ppermute(piece, 'z', [(i, (i + k) % layers) for i in range(layers)])]
    all_to_all x1 -> x0, waiting for transfers between devices: 13 us -> none  [on_device(): lax.all_to_all(sorted_targets, 'z', 0, 0, tiled=True).reshape(length, INNER)]
    all_gather x1, waiting for transfers between devices: 12.3 us -> 0.01 us  [on_device(): rows_phase = lax.all_gather(mine, 'z', axis=0, tiled=True)]
    all_to_all x1 -> x0, starting transfers between devices: 8.47 us -> none  [on_device(): lax.all_to_all(sorted_targets, 'z', 0, 0, tiled=True).reshape(length, INNER)]
  transfers between devices with their start and end apart: 5 -> 11, of which waited for: 5 -> 6; matrix products, arithmetic and copies ran while one was open for 1% -> 3% of each run, Pallas kernels for 2% -> 1%
where the time goes in v2:
time: 296 us
  blocking collectives  114 us (39%)
  waiting for transfers between devices  84.6 us (29%)
  Pallas kernels  31.6 us (11%)
  starting transfers between devices  31 us (10%)
  between operations  15.1 us (5%)
  local copies, waits for them, and re-layouts  14.3 us (5%)
  other arithmetic  4.96 us (2%)
    all_to_all x1, blocking collectives, on_device(): spectrum = lax.all_to_all(spectrum, SLAB, 0, 0, tiled=True)  56 us
    reduce_scatter x1, waiting for transfers between devices, on_device(): part = lax.psum_scatter(part, 'z', scatter_dimension=0, tiled=True)  42.9 us
    ppermute x7, waiting for transfers between devices, on_device(): lax.ppermute(piece, 'z', [(i, (i + k) % layers) for i in range(layers)])  41.7 us
    pallas_call x4, Pallas kernels, call(): pl.pallas_call(kernel, out_shape=[jax.ShapeDtypeStruct(shape, F32) for sh...  31.6 us
    unnamed x1, blocking collectives  30.5 us
    all_to_all x1, blocking collectives, on_device(): lax.all_to_all(part, ('xl', 'y'), 0, 0, tiled=True)  27.5 us
    ppermute x7, starting transfers between devices, on_device(): lax.ppermute(piece, 'z', [(i, (i + k) % layers) for i in range(layers)])  15.2 us
    unnamed x20, local copies, waits for them, and re-layouts  8.41 us
  transfers between devices with their start and end apart: 11, of which 6 were waited for; matrix products, arithmetic and copies ran while one was open for 3% of the time, Pallas kernels for 1%

profile of v2, /device:TPU:4, one launch (start us, length us, event | category | flops | bytes accessed | tf_op | source)
XLA Modules:
  0.0 295.6 jit_solution(6142174074401488706)
XLA Ops:
  6.5 1.6 copy-done
  8.1 0.7 constant_dynamic-slice_fusion.8
  8.9 1.6 copy-done.5
  10.5 1.7 shard_map.37
  12.2 1.3 copy-done.1
  13.5 7.8 %all-to-all-start = ((f32[32,128,128]{2,1,0:T(8,128)}), f32[32,128,128]{2,1,0:T(8,128)}, u32[]{:S(2)}, u32[]{:S(2)}) async-start(f32[32,128,128]{2,1,0:T(8,128)} %copy-done.1), calls=%async_computation | async-start | bytes 4194304 | tf_op jit(solution)/shard_map/all_to_all | solution.py:334
  23.3 30.5 %all-reduce = s32[8]{0:T(128)S(1)} all-reduce(s32[8]{0:T(128)S(1)} %dynamic-update-slice), channel_id=1, replica_groups=mesh['xl'=2,'y'=4,'z'=8,'xh'=2,'c'=2] {'xl','y'}, use_global_device_ids=true, to_apply=%add | all-reduce | flops 8 | bytes 64
  56.4 0.7 maximum_maximum_fusion.dft_ref.refs_11_
  57.1 0.7 fusion.17.col_ref
  58.6 9.9 %shard_map.38 = (f32[32,2,128,128]{3,2,1,0:T(8,128)}, f32[2,128,4096]{2,1,0:T(8,128)}) custom-call(f32[128,4096]{1,0:T(8,128)} %all-gather.2.cloned.1.call-done.phase_ref, f32[128,128]{1,0:T(8,128)} %broadcast_in_dim.7.row_ref, f32[1,4096]{1,0:T(1,128)} %fusion.17.col_ref, f32[2,32,128]{2,1,0:T(8,128)} %pad_maximum_fusion.tw_ref, ...), custom_call_target="tpu_custom_call" | custom-call | tf_op jit(solution)/shard_map/pallas_call | solution.py:284
  68.4 8.0 %all-to-all-start.1 = ((f32[32,2,128,128]{3,2,1,0:T(8,128)}), f32[32,2,128,128]{3,2,1,0:T(8,128)}, u32[]{:S(2)}, u32[]{:S(2)}) async-start(f32[32,2,128,128]{3,2,1,0:T(8,128)} %get-tuple-element.14), calls=%async_computation.1 | async-start | bytes 8388608 | tf_op jit(solution)/shard_map/all_to_all | solution.py:388
  76.6 2.6 constant_dynamic-slice_fusion
  79.2 6.3 %collective-permute-start.5 = (f32[4,128,128]{2,1,0:T(8,128)S(1)}, f32[4,128,128]{2,1,0:T(8,128)S(1)}, u32[]{:S(2)}, u32[]{:S(2)}) collective-permute-start(f32[4,128,128]{2,1,0:T(8,128)S(1)} %get-tuple-element.18), channel_id=1, source_target_pairs={{0,24},{4,28},{8,0},{12,4},{16,8},{20,12},{24,16},{28,20},{1,25},{... | collective-permute-start | bytes 786440 | tf_op jit(solution)/shard_map/ppermute | solution.py:342
  85.5 1.0 collective-permute-start.6
  86.6 0.9 fusion.8
  87.5 1.0 collective-permute-start
  89.0 2.0 collective-permute-start.2
  91.0 6.4 %collective-permute-done.5 = f32[4,128,128]{2,1,0:T(8,128)S(1)} collective-permute-done((f32[4,128,128]{2,1,0:T(8,128)S(1)}, f32[4,128,128]{2,1,0:T(8,128)S(1)}, u32[]{:S(2)}, u32[]{:S(2)}) %collective-permute-start.5) | collective-permute-done | bytes 262176 | tf_op jit(solution)/shard_map/ppermute | solution.py:342
  97.4 4.4 %collective-permute-start.3 = (f32[4,128,128]{2,1,0:T(8,128)}, f32[4,128,128]{2,1,0:T(8,128)}, u32[]{:S(2)}, u32[]{:S(2)}) collective-permute-start(f32[4,128,128]{2,1,0:T(8,128)} %get-tuple-element.20), channel_id=1, source_target_pairs={{0,16},{4,20},{8,24},{12,28},{16,0},{20,4},{24,8},{28,12},{1,17},{... | collective-permute-start | bytes 786440 | tf_op jit(solution)/shard_map/ppermute | solution.py:342
  101.8 17.7 %collective-permute-done.6 = f32[4,128,128]{2,1,0:T(8,128)S(1)} collective-permute-done((f32[4,128,128]{2,1,0:T(8,128)S(1)}, f32[4,128,128]{2,1,0:T(8,128)S(1)}, u32[]{:S(2)}, u32[]{:S(2)}) %collective-permute-start.6) | collective-permute-done | bytes 262176 | tf_op jit(solution)/shard_map/ppermute | solution.py:342
  119.9 0.9 maximum_maximum_fusion.1.refs_12_.dft_ref
  120.8 8.5 %collective-permute-done.2 = f32[4,128,128]{2,1,0:T(8,128)} collective-permute-done((f32[4,128,128]{2,1,0:T(8,128)}, f32[4,128,128]{2,1,0:T(8,128)}, u32[]{:S(2)}, u32[]{:S(2)}) %collective-permute-start.2) | collective-permute-done | bytes 262176 | tf_op jit(solution)/shard_map/ppermute | solution.py:342
  129.3 1.6 collective-permute-done.3
  130.9 7.5 %collective-permute-done.4 = f32[4,128,128]{2,1,0:T(8,128)} collective-permute-done((f32[4,128,128]{2,1,0:T(8,128)}, f32[4,128,128]{2,1,0:T(8,128)}, u32[]{:S(2)}, u32[]{:S(2)}) %collective-permute-start.4) | collective-permute-done | bytes 262176 | tf_op jit(solution)/shard_map/ppermute | solution.py:342
  138.5 15.1 %shard_map.39 = f32[32,2,128,128]{3,2,1,0:T(8,128)S(1)} custom-call(s32[1]{0:T(128)} %bitcast.refs_0_, f32[32,2,128,128]{3,2,1,0:T(8,128)} %all-to-all-done.1.refs_1_, f32[512,128]{1,0:T(8,128)S(1)} %bitcast.14, f32[512,128]{1,0:T(8,128)} %bitcast.5.refs_3_, f32[512,128]{1,0:T(8,128)} %bitcast.6.refs_4_, f32[512,128]{1,0:T(8,128)} %bitcast.7.refs_5_, ...), custom_call_target="tpu_custom_call" | custom-call | tf_op jit(solution)/shard_map/pallas_call | solution.py:284
  153.6 56.0 %all_to_all.20.in_ref = f32[32,2,128,128]{3,2,1,0:T(8,128)S(1)} all-to-all(f32[32,2,128,128]{3,2,1,0:T(8,128)S(1)} %shard_map.39), channel_id=1, replica_groups=mesh['xl'=2,'y'=4,'z'=8,'xh'=2,'c'=2] {'xl','y','xh','c'}, dimensions={0} | all-to-all | bytes 8388608 | tf_op jit(solution)/shard_map/all_to_all | solution.py:408
  209.6 5.0 %shard_map.40 = f32[128,4096]{1,0:T(8,128)S(1)} custom-call(f32[32,2,128,128]{3,2,1,0:T(8,128)S(1)} %all_to_all.20.in_ref, f32[2,128,4096]{2,1,0:T(8,128)S(1)} %copy-done.3, f32[2,32,128]{2,1,0:T(8,128)S(1)} %copy-done.6, f32[256,256]{1,0:T(8,128)S(1)} %maximum_maximum_fusion.1.refs_12_.dft_ref), custom_call_target="tpu_custom_call" | custom-call | tf_op jit(solution)/shard_map/pallas_call | solution.py:284
  214.6 1.3 copy-done.2
  215.9 42.9 %reduce-scatter.2.cloned.1.call-done = f32[16,4096]{1,0:T(8,128)} async-done(((f32[128,4096]{1,0:T(8,128)}), f32[16,4096]{1,0:T(8,128)}) %reduce-scatter.2.cloned.1.call-update) | async-done | bytes 262160 | tf_op jit(solution)/shard_map/reduce_scatter | solution.py:418
  258.8 1.1 broadcast_in_dim.8
  259.9 27.5 %all_to_all.21 = f32[8,16,4096]{2,1,0:T(8,128)S(1)} all-to-all(f32[8,16,4096]{2,1,0:T(8,128)S(1)} %broadcast_in_dim.8), channel_id=1, replica_groups=mesh['xl'=2,'y'=4,'z'=8,'xh'=2,'c'=2] {'xl','y'}, dimensions={0} | all-to-all | bytes 4194304 | tf_op jit(solution)/shard_map/all_to_all | solution.py:420
  287.5 1.3 copy.8
  (37 shorter events, 5.0 us)
Async XLA Ops:
  6.5 1.6 copy-start
  6.5 51.3 %all-gather.2.cloned.1.call-start = ((), (), s32[]{:S(2)}) async-start(), calls=%async_computation.5 | async-start | bytes 2359296 | tf_op jit(solution)/shard_map/all_gather | solution.py:324
  8.9 1.6 copy-start.5
  12.2 1.3 copy-start.1
  13.5 8.4 %copy-start.7 = (u32[256]{0:T(256)S(1)}, u32[256]{0:T(256)}, u32[]{:S(2)}) copy-start(u32[256]{0:T(256)} %constant.249) | copy-start | bytes 3076
  13.5 44.3 %all-to-all-start = ((f32[32,128,128]{2,1,0:T(8,128)}), f32[32,128,128]{2,1,0:T(8,128)}, u32[]{:S(2)}, u32[]{:S(2)}) async-start(f32[32,128,128]{2,1,0:T(8,128)} %copy-done.1), calls=%async_computation | async-start | bytes 4194304 | tf_op jit(solution)/shard_map/all_to_all | solution.py:334
  68.4 70.0 %all-to-all-start.1 = ((f32[32,2,128,128]{3,2,1,0:T(8,128)}), f32[32,2,128,128]{3,2,1,0:T(8,128)}, u32[]{:S(2)}, u32[]{:S(2)}) async-start(f32[32,2,128,128]{3,2,1,0:T(8,128)} %get-tuple-element.14), calls=%async_computation.1 | async-start | bytes 8388608 | tf_op jit(solution)/shard_map/all_to_all | solution.py:388
  76.4 182.4 %reduce-scatter.2.cloned.1.call-start = ((), (), s32[]{:S(2)}) async-start(), calls=%async_computation.6 | async-start | bytes 2359296 | tf_op jit(solution)/shard_map/reduce_scatter | solution.py:418
  76.6 61.9 %copy-start.4 = (f32[256,256]{1,0:T(8,128)S(1)}, f32[256,256]{1,0:T(8,128)}, u32[]{:S(2)}) copy-start(f32[256,256]{1,0:T(8,128)} %maximum_maximum_fusion.dft_ref.refs_11_) | copy-start | bytes 786436
  79.2 18.2 %collective-permute-start.5 = (f32[4,128,128]{2,1,0:T(8,128)S(1)}, f32[4,128,128]{2,1,0:T(8,128)S(1)}, u32[]{:S(2)}, u32[]{:S(2)}) collective-permute-start(f32[4,128,128]{2,1,0:T(8,128)S(1)} %get-tuple-element.18), channel_id=1, source_target_pairs={{0,24},{4,28},{8,0},{12,4},{16,8},{20,12},{24,16},{28,20},{1,25},{... | collective-permute-start | bytes 786440 | tf_op jit(solution)/shard_map/ppermute | solution.py:342
  85.5 34.0 %collective-permute-start.6 = (f32[4,128,128]{2,1,0:T(8,128)S(1)}, f32[4,128,128]{2,1,0:T(8,128)S(1)}, u32[]{:S(2)}, u32[]{:S(2)}) collective-permute-start(f32[4,128,128]{2,1,0:T(8,128)S(1)} %get-tuple-element.17), channel_id=1, source_target_pairs={{0,28},{4,0},{8,4},{12,8},{16,12},{20,16},{24,20},{28,24},{1,29},{... | collective-permute-start | bytes 786440 | tf_op jit(solution)/shard_map/ppermute | solution.py:342
  87.5 33.3 %collective-permute-start = (f32[4,128,128]{2,1,0:T(8,128)}, f32[4,128,128]{2,1,0:T(8,128)}, u32[]{:S(2)}, u32[]{:S(2)}) collective-permute-start(f32[4,128,128]{2,1,0:T(8,128)} %get-tuple-element.23), channel_id=1, source_target_pairs={{0,4},{4,8},{8,12},{12,16},{16,20},{20,24},{24,28},{28,0},{1,5},{5... | collective-permute-start | bytes 786440 | tf_op jit(solution)/shard_map/ppermute | solution.py:342
  88.5 32.3 %collective-permute-start.1 = (f32[4,128,128]{2,1,0:T(8,128)}, f32[4,128,128]{2,1,0:T(8,128)}, u32[]{:S(2)}, u32[]{:S(2)}) collective-permute-start(f32[4,128,128]{2,1,0:T(8,128)} %get-tuple-element.22), channel_id=1, source_target_pairs={{0,8},{4,12},{8,16},{12,20},{16,24},{20,28},{24,0},{28,4},{1,9},{5... | collective-permute-start | bytes 786440 | tf_op jit(solution)/shard_map/ppermute | solution.py:342
  89.0 40.3 %collective-permute-start.2 = (f32[4,128,128]{2,1,0:T(8,128)}, f32[4,128,128]{2,1,0:T(8,128)}, u32[]{:S(2)}, u32[]{:S(2)}) collective-permute-start(f32[4,128,128]{2,1,0:T(8,128)} %get-tuple-element.21), channel_id=1, source_target_pairs={{0,12},{4,16},{8,20},{12,24},{16,28},{20,0},{24,4},{28,8},{1,13},{... | collective-permute-start | bytes 786440 | tf_op jit(solution)/shard_map/ppermute | solution.py:342
  97.4 33.5 %collective-permute-start.3 = (f32[4,128,128]{2,1,0:T(8,128)}, f32[4,128,128]{2,1,0:T(8,128)}, u32[]{:S(2)}, u32[]{:S(2)}) collective-permute-start(f32[4,128,128]{2,1,0:T(8,128)} %get-tuple-element.20), channel_id=1, source_target_pairs={{0,16},{4,20},{8,24},{12,28},{16,0},{20,4},{24,8},{28,12},{1,17},{... | collective-permute-start | bytes 786440 | tf_op jit(solution)/shard_map/ppermute | solution.py:342
  119.5 18.9 %collective-permute-start.4 = (f32[4,128,128]{2,1,0:T(8,128)}, f32[4,128,128]{2,1,0:T(8,128)}, u32[]{:S(2)}, u32[]{:S(2)}) collective-permute-start(f32[4,128,128]{2,1,0:T(8,128)} %get-tuple-element.19), channel_id=1, source_target_pairs={{0,20},{4,24},{8,28},{12,0},{16,4},{20,8},{24,12},{28,16},{1,21},{... | collective-permute-start | bytes 786440 | tf_op jit(solution)/shard_map/ppermute | solution.py:342
  153.5 56.1 %copy-start.3 = (f32[2,128,4096]{2,1,0:T(8,128)S(1)}, f32[2,128,4096]{2,1,0:T(8,128)}, u32[]{:S(2)}) copy-start(f32[2,128,4096]{2,1,0:T(8,128)} %get-tuple-element.16.wave_ref) | copy-start | bytes 12582916
  153.6 56.0 %copy-start.6 = (f32[2,32,128]{2,1,0:T(8,128)S(1)}, f32[2,32,128]{2,1,0:T(8,128)}, u32[]{:S(2)}) copy-start(f32[2,32,128]{2,1,0:T(8,128)} %pad_maximum_fusion.tw_ref) | copy-start | bytes 98308
  214.6 1.3 copy-start.2
Sparse Core Ops, SparseCore 0:
  9.1 44.1 all-gather.1
  216.0 42.7 reduce-scatter.1

commit v3 on v2

--- a/solution.py
+++ b/solution.py
@@ -1,3 +1,4 @@
+import functools
 import math
 
 import jax
@@ -13,7 +14,8 @@
 OUTER = 32
 INNER = 128
 BLOCK = 16
-WIDE = 4
+WIDE = 16
+NOTE = 8
 F32 = jnp.float32
 BF16 = jnp.bfloat16
 
@@ -114,15 +116,68 @@
     return slice(index * INNER, (index + 1) * INNER)
 
 
-def sort_kernel(target_ref, out_ref, turned_ref):
+def sort_kernel(depth_ref, target_ref, out_ref, turned_ref):
     for k in range(OUTER):
         turned_ref[tile(k), :] = target_ref[:, tile(k)].T
     for j in range(OUTER):
-        out_ref[j] = turned_ref[pl.ds(j, INNER, stride=OUTER), :].T
-
-
-def rows_kernel(phase_ref, row_ref, col_ref, tw_ref, dft_ref, out_hbm, wave_hbm, high_ref, low_ref, mid_ref, sh_ref, sl_ref, out_ref, wave_ref, sem):
+        out_ref[j, :INNER] = turned_ref[pl.ds(j, INNER, stride=OUTER), :].T
+        out_ref[j, INNER:] = jnp.full((NOTE, INNER), depth_ref[0].astype(F32))
+
+
+def rows_kernel(
+    length, place_ref, phase_ref, targets_hbm, out_hbm, wave_hbm, tw_ref, tall_ref, dft_ref, *refs
+):
+    sent = refs[:-12]
+    high_ref, low_ref, mid_ref, sh_ref, sl_ref, out_ref, wave_ref, row_ref, col_ref, note_ref, sem, send_sem = refs[-12:]
+    layers = len(sent) + 1
+    group = targets_hbm.shape[0] // layers
+    layer = place_ref[0]
+
+    note = pltpu.make_async_copy(targets_hbm.at[layer * group, pl.ds(INNER, NOTE)], note_ref, sem.at[2])
+    note.start()
+    sends = [
+        pltpu.make_async_copy(
+            targets_hbm.at[pl.ds(lax.rem(layer + k, layers) * group, group), pl.ds(0, INNER)],
+            sent[k - 1],
+            send_sem.at[k - 1],
+        )
+        for k in range(1, layers)
+    ]
+    for send in sends:
+        send.start()
+    note.wait()
+    modulus = 2 * length
+    weight = inverse_odd(
+        ((note_ref[0:1, :].astype(jnp.int32) + 8) * (length // 64) + 1) & (modulus - 1), modulus
+    )
+
+    def index(shape, axis):
+        return lax.broadcasted_iota(jnp.int32, shape, axis)
+
+    def waves(steps, size):
+        return unit_wave(steps.astype(F32) * (-1.0 / size))
+
+    flat = (OUTER, INNER)
+    tw_ref[0], tw_ref[1] = waves((index(flat, 0) * index(flat, 1) * weight) & (length - 1), length)
+    tall = (INNER, OUTER)
+    tall_ref[0], tall_ref[1] = waves(
+        (index(tall, 0) * index(tall, 1) * weight[:, :OUTER]) & (length - 1), length
+    )
+    square = (INNER, INNER)
+    steps = (index(square, 0) * index(square, 1)) & (INNER - 1)
+    cos, sin = waves((steps * (weight & (INNER - 1))) & (INNER - 1), INNER)
+    cos, sin = cos * (1.0 / math.sqrt(length)), sin * (1.0 / math.sqrt(length))
+    dft_ref[:INNER, :INNER], dft_ref[:INNER, INNER:] = cos, sin
+    dft_ref[INNER:, :INNER], dft_ref[INNER:, INNER:] = -sin, cos
     high_ref[...], low_ref[...] = split(dft_ref[...])
+
+    def chirp(pixel):
+        return ((((pixel * pixel) & (modulus - 1)) * weight) & (modulus - 1)).astype(F32) * (1.0 / modulus)
+
+    col_ref[...] = chirp(index(flat, 0) * INNER + index(flat, 1))
+    local = index(square, 0)
+    inside = local & (BLOCK - 1)
+    row_ref[...] = chirp((local - inside) * (length // layers // BLOCK) + place_ref[1] + inside)
 
     def save_wave(step):
         rows = row_block(step)
@@ -137,7 +192,7 @@
         row_turn = row_ref[rows, :]
 
         def load(k):
-            turns = phase_ref[rows, tile(k)] * (0.5 / math.pi) + (row_turn + col_ref[:, tile(k)])
+            turns = phase_ref[rows, tile(k)] * (0.5 / math.pi) + (row_turn + col_ref[k : k + 1, :])
             cos, sin = unit_wave(turns)
             wave_ref[0, rows, tile(k)] = cos
             wave_ref[1, rows, tile(k)] = sin
@@ -161,7 +216,10 @@
         group = pl.ds(step * 4, 4)
         high = sh_ref[group].reshape(4 * INNER, 2 * INNER)
         low = sl_ref[group].reshape(4 * INNER, 2 * INNER)
-        out = dot(high, high_ref[...]) + dot(low, high_ref[...]) + dot(high, low_ref[...])
+        out = dot(
+            jnp.concatenate([high, low, high], axis=1),
+            jnp.concatenate([high_ref[...], high_ref[...], low_ref[...]], axis=0),
+        )
         out = out.reshape(4, INNER, 2 * INNER)
         out_ref[group, 0] = out[:, :, :INNER]
         out_ref[group, 1] = out[:, :, INNER:]
@@ -171,26 +229,37 @@
     lax.fori_loop(0, OUTER // 4, multiply, 0)
     pltpu.make_async_copy(wave_ref, wave_hbm, sem.at[0]).wait()
     pltpu.make_async_copy(out_ref, out_hbm, sem.at[1]).wait()
+    for send in sends:
+        send.wait()
 
 
 def columns_kernel(
-    scale, layer_ref, in_ref, *refs
+    scale, layer_ref, tw_ref, there_ref, in_hbm, *refs
 ):
-    pieces, refs = refs[: len(refs) - 11], refs[len(refs) - 11 :]
-    tw_ref, there_ref, home_ref, out_ref, there_both, home_both, mid_ref, sh_ref, sl_ref, back_ref, target_ref = refs
-    for both, ref in ((there_both, home_ref), (home_both, there_ref)):
-        both[: 2 * INNER, :], both[2 * INNER :, :] = split(ref[...])
-
-    layers = len(pieces)
+    pieces_hbm, refs = refs[: len(refs) - 11], refs[len(refs) - 11 :]
+    out_ref, there_both, home_both, mid_ref, sh_ref, sl_ref, back_ref, target_ref, in_ref, pieces_ref, sem = refs
+    layers = len(pieces_hbm)
     run = INNER // layers
-    for k, piece in enumerate(pieces):
-        start = lax.rem(layer_ref[0] + (layers - k), layers) * run
-        spot = pl.ds(pl.multiple_of(start, run), run)
-        for u0 in range(OUTER):
-            target_ref[u0, spot, :] = piece[pl.ds(u0, run, stride=OUTER), :]
+
+    def fetch(step):
+        group = pl.ds(step * 4, 4)
+        return pltpu.make_async_copy(in_hbm.at[group], in_ref.at[group], sem.at[step])
+
+    def fetch_piece(k):
+        return pltpu.make_async_copy(pieces_hbm[k], pieces_ref.at[k], sem.at[INNER // BLOCK + k])
+
+    for step in range(INNER // BLOCK):
+        fetch(step).start()
+    for k in range(layers):
+        fetch_piece(k).start()
+
+    for both, matrix in ((there_both, transposed(there_ref)), (home_both, there_ref[...])):
+        high, low = split(matrix)
+        both[...] = jnp.concatenate([high, low, high], axis=1)
 
     def forward(step, carry):
         rows = row_block(step)
+        fetch(step).wait()
 
         def load(k):
             return tuple(in_ref[step * 4 + k % 4, side, tile_rows(k // 4), :] for side in (0, 1))
@@ -208,12 +277,18 @@
 
     lax.fori_loop(0, INNER // BLOCK, forward, 0)
 
+    for k in range(layers):
+        fetch_piece(k).wait()
+        start = lax.rem(layer_ref[0] + (layers - k), layers) * run
+        spot = pl.ds(pl.multiple_of(start, run), run)
+        for u0 in range(OUTER):
+            target_ref[u0, spot, :] = pieces_ref[k, pl.ds(u0, run, stride=OUTER), :]
+
     def wide(ref, first):
         return jnp.concatenate([ref[first + k].reshape(2 * INNER, INNER) for k in range(WIDE)], axis=1)
 
     def product(table_ref, high, low):
-        out = dot(table_ref[...], high)
-        return out[: 2 * INNER] + (out[2 * INNER :] + dot(table_ref[: 2 * INNER, :], low))
+        return dot(table_ref[...], jnp.concatenate([high, high, low], axis=0))
 
     def multiply(step, carry):
         first = step * WIDE
@@ -246,18 +321,31 @@
     lax.fori_loop(0, INNER // BLOCK, backward, 0)
 
 
+def transposed(ref):
+    return jnp.concatenate(
+        [
+            jnp.concatenate([ref[:INNER, :INNER], ref[INNER:, :INNER]], axis=1),
+            jnp.concatenate([ref[:INNER, INNER:], ref[INNER:, INNER:]], axis=1),
+        ],
+        axis=0,
+    )
+
+
 def tile_rows(index):
     return slice(index * BLOCK, (index + 1) * BLOCK)
 
 
 def gradient_kernel(in_ref, wave_ref, tw_ref, dft_ref, out_ref, high_ref, low_ref, mid_ref, back_ref):
-    high_ref[...], low_ref[...] = split(dft_ref[...])
+    high_ref[...], low_ref[...] = split(transposed(dft_ref))
 
     def multiply(step, carry):
         group = pl.ds(step * 4, 4)
         both = jnp.concatenate([in_ref[group, 0], in_ref[group, 1]], axis=-1).reshape(4 * INNER, 2 * INNER)
         high, low = split(both)
-        out = dot(high, high_ref[...]) + dot(low, high_ref[...]) + dot(high, low_ref[...])
+        out = dot(
+            jnp.concatenate([high, low, high], axis=1),
+            jnp.concatenate([high_ref[...], high_ref[...], low_ref[...]], axis=0),
+        )
         back_ref[group] = out.reshape(4, INNER, 2 * INNER)
         return carry
 
@@ -280,12 +368,17 @@
     lax.fori_loop(0, INNER // BLOCK, block, 0)
 
 
-def call(kernel, out_shapes, scratch, *args, space=pltpu.VMEM, limit=28):
+def call(kernel, out_shapes, scratch, *args, direct=(), limit=28, held=0):
     return pl.pallas_call(
         kernel,
         out_shape=[jax.ShapeDtypeStruct(shape, F32) for shape in out_shapes],
-        in_specs=[pl.BlockSpec(memory_space=pltpu.SMEM if arg.dtype == jnp.int32 else pltpu.VMEM) for arg in args],
-        out_specs=[pl.BlockSpec(memory_space=space)] * len(out_shapes),
+        in_specs=[
+            pl.BlockSpec(
+                memory_space=pltpu.SMEM if arg.dtype == jnp.int32 else pl.ANY if k >= len(args) - held else pltpu.VMEM
+            )
+            for k, arg in enumerate(args)
+        ],
+        out_specs=[pl.BlockSpec(memory_space=pltpu.HBM if k in direct else pltpu.VMEM) for k in range(len(out_shapes))],
         scratch_shapes=[pltpu.VMEM(*item) if isinstance(item, tuple) else item for item in scratch],
         compiler_params=pltpu.CompilerParams(vmem_limit_bytes=limit * 2**20),
     )(*args)
@@ -294,20 +387,8 @@
 def inverse_odd(value, modulus):
     result = value
     for _ in range(4):
-        result = result * ((2 - value * result) % modulus) % modulus
+        result = (result * ((2 - value * result) & (modulus - 1))) & (modulus - 1)
     return result
-
-
-def turns_of(steps, modulus):
-    return steps.astype(F32) * (1.0 / modulus)
-
-
-def table(weight, length, sign):
-    index = jnp.arange(INNER, dtype=jnp.int32)
-    steps = (index[:, None] * index[None, :] % INNER) * (weight % INNER) % INNER
-    angle = steps.astype(F32) * (sign * 2.0 * math.pi / INNER)
-    cos, sin = jnp.cos(angle) / math.sqrt(length), jnp.sin(angle) / math.sqrt(length)
-    return jnp.block([[cos, sin], [-sin, cos]])
 
 
 def on_device(phase, depths, targets):
@@ -316,57 +397,38 @@
     layers = lax.axis_size("z")
     place = lax.axis_index("xl") * lax.axis_size("y") + lax.axis_index("y")
     slab_size = math.prod(lax.axis_size(axis) for axis in SLAB)
-    modulus = 2 * length
-
     share = rows_dev // planes
     mine = lax.dynamic_slice_in_dim(phase, place * share, share, 0)
     mine, targets = lax.optimization_barrier((mine, targets))
     rows_phase = lax.all_gather(mine, "z", axis=0, tiled=True)
 
-    all_depths = lax.all_gather(depths, ("xl", "y"), axis=0, tiled=True)
-    depth = lax.dynamic_index_in_dim(all_depths, lax.axis_index("z"), keepdims=False)
     (sorted_targets,) = call(
         sort_kernel,
-        [(slab_size, rows_dev, INNER)],
+        [(slab_size, rows_dev + NOTE, INNER)],
         [((length, rows_dev), F32)],
+        depths,
         targets[0],
+        limit=60,
     )
     sorted_targets = lax.all_to_all(sorted_targets, SLAB, 0, 0, tiled=True)
-    rows_phase, sorted_targets = lax.optimization_barrier((rows_phase, sorted_targets))
     layer = lax.axis_index("z")
     group = slab_size // layers
-    pieces = []
-    for k in range(layers):
-        piece = lax.dynamic_slice_in_dim(sorted_targets, (layer + k) % layers * group, group, 0)
-        if k:
-            piece = lax.ppermute(piece, "z", [(i, (i + k) % layers) for i in range(layers)])
-        pieces.append(piece.reshape(group * rows_dev, INNER))
-
-    strength = ((depth + 8) * (length // 64) + 1) % modulus
-    weight = inverse_odd(strength, modulus)
-
-    pixel = jnp.arange(length, dtype=jnp.int32)
-    chirp = turns_of(pixel * pixel % modulus * weight % modulus, modulus)
-    slot = lax.axis_index("xh") * lax.axis_size("c") + lax.axis_index("c")
-    local = jnp.arange(layers * share, dtype=jnp.int32)
-    row = (local // share * (length // layers)) + slot * rows_dev + place * share + local % share
-    row_chirp = turns_of(row * row % modulus * weight % modulus, modulus)
-    row_chirp = jnp.broadcast_to(row_chirp[:, None], (layers * share, INNER))
-
-    outer = jnp.arange(OUTER, dtype=jnp.int32)[:, None]
-    inner = jnp.arange(INNER, dtype=jnp.int32)[None, :]
-    angle = (outer * inner * weight % length).astype(F32) * (-2.0 * math.pi / length)
-    twiddle = jnp.stack([jnp.cos(angle), jnp.sin(angle)])
-    tall_twiddle = jnp.stack([jnp.cos(angle.T), jnp.sin(angle.T)])
-    there = table(weight, length, -1.0)
-    back = table(weight, length, 1.0)
+    layer_index = layer.astype(jnp.int32)
+    first_row = (lax.axis_index("xh") * lax.axis_size("c") + lax.axis_index("c")) * rows_dev + place * share
 
     mid = ((OUTER, 2, BLOCK, INNER), F32)
     matrix = ((2 * INNER, 2 * INNER), BF16)
     chunks = (slab_size, 2, layers * share, INNER)
-    spectrum, wave = call(
-        rows_kernel,
-        [chunks, (2, layers * share, length)],
+    spectrum, wave, twiddle, tall_twiddle, there, *sent = call(
+        functools.partial(rows_kernel, length),
+        [
+            chunks,
+            (2, layers * share, length),
+            (2, OUTER, INNER),
+            (2, INNER, OUTER),
+            (2 * INNER, 2 * INNER),
+        ]
+        + [(group, rows_dev, INNER)] * (layers - 1),
         [
             matrix,
             matrix,
@@ -375,35 +437,46 @@
             ((OUTER, INNER, 2 * INNER), BF16),
             (chunks, F32),
             ((2, layers * share, length), F32),
-            pltpu.SemaphoreType.DMA((2,)),
+            ((INNER, INNER), F32),
+            ((OUTER, INNER), F32),
+            ((NOTE, INNER), F32),
+            pltpu.SemaphoreType.DMA((3,)),
+            pltpu.SemaphoreType.DMA((layers - 1,)),
         ],
+        jnp.stack([layer_index, first_row.astype(jnp.int32)]),
         rows_phase,
-        row_chirp,
-        chirp[None, :],
-        twiddle,
-        there,
-        space=pltpu.HBM,
+        sorted_targets,
+        held=1,
+        direct=(0, 1) + tuple(range(5, 4 + layers)),
         limit=60,
     )
+    own = lax.dynamic_slice(sorted_targets, (layer * group, 0, 0), (group, rows_dev, INNER))
+    pieces = [own] + [
+        lax.ppermute(piece, "z", [(i, (i + k) % layers) for i in range(layers)]) for k, piece in enumerate(sent, 1)
+    ]
+    pieces = [piece.reshape(group * rows_dev, INNER) for piece in pieces]
     spectrum = lax.all_to_all(spectrum, SLAB, 0, 0, tiled=True)
     (spectrum,) = call(
         lambda *refs: columns_kernel(4.0 / planes, *refs),
         [chunks],
         [
-            ((4 * INNER, 2 * INNER), BF16),
-            ((4 * INNER, 2 * INNER), BF16),
+            ((2 * INNER, 6 * INNER), BF16),
+            ((2 * INNER, 6 * INNER), BF16),
             mid,
             ((OUTER, 2, INNER, INNER), BF16),
             ((OUTER, 2, INNER, INNER), BF16),
             ((OUTER, 2, INNER, INNER), F32),
             ((OUTER, INNER, INNER), F32),
+            (chunks, F32),
+            ((layers, group * rows_dev, INNER), F32),
+            pltpu.SemaphoreType.DMA((INNER // BLOCK + layers,)),
         ],
-        layer.astype(jnp.int32)[None],
+        layer_index[None],
+        tall_twiddle,
+        there,
         spectrum,
         *pieces,
-        tall_twiddle,
-        there,
-        back,
+        held=1 + layers,
     )
     spectrum = lax.all_to_all(spectrum, SLAB, 0, 0, tiled=True)
     (part,) = call(
@@ -413,7 +486,7 @@
         spectrum,
         wave,
         twiddle,
-        back,
+        there,
     )
     part = lax.psum_scatter(part, "z", scatter_dimension=0, tiled=True)
     part = jnp.broadcast_to(part[None], (planes, share, length))

time: 296 us -> 327 us (1.10)
  Pallas kernels: 31.6 us -> 80.2 us
  blocking collectives: 114 us -> 83.6 us
  waiting for transfers between devices: 84.6 us -> 106 us
  local copies, waits for them, and re-layouts: 14.3 us -> 7.08 us
  other arithmetic: 4.96 us -> 0.59 us
  starting transfers between devices: 31 us -> 34.5 us
    pallas_call x4, Pallas kernels: 31.6 us -> 80.2 us  [call(): pl.pallas_call(kernel, out_shape=[jax.ShapeDtypeStruct(shape, F32) for sh...]
    unnamed x1 -> x0, blocking collectives: 30.5 us -> none
    all_to_all x1, waiting for transfers between devices: 0.01 us -> 26.7 us  [on_device(): sorted_targets = lax.all_to_all(sorted_targets, SLAB, 0, 0, tiled=True)]
    ppermute x7, waiting for transfers between devices: 41.7 us -> 34.8 us  [on_device(): lax.ppermute(piece, 'z', [(i, (i + k) % layers) for i in range(layers)])]
    unnamed x20 -> x15, local copies, waits for them, and re-layouts: 8.41 us -> 4.24 us
    all_gather x1, waiting for transfers between devices: 0.01 us -> 4.15 us  [on_device(): rows_phase = lax.all_gather(mine, 'z', axis=0, tiled=True)]
    ppermute x7, starting transfers between devices: 15.2 us -> 19.2 us  [on_device(): lax.ppermute(piece, 'z', [(i, (i + k) % layers) for i in range(layers)])]
  transfers between devices with their start and end apart: 11 -> 11, of which waited for: 6 -> 7; matrix products, arithmetic and copies ran while one was open for 3% -> 0% of each run, Pallas kernels for 1% -> 1%
where the time goes in v3:
time: 327 us; the launch traced here: 326 us
  waiting for transfers between devices  106 us (32%)
  blocking collectives  83.6 us (26%)
  Pallas kernels  80.2 us (25%)
  starting transfers between devices  34.5 us (11%)
  between operations  14.2 us (4%)
  local copies, waits for them, and re-layouts  7.08 us (2%)
    pallas_call x4, Pallas kernels, call(): pl.pallas_call(kernel, out_shape=[jax.ShapeDtypeStruct(shape, F32) for sh...  80.2 us
    all_to_all x1, blocking collectives, on_device(): spectrum = lax.all_to_all(spectrum, SLAB, 0, 0, tiled=True)  56 us
    reduce_scatter x1, waiting for transfers between devices, on_device(): part = lax.psum_scatter(part, 'z', scatter_dimension=0, tiled=True)  40.4 us
    ppermute x7, waiting for transfers between devices, on_device(): lax.ppermute(piece, 'z', [(i, (i + k) % layers) for i in range(layers)])  34.8 us
    all_to_all x1, blocking collectives, on_device(): lax.all_to_all(part, ('xl', 'y'), 0, 0, tiled=True)  27.6 us
    all_to_all x1, waiting for transfers between devices, on_device(): sorted_targets = lax.all_to_all(sorted_targets, SLAB, 0, 0, tiled=True)  26.7 us
    ppermute x7, starting transfers between devices, on_device(): lax.ppermute(piece, 'z', [(i, (i + k) % layers) for i in range(layers)])  19.2 us
    all_to_all x1, starting transfers between devices, on_device(): sorted_targets = lax.all_to_all(sorted_targets, SLAB, 0, 0, tiled=True)  7.64 us
  transfers between devices with their start and end apart: 11, of which 7 were waited for; matrix products, arithmetic and copies ran while one was open for 0% of the time, Pallas kernels for 1%

profile of v3, /device:TPU:4, one launch (start us, length us, event | category | flops | bytes accessed | tf_op | source)
XLA Modules:
  0.0 326.2 jit_solution(14291829246413345595)
XLA Ops:
  6.5 1.6 copy-done
  8.1 0.7 constant_dynamic-slice_fusion.1
  8.8 0.0 all-gather.2.cloned.1.call-update
  9.5 4.7 %shard_map.37 = f32[32,136,128]{2,1,0:T(8,128)} custom-call(s32[1]{0:T(128)S(6)} %copy.5.depth_ref, f32[128,4096]{1,0:T(8,128)} %bitcast.17), custom_call_target="tpu_custom_call" | custom-call | tf_op jit(solution)/shard_map/pallas_call | solution.py:372
  14.2 7.6 %all-to-all-start = ((f32[32,136,128]{2,1,0:T(8,128)}), f32[32,136,128]{2,1,0:T(8,128)}, u32[]{:S(2)}, u32[]{:S(2)}) async-start(f32[32,136,128]{2,1,0:T(8,128)} %shard_map.37), calls=%async_computation | async-start | bytes 4456448 | tf_op jit(solution)/shard_map/all_to_all | solution.py:413
  21.9 0.6 pad_add_fusion.place_ref
  22.5 26.7 %all-to-all-done.targets_hbm = f32[32,136,128]{2,1,0:T(8,128)} async-done(((f32[32,136,128]{2,1,0:T(8,128)}), f32[32,136,128]{2,1,0:T(8,128)}, u32[]{:S(2)}, u32[]{:S(2)}) %all-to-all-start) | async-done | bytes 2228256 | tf_op jit(solution)/shard_map/all_to_all | solution.py:413
  49.2 4.1 %all-gather.2.cloned.1.call-done.phase_ref = f32[128,4096]{1,0:T(8,128)} async-done(((f32[16,4096]{1,0:T(8,128)}), f32[128,4096]{1,0:T(8,128)}) %all-gather.2.cloned.1.call-update) | async-done | bytes 2097168 | tf_op jit(solution)/shard_map/all_gather | solution.py:403
  53.3 59.1 %shard_map.38 = (f32[32,2,128,128]{3,2,1,0:T(8,128)}, f32[2,128,4096]{2,1,0:T(8,128)}, f32[2,32,128]{2,1,0:T(8,128)}, f32[2,128,32]{2,1,0:T(8,128)}, f32[256,256...) custom-call(s32[2]{0:T(128)} %pad_add_fusion.place_ref, ...), custom_call_target="tpu_custom_call" | custom-call | tf_op jit(solution)/shard_map/pallas_call | solution.py:372
  112.5 7.6 %all-to-all-start.1 = ((f32[32,2,128,128]{3,2,1,0:T(8,128)}), f32[32,2,128,128]{3,2,1,0:T(8,128)}, u32[]{:S(2)}, u32[]{:S(2)}) async-start(f32[32,2,128,128]{3,2,1,0:T(8,128)} %get-tuple-element.23), calls=%async_computation.1 | async-start | bytes 8388608 | tf_op jit(solution)/shard_map/all_to_all | solution.py:458
  120.2 0.0 reduce-scatter.2.cloned.1.call-start
  120.2 1.2 collective-permute-start
  121.4 2.0 collective-permute-start.1
  123.4 3.7 %collective-permute-start.2 = (f32[4,128,128]{2,1,0:T(8,128)}, f32[4,128,128]{2,1,0:T(8,128)S(1)}, u32[]{:S(2)}, u32[]{:S(2)}) collective-permute-start(f32[4,128,128]{2,1,0:T(8,128)} %get-tuple-element.26), channel_id=1, source_target_pairs={{0,12},{4,16},{8,20},{12,24},{16,28},{20,0},{24,4},{28,8},{1,13},{... | collective-permute-start | bytes 786440 | tf_op jit(solution)/shard_map/ppermute | solution.py:455
  127.1 0.9 collective-permute-start.3
  128.0 4.6 %collective-permute-start.4 = (f32[4,128,128]{2,1,0:T(8,128)}, f32[4,128,128]{2,1,0:T(8,128)}, u32[]{:S(2)}, u32[]{:S(2)}) collective-permute-start(f32[4,128,128]{2,1,0:T(8,128)} %get-tuple-element.28), channel_id=1, source_target_pairs={{0,20},{4,24},{8,28},{12,0},{16,4},{20,8},{24,12},{28,16},{1,21},{... | collective-permute-start | bytes 786440 | tf_op jit(solution)/shard_map/ppermute | solution.py:455
  132.6 3.6 %collective-permute-start.5 = (f32[4,128,128]{2,1,0:T(8,128)}, f32[4,128,128]{2,1,0:T(8,128)}, u32[]{:S(2)}, u32[]{:S(2)}) collective-permute-start(f32[4,128,128]{2,1,0:T(8,128)} %get-tuple-element.29), channel_id=1, source_target_pairs={{0,24},{4,28},{8,0},{12,4},{16,8},{20,12},{24,16},{28,20},{1,25},{... | collective-permute-start | bytes 786440 | tf_op jit(solution)/shard_map/ppermute | solution.py:455
  136.2 8.9 %collective-permute-done.1 = f32[4,128,128]{2,1,0:T(8,128)S(1)} collective-permute-done((f32[4,128,128]{2,1,0:T(8,128)S(1)}, f32[4,128,128]{2,1,0:T(8,128)S(1)}, u32[]{:S(2)}, u32[]{:S(2)}) %collective-permute-start.1) | collective-permute-done | bytes 262176 | tf_op jit(solution)/shard_map/ppermute | solution.py:455
  145.0 3.2 collective-permute-start.6
  148.3 1.0 constant_dynamic-slice_fusion
  149.2 15.6 %collective-permute-done.2 = f32[4,128,128]{2,1,0:T(8,128)S(1)} collective-permute-done((f32[4,128,128]{2,1,0:T(8,128)}, f32[4,128,128]{2,1,0:T(8,128)S(1)}, u32[]{:S(2)}, u32[]{:S(2)}) %collective-permute-start.2) | collective-permute-done | bytes 262176 | tf_op jit(solution)/shard_map/ppermute | solution.py:455
  164.8 6.7 %collective-permute-done.5 = f32[4,128,128]{2,1,0:T(8,128)} collective-permute-done((f32[4,128,128]{2,1,0:T(8,128)}, f32[4,128,128]{2,1,0:T(8,128)}, u32[]{:S(2)}, u32[]{:S(2)}) %collective-permute-start.5) | collective-permute-done | bytes 262176 | tf_op jit(solution)/shard_map/ppermute | solution.py:455
  171.6 3.6 %collective-permute-done.6 = f32[4,128,128]{2,1,0:T(8,128)} collective-permute-done((f32[4,128,128]{2,1,0:T(8,128)}, f32[4,128,128]{2,1,0:T(8,128)}, u32[]{:S(2)}, u32[]{:S(2)}) %collective-permute-start.6) | collective-permute-done | bytes 262176 | tf_op jit(solution)/shard_map/ppermute | solution.py:455
  175.1 11.5 %shard_map.39 = f32[32,2,128,128]{3,2,1,0:T(8,128)S(1)} custom-call(s32[1]{0:T(128)} %bitcast.refs_0_, f32[2,128,32]{2,1,0:T(8,128)S(1)} %copy-done.4, f32[256,256]{1,0:T(8,128)S(1)} %copy-done.3, f32[32,2,128,128]{3,2,1,0:T(8,128)} %all-to-all-done.1.refs_3_, f32[512,128]{1,0:T(8,128)S(1)} %bitcast.12, f32[512,128]{1,0:T(8,128)S(1)} %bitcast.13, ...), custom_call_target="tpu_custom_call" | custom-call | tf_op jit(solution)/shard_map/pallas_call | solution.py:372
  186.6 56.0 %all_to_all.20.in_ref = f32[32,2,128,128]{3,2,1,0:T(8,128)S(1)} all-to-all(f32[32,2,128,128]{3,2,1,0:T(8,128)S(1)} %shard_map.39), channel_id=1, replica_groups=mesh['xl'=2,'y'=4,'z'=8,'xh'=2,'c'=2] {'xl','y','xh','c'}, dimensions={0} | all-to-all | bytes 8388608 | tf_op jit(solution)/shard_map/all_to_all | solution.py:481
  242.7 4.9 %shard_map.40 = f32[128,4096]{1,0:T(8,128)S(1)} custom-call(f32[32,2,128,128]{3,2,1,0:T(8,128)S(1)} %all_to_all.20.in_ref, f32[2,128,4096]{2,1,0:T(8,128)S(1)} %copy-done.2, f32[2,32,128]{2,1,0:T(8,128)S(1)} %copy-done.5, f32[256,256]{1,0:T(8,128)S(1)} %copy-done.3), custom_call_target="tpu_custom_call" | custom-call | tf_op jit(solution)/shard_map/pallas_call | solution.py:372
  247.6 1.3 copy-done.1
  248.9 0.0 reduce-scatter.2.cloned.1.call-update
  248.9 40.4 %reduce-scatter.2.cloned.1.call-done = f32[16,4096]{1,0:T(8,128)} async-done(((f32[128,4096]{1,0:T(8,128)}), f32[16,4096]{1,0:T(8,128)}) %reduce-scatter.2.cloned.1.call-update) | async-done | bytes 262160 | tf_op jit(solution)/shard_map/reduce_scatter | solution.py:491
  289.3 1.1 broadcast_in_dim.10
  290.4 27.6 %all_to_all.21 = f32[8,16,4096]{2,1,0:T(8,128)S(1)} all-to-all(f32[8,16,4096]{2,1,0:T(8,128)S(1)} %broadcast_in_dim.10), channel_id=1, replica_groups=mesh['xl'=2,'y'=4,'z'=8,'xh'=2,'c'=2] {'xl','y'}, dimensions={0} | all-to-all | bytes 4194304 | tf_op jit(solution)/shard_map/all_to_all | solution.py:493
  318.1 1.3 copy.6
  (17 shorter events, 0.0 us)
Async XLA Ops:
  6.5 1.6 copy-start
  6.5 46.8 %all-gather.2.cloned.1.call-start = ((), (), s32[]{:S(2)}) async-start(), calls=%async_computation.5 | async-start | bytes 2359296 | tf_op jit(solution)/shard_map/all_gather | solution.py:403
  14.2 34.9 %all-to-all-start = ((f32[32,136,128]{2,1,0:T(8,128)}), f32[32,136,128]{2,1,0:T(8,128)}, u32[]{:S(2)}, u32[]{:S(2)}) async-start(f32[32,136,128]{2,1,0:T(8,128)} %shard_map.37), calls=%async_computation | async-start | bytes 4456448 | tf_op jit(solution)/shard_map/all_to_all | solution.py:413
  112.5 8.9 %copy-start.6 = (f32[4,128,128]{2,1,0:T(8,128)S(1)}, f32[4,128,128]{2,1,0:T(8,128)}, u32[]{:S(2)}) copy-start(f32[4,128,128]{2,1,0:T(8,128)} %get-tuple-element.25) | copy-start | bytes 786436
  112.5 62.7 %copy-start.3 = (f32[256,256]{1,0:T(8,128)S(1)}, f32[256,256]{1,0:T(8,128)}, u32[]{:S(2)}) copy-start(f32[256,256]{1,0:T(8,128)} %get-tuple-element.22.refs_2_.dft_ref) | copy-start | bytes 786436
  112.5 62.6 %copy-start.4 = (f32[2,128,32]{2,1,0:T(8,128)S(1)}, f32[2,128,32]{2,1,0:T(8,128)}, u32[]{:S(2)}) copy-start(f32[2,128,32]{2,1,0:T(8,128)} %get-tuple-element.21.refs_1_) | copy-start | bytes 98308
  112.5 62.6 %all-to-all-start.1 = ((f32[32,2,128,128]{3,2,1,0:T(8,128)}), f32[32,2,128,128]{3,2,1,0:T(8,128)}, u32[]{:S(2)}, u32[]{:S(2)}) async-start(f32[32,2,128,128]{3,2,1,0:T(8,128)} %get-tuple-element.23), calls=%async_computation.1 | async-start | bytes 8388608 | tf_op jit(solution)/shard_map/all_to_all | solution.py:458
  120.2 169.1 %reduce-scatter.2.cloned.1.call-start = ((), (), s32[]{:S(2)}) async-start(), calls=%async_computation.6 | async-start | bytes 2359296 | tf_op jit(solution)/shard_map/reduce_scatter | solution.py:491
  120.2 12.4 %collective-permute-start = (f32[4,128,128]{2,1,0:T(8,128)}, f32[4,128,128]{2,1,0:T(8,128)S(1)}, u32[]{:S(2)}, u32[]{:S(2)}) collective-permute-start(f32[4,128,128]{2,1,0:T(8,128)} %get-tuple-element.24), channel_id=1, source_target_pairs={{0,4},{4,8},{8,12},{12,16},{16,20},{20,24},{24,28},{28,0},{1,5},{5... | collective-permute-start | bytes 786440 | tf_op jit(solution)/shard_map/ppermute | solution.py:455
  121.4 23.7 %collective-permute-start.1 = (f32[4,128,128]{2,1,0:T(8,128)S(1)}, f32[4,128,128]{2,1,0:T(8,128)S(1)}, u32[]{:S(2)}, u32[]{:S(2)}) collective-permute-start(f32[4,128,128]{2,1,0:T(8,128)S(1)} %copy-done.6), channel_id=1, source_target_pairs={{0,8},{4,12},{8,16},{12,20},{16,24},{20,28},{24,0},{28,4},{1,9},{5... | collective-permute-start | bytes 786440 | tf_op jit(solution)/shard_map/ppermute | solution.py:455
  123.4 41.4 %collective-permute-start.2 = (f32[4,128,128]{2,1,0:T(8,128)}, f32[4,128,128]{2,1,0:T(8,128)S(1)}, u32[]{:S(2)}, u32[]{:S(2)}) collective-permute-start(f32[4,128,128]{2,1,0:T(8,128)} %get-tuple-element.26), channel_id=1, source_target_pairs={{0,12},{4,16},{8,20},{12,24},{16,28},{20,0},{24,4},{28,8},{1,13},{... | collective-permute-start | bytes 786440 | tf_op jit(solution)/shard_map/ppermute | solution.py:455
  127.1 37.7 %collective-permute-start.3 = (f32[4,128,128]{2,1,0:T(8,128)}, f32[4,128,128]{2,1,0:T(8,128)}, u32[]{:S(2)}, u32[]{:S(2)}) collective-permute-start(f32[4,128,128]{2,1,0:T(8,128)} %get-tuple-element.27), channel_id=1, source_target_pairs={{0,16},{4,20},{8,24},{12,28},{16,0},{20,4},{24,8},{28,12},{1,17},{... | collective-permute-start | bytes 786440 | tf_op jit(solution)/shard_map/ppermute | solution.py:455
  128.0 36.9 %collective-permute-start.4 = (f32[4,128,128]{2,1,0:T(8,128)}, f32[4,128,128]{2,1,0:T(8,128)}, u32[]{:S(2)}, u32[]{:S(2)}) collective-permute-start(f32[4,128,128]{2,1,0:T(8,128)} %get-tuple-element.28), channel_id=1, source_target_pairs={{0,20},{4,24},{8,28},{12,0},{16,4},{20,8},{24,12},{28,16},{1,21},{... | collective-permute-start | bytes 786440 | tf_op jit(solution)/shard_map/ppermute | solution.py:455
  132.6 39.0 %collective-permute-start.5 = (f32[4,128,128]{2,1,0:T(8,128)}, f32[4,128,128]{2,1,0:T(8,128)}, u32[]{:S(2)}, u32[]{:S(2)}) collective-permute-start(f32[4,128,128]{2,1,0:T(8,128)} %get-tuple-element.29), channel_id=1, source_target_pairs={{0,24},{4,28},{8,0},{12,4},{16,8},{20,12},{24,16},{28,20},{1,25},{... | collective-permute-start | bytes 786440 | tf_op jit(solution)/shard_map/ppermute | solution.py:455
  145.0 30.1 %collective-permute-start.6 = (f32[4,128,128]{2,1,0:T(8,128)}, f32[4,128,128]{2,1,0:T(8,128)}, u32[]{:S(2)}, u32[]{:S(2)}) collective-permute-start(f32[4,128,128]{2,1,0:T(8,128)} %get-tuple-element.30), channel_id=1, source_target_pairs={{0,28},{4,0},{8,4},{12,8},{16,12},{20,16},{24,20},{28,24},{1,29},{... | collective-permute-start | bytes 786440 | tf_op jit(solution)/shard_map/ppermute | solution.py:455
  186.6 56.0 %copy-start.2 = (f32[2,128,4096]{2,1,0:T(8,128)S(1)}, f32[2,128,4096]{2,1,0:T(8,128)}, u32[]{:S(2)}) copy-start(f32[2,128,4096]{2,1,0:T(8,128)} %get-tuple-element.31.wave_ref) | copy-start | bytes 12582916
  186.6 56.0 %copy-start.5 = (f32[2,32,128]{2,1,0:T(8,128)S(1)}, f32[2,32,128]{2,1,0:T(8,128)}, u32[]{:S(2)}) copy-start(f32[2,32,128]{2,1,0:T(8,128)} %get-tuple-element.32.tw_ref) | copy-start | bytes 98308
  247.6 1.3 copy-start.1
Sparse Core Ops, SparseCore 0:
  9.1 44.1 all-gather.1
  249.0 40.1 reduce-scatter.1

commit v4 on v3

--- a/solution.py
+++ b/solution.py
@@ -127,24 +127,24 @@
 def rows_kernel(
     length, place_ref, phase_ref, targets_hbm, out_hbm, wave_hbm, tw_ref, tall_ref, dft_ref, *refs
 ):
-    sent = refs[:-12]
-    high_ref, low_ref, mid_ref, sh_ref, sl_ref, out_ref, wave_ref, row_ref, col_ref, note_ref, sem, send_sem = refs[-12:]
+    sent = refs[:-13]
+    high_ref, low_ref, mid_ref, sh_ref, sl_ref, out_ref, wave_ref, row_ref, col_ref, note_ref, stage_ref, sem, send_sem = refs[-13:]
     layers = len(sent) + 1
     group = targets_hbm.shape[0] // layers
     layer = place_ref[0]
 
     note = pltpu.make_async_copy(targets_hbm.at[layer * group, pl.ds(INNER, NOTE)], note_ref, sem.at[2])
     note.start()
+    stage = pltpu.make_async_copy(targets_hbm.at[:, pl.ds(0, INNER)], stage_ref, sem.at[3])
+    stage.start()
     sends = [
         pltpu.make_async_copy(
-            targets_hbm.at[pl.ds(lax.rem(layer + k, layers) * group, group), pl.ds(0, INNER)],
+            stage_ref.at[pl.ds(lax.rem(layer + k, layers) * group, group)],
             sent[k - 1],
             send_sem.at[k - 1],
         )
         for k in range(1, layers)
     ]
-    for send in sends:
-        send.start()
     note.wait()
     modulus = 2 * length
     weight = inverse_odd(
@@ -178,6 +178,10 @@
     local = index(square, 0)
     inside = local & (BLOCK - 1)
     row_ref[...] = chirp((local - inside) * (length // layers // BLOCK) + place_ref[1] + inside)
+
+    stage.wait()
+    for send in sends:
+        send.start()
 
     def save_wave(step):
         rows = row_block(step)
@@ -440,7 +444,8 @@
             ((INNER, INNER), F32),
             ((OUTER, INNER), F32),
             ((NOTE, INNER), F32),
-            pltpu.SemaphoreType.DMA((3,)),
+            ((slab_size, rows_dev, INNER), F32),
+            pltpu.SemaphoreType.DMA((4,)),
             pltpu.SemaphoreType.DMA((layers - 1,)),
         ],
         jnp.stack([layer_index, first_row.astype(jnp.int32)]),

time: 327 us -> 280 us (0.86)
  Pallas kernels: 80.2 us -> 33.3 us
    pallas_call x4, Pallas kernels: 80.2 us -> 33.3 us  [call(): pl.pallas_call(kernel, out_shape=[jax.ShapeDtypeStruct(shape, F32) for sh...]
  transfers between devices with their start and end apart: 11 -> 11, of which waited for: 7 -> 7; matrix products, arithmetic and copies ran while one was open for 0% -> 1% of each run, Pallas kernels for 1% -> 2%
where the time goes in v4:
time: 280 us; the launch traced here: 279 us
  waiting for transfers between devices  106 us (38%)
  blocking collectives  83.6 us (30%)
  starting transfers between devices  34.5 us (12%)
  Pallas kernels  33.3 us (12%)
  between operations  14.2 us (5%)
  local copies, waits for them, and re-layouts  7.08 us (3%)
    all_to_all x1, blocking collectives, on_device(): spectrum = lax.all_to_all(spectrum, SLAB, 0, 0, tiled=True)  56 us
    reduce_scatter x1, waiting for transfers between devices, on_device(): part = lax.psum_scatter(part, 'z', scatter_dimension=0, tiled=True)  40.3 us
    ppermute x7, waiting for transfers between devices, on_device(): lax.ppermute(piece, 'z', [(i, (i + k) % layers) for i in range(layers)])  34.8 us
    pallas_call x4, Pallas kernels, call(): pl.pallas_call(kernel, out_shape=[jax.ShapeDtypeStruct(shape, F32) for sh...  33.3 us
    all_to_all x1, blocking collectives, on_device(): lax.all_to_all(part, ('xl', 'y'), 0, 0, tiled=True)  27.6 us
    all_to_all x1, waiting for transfers between devices, on_device(): sorted_targets = lax.all_to_all(sorted_targets, SLAB, 0, 0, tiled=True)  26.7 us
    ppermute x7, starting transfers between devices, on_device(): lax.ppermute(piece, 'z', [(i, (i + k) % layers) for i in range(layers)])  19.2 us
    all_to_all x1, starting transfers between devices, on_device(): sorted_targets = lax.all_to_all(sorted_targets, SLAB, 0, 0, tiled=True)  7.64 us
  transfers between devices with their start and end apart: 11, of which 7 were waited for; matrix products, arithmetic and copies ran while one was open for 1% of the time, Pallas kernels for 2%

profile of v4, /device:TPU:4, one launch (start us, length us, event | category | flops | bytes accessed | tf_op | source)
XLA Modules:
  0.0 279.2 jit_solution(5727157403056007052)
XLA Ops:
  6.5 1.6 copy-done
  8.1 0.7 constant_dynamic-slice_fusion.1
  8.8 0.0 all-gather.2.cloned.1.call-update
  9.5 4.7 %shard_map.37 = f32[32,136,128]{2,1,0:T(8,128)} custom-call(s32[1]{0:T(128)S(6)} %copy.5.depth_ref, f32[128,4096]{1,0:T(8,128)} %bitcast.17), custom_call_target="tpu_custom_call" | custom-call | tf_op jit(solution)/shard_map/pallas_call | solution.py:376
  14.2 7.6 %all-to-all-start = ((f32[32,136,128]{2,1,0:T(8,128)}), f32[32,136,128]{2,1,0:T(8,128)}, u32[]{:S(2)}, u32[]{:S(2)}) async-start(f32[32,136,128]{2,1,0:T(8,128)} %shard_map.37), calls=%async_computation | async-start | bytes 4456448 | tf_op jit(solution)/shard_map/all_to_all | solution.py:417
  21.9 0.6 pad_add_fusion.place_ref
  22.5 26.7 %all-to-all-done.targets_hbm = f32[32,136,128]{2,1,0:T(8,128)} async-done(((f32[32,136,128]{2,1,0:T(8,128)}), f32[32,136,128]{2,1,0:T(8,128)}, u32[]{:S(2)}, u32[]{:S(2)}) %all-to-all-start) | async-done | bytes 2228256 | tf_op jit(solution)/shard_map/all_to_all | solution.py:417
  49.2 4.1 %all-gather.2.cloned.1.call-done.phase_ref = f32[128,4096]{1,0:T(8,128)} async-done(((f32[16,4096]{1,0:T(8,128)}), f32[128,4096]{1,0:T(8,128)}) %all-gather.2.cloned.1.call-update) | async-done | bytes 2097168 | tf_op jit(solution)/shard_map/all_gather | solution.py:407
  53.3 12.2 %shard_map.38 = (f32[32,2,128,128]{3,2,1,0:T(8,128)}, f32[2,128,4096]{2,1,0:T(8,128)}, f32[2,32,128]{2,1,0:T(8,128)}, f32[2,128,32]{2,1,0:T(8,128)}, f32[256,256...) custom-call(s32[2]{0:T(128)} %pad_add_fusion.place_ref, ...), custom_call_target="tpu_custom_call" | custom-call | tf_op jit(solution)/shard_map/pallas_call | solution.py:376
  65.6 7.6 %all-to-all-start.1 = ((f32[32,2,128,128]{3,2,1,0:T(8,128)}), f32[32,2,128,128]{3,2,1,0:T(8,128)}, u32[]{:S(2)}, u32[]{:S(2)}) async-start(f32[32,2,128,128]{3,2,1,0:T(8,128)} %get-tuple-element.23), calls=%async_computation.1 | async-start | bytes 8388608 | tf_op jit(solution)/shard_map/all_to_all | solution.py:463
  73.2 0.0 reduce-scatter.2.cloned.1.call-start
  73.3 1.2 collective-permute-start
  74.4 2.0 collective-permute-start.1
  76.5 3.7 %collective-permute-start.2 = (f32[4,128,128]{2,1,0:T(8,128)}, f32[4,128,128]{2,1,0:T(8,128)S(1)}, u32[]{:S(2)}, u32[]{:S(2)}) collective-permute-start(f32[4,128,128]{2,1,0:T(8,128)} %get-tuple-element.26), channel_id=1, source_target_pairs={{0,12},{4,16},{8,20},{12,24},{16,28},{20,0},{24,4},{28,8},{1,13},{... | collective-permute-start | bytes 786440 | tf_op jit(solution)/shard_map/ppermute | solution.py:460
  80.1 0.9 collective-permute-start.3
  81.0 4.6 %collective-permute-start.4 = (f32[4,128,128]{2,1,0:T(8,128)}, f32[4,128,128]{2,1,0:T(8,128)}, u32[]{:S(2)}, u32[]{:S(2)}) collective-permute-start(f32[4,128,128]{2,1,0:T(8,128)} %get-tuple-element.28), channel_id=1, source_target_pairs={{0,20},{4,24},{8,28},{12,0},{16,4},{20,8},{24,12},{28,16},{1,21},{... | collective-permute-start | bytes 786440 | tf_op jit(solution)/shard_map/ppermute | solution.py:460
  85.6 3.6 %collective-permute-start.5 = (f32[4,128,128]{2,1,0:T(8,128)}, f32[4,128,128]{2,1,0:T(8,128)}, u32[]{:S(2)}, u32[]{:S(2)}) collective-permute-start(f32[4,128,128]{2,1,0:T(8,128)} %get-tuple-element.29), channel_id=1, source_target_pairs={{0,24},{4,28},{8,0},{12,4},{16,8},{20,12},{24,16},{28,20},{1,25},{... | collective-permute-start | bytes 786440 | tf_op jit(solution)/shard_map/ppermute | solution.py:460
  89.2 8.9 %collective-permute-done.1 = f32[4,128,128]{2,1,0:T(8,128)S(1)} collective-permute-done((f32[4,128,128]{2,1,0:T(8,128)S(1)}, f32[4,128,128]{2,1,0:T(8,128)S(1)}, u32[]{:S(2)}, u32[]{:S(2)}) %collective-permute-start.1) | collective-permute-done | bytes 262176 | tf_op jit(solution)/shard_map/ppermute | solution.py:460
  98.1 3.2 %collective-permute-start.6 = (f32[4,128,128]{2,1,0:T(8,128)}, f32[4,128,128]{2,1,0:T(8,128)}, u32[]{:S(2)}, u32[]{:S(2)}) collective-permute-start(f32[4,128,128]{2,1,0:T(8,128)} %get-tuple-element.30), channel_id=1, source_target_pairs={{0,28},{4,0},{8,4},{12,8},{16,12},{20,16},{24,20},{28,24},{1,29},{... | collective-permute-start | bytes 786440 | tf_op jit(solution)/shard_map/ppermute | solution.py:460
  101.3 1.0 constant_dynamic-slice_fusion
  102.3 15.6 %collective-permute-done.2 = f32[4,128,128]{2,1,0:T(8,128)S(1)} collective-permute-done((f32[4,128,128]{2,1,0:T(8,128)}, f32[4,128,128]{2,1,0:T(8,128)S(1)}, u32[]{:S(2)}, u32[]{:S(2)}) %collective-permute-start.2) | collective-permute-done | bytes 262176 | tf_op jit(solution)/shard_map/ppermute | solution.py:460
  117.9 6.7 %collective-permute-done.5 = f32[4,128,128]{2,1,0:T(8,128)} collective-permute-done((f32[4,128,128]{2,1,0:T(8,128)}, f32[4,128,128]{2,1,0:T(8,128)}, u32[]{:S(2)}, u32[]{:S(2)}) %collective-permute-start.5) | collective-permute-done | bytes 262176 | tf_op jit(solution)/shard_map/ppermute | solution.py:460
  124.6 3.6 %collective-permute-done.6 = f32[4,128,128]{2,1,0:T(8,128)} collective-permute-done((f32[4,128,128]{2,1,0:T(8,128)}, f32[4,128,128]{2,1,0:T(8,128)}, u32[]{:S(2)}, u32[]{:S(2)}) %collective-permute-start.6) | collective-permute-done | bytes 262176 | tf_op jit(solution)/shard_map/ppermute | solution.py:460
  128.2 11.5 %shard_map.39 = f32[32,2,128,128]{3,2,1,0:T(8,128)S(1)} custom-call(s32[1]{0:T(128)} %bitcast.refs_0_, f32[2,128,32]{2,1,0:T(8,128)S(1)} %copy-done.4, f32[256,256]{1,0:T(8,128)S(1)} %copy-done.3, f32[32,2,128,128]{3,2,1,0:T(8,128)} %all-to-all-done.1.refs_3_, f32[512,128]{1,0:T(8,128)S(1)} %bitcast.12, f32[512,128]{1,0:T(8,128)S(1)} %bitcast.13, ...), custom_call_target="tpu_custom_call" | custom-call | tf_op jit(solution)/shard_map/pallas_call | solution.py:376
  139.7 56.0 %all_to_all.20.in_ref = f32[32,2,128,128]{3,2,1,0:T(8,128)S(1)} all-to-all(f32[32,2,128,128]{3,2,1,0:T(8,128)S(1)} %shard_map.39), channel_id=1, replica_groups=mesh['xl'=2,'y'=4,'z'=8,'xh'=2,'c'=2] {'xl','y','xh','c'}, dimensions={0} | all-to-all | bytes 8388608 | tf_op jit(solution)/shard_map/all_to_all | solution.py:486
  195.7 4.9 %shard_map.40 = f32[128,4096]{1,0:T(8,128)S(1)} custom-call(f32[32,2,128,128]{3,2,1,0:T(8,128)S(1)} %all_to_all.20.in_ref, f32[2,128,4096]{2,1,0:T(8,128)S(1)} %copy-done.2, f32[2,32,128]{2,1,0:T(8,128)S(1)} %copy-done.5, f32[256,256]{1,0:T(8,128)S(1)} %copy-done.3), custom_call_target="tpu_custom_call" | custom-call | tf_op jit(solution)/shard_map/pallas_call | solution.py:376
  200.7 1.3 copy-done.1
  202.0 0.0 reduce-scatter.2.cloned.1.call-update
  202.0 40.3 %reduce-scatter.2.cloned.1.call-done = f32[16,4096]{1,0:T(8,128)} async-done(((f32[128,4096]{1,0:T(8,128)}), f32[16,4096]{1,0:T(8,128)}) %reduce-scatter.2.cloned.1.call-update) | async-done | bytes 262160 | tf_op jit(solution)/shard_map/reduce_scatter | solution.py:496
  242.3 1.1 broadcast_in_dim.10
  243.4 27.6 %all_to_all.21 = f32[8,16,4096]{2,1,0:T(8,128)S(1)} all-to-all(f32[8,16,4096]{2,1,0:T(8,128)S(1)} %broadcast_in_dim.10), channel_id=1, replica_groups=mesh['xl'=2,'y'=4,'z'=8,'xh'=2,'c'=2] {'xl','y'}, dimensions={0} | all-to-all | bytes 4194304 | tf_op jit(solution)/shard_map/all_to_all | solution.py:498
  271.0 1.3 copy.6
  (17 shorter events, 0.0 us)
Async XLA Ops:
  6.5 1.6 copy-start
  6.5 46.8 %all-gather.2.cloned.1.call-start = ((), (), s32[]{:S(2)}) async-start(), calls=%async_computation.5 | async-start | bytes 2359296 | tf_op jit(solution)/shard_map/all_gather | solution.py:407
  14.2 34.9 %all-to-all-start = ((f32[32,136,128]{2,1,0:T(8,128)}), f32[32,136,128]{2,1,0:T(8,128)}, u32[]{:S(2)}, u32[]{:S(2)}) async-start(f32[32,136,128]{2,1,0:T(8,128)} %shard_map.37), calls=%async_computation | async-start | bytes 4456448 | tf_op jit(solution)/shard_map/all_to_all | solution.py:417
  65.5 8.9 %copy-start.6 = (f32[4,128,128]{2,1,0:T(8,128)S(1)}, f32[4,128,128]{2,1,0:T(8,128)}, u32[]{:S(2)}) copy-start(f32[4,128,128]{2,1,0:T(8,128)} %get-tuple-element.25) | copy-start | bytes 786436
  65.6 62.7 %copy-start.3 = (f32[256,256]{1,0:T(8,128)S(1)}, f32[256,256]{1,0:T(8,128)}, u32[]{:S(2)}) copy-start(f32[256,256]{1,0:T(8,128)} %get-tuple-element.22.refs_2_.dft_ref) | copy-start | bytes 786436
  65.6 62.6 %copy-start.4 = (f32[2,128,32]{2,1,0:T(8,128)S(1)}, f32[2,128,32]{2,1,0:T(8,128)}, u32[]{:S(2)}) copy-start(f32[2,128,32]{2,1,0:T(8,128)} %get-tuple-element.21.refs_1_) | copy-start | bytes 98308
  65.6 62.6 %all-to-all-start.1 = ((f32[32,2,128,128]{3,2,1,0:T(8,128)}), f32[32,2,128,128]{3,2,1,0:T(8,128)}, u32[]{:S(2)}, u32[]{:S(2)}) async-start(f32[32,2,128,128]{3,2,1,0:T(8,128)} %get-tuple-element.23), calls=%async_computation.1 | async-start | bytes 8388608 | tf_op jit(solution)/shard_map/all_to_all | solution.py:463
  73.2 169.1 %reduce-scatter.2.cloned.1.call-start = ((), (), s32[]{:S(2)}) async-start(), calls=%async_computation.6 | async-start | bytes 2359296 | tf_op jit(solution)/shard_map/reduce_scatter | solution.py:496
  73.3 12.4 %collective-permute-start = (f32[4,128,128]{2,1,0:T(8,128)}, f32[4,128,128]{2,1,0:T(8,128)S(1)}, u32[]{:S(2)}, u32[]{:S(2)}) collective-permute-start(f32[4,128,128]{2,1,0:T(8,128)} %get-tuple-element.24), channel_id=1, source_target_pairs={{0,4},{4,8},{8,12},{12,16},{16,20},{20,24},{24,28},{28,0},{1,5},{5... | collective-permute-start | bytes 786440 | tf_op jit(solution)/shard_map/ppermute | solution.py:460
  74.4 23.7 %collective-permute-start.1 = (f32[4,128,128]{2,1,0:T(8,128)S(1)}, f32[4,128,128]{2,1,0:T(8,128)S(1)}, u32[]{:S(2)}, u32[]{:S(2)}) collective-permute-start(f32[4,128,128]{2,1,0:T(8,128)S(1)} %copy-done.6), channel_id=1, source_target_pairs={{0,8},{4,12},{8,16},{12,20},{16,24},{20,28},{24,0},{28,4},{1,9},{5... | collective-permute-start | bytes 786440 | tf_op jit(solution)/shard_map/ppermute | solution.py:460
  76.5 41.4 %collective-permute-start.2 = (f32[4,128,128]{2,1,0:T(8,128)}, f32[4,128,128]{2,1,0:T(8,128)S(1)}, u32[]{:S(2)}, u32[]{:S(2)}) collective-permute-start(f32[4,128,128]{2,1,0:T(8,128)} %get-tuple-element.26), channel_id=1, source_target_pairs={{0,12},{4,16},{8,20},{12,24},{16,28},{20,0},{24,4},{28,8},{1,13},{... | collective-permute-start | bytes 786440 | tf_op jit(solution)/shard_map/ppermute | solution.py:460
  80.1 37.7 %collective-permute-start.3 = (f32[4,128,128]{2,1,0:T(8,128)}, f32[4,128,128]{2,1,0:T(8,128)}, u32[]{:S(2)}, u32[]{:S(2)}) collective-permute-start(f32[4,128,128]{2,1,0:T(8,128)} %get-tuple-element.27), channel_id=1, source_target_pairs={{0,16},{4,20},{8,24},{12,28},{16,0},{20,4},{24,8},{28,12},{1,17},{... | collective-permute-start | bytes 786440 | tf_op jit(solution)/shard_map/ppermute | solution.py:460
  81.0 36.9 %collective-permute-start.4 = (f32[4,128,128]{2,1,0:T(8,128)}, f32[4,128,128]{2,1,0:T(8,128)}, u32[]{:S(2)}, u32[]{:S(2)}) collective-permute-start(f32[4,128,128]{2,1,0:T(8,128)} %get-tuple-element.28), channel_id=1, source_target_pairs={{0,20},{4,24},{8,28},{12,0},{16,4},{20,8},{24,12},{28,16},{1,21},{... | collective-permute-start | bytes 786440 | tf_op jit(solution)/shard_map/ppermute | solution.py:460
  85.6 39.0 %collective-permute-start.5 = (f32[4,128,128]{2,1,0:T(8,128)}, f32[4,128,128]{2,1,0:T(8,128)}, u32[]{:S(2)}, u32[]{:S(2)}) collective-permute-start(f32[4,128,128]{2,1,0:T(8,128)} %get-tuple-element.29), channel_id=1, source_target_pairs={{0,24},{4,28},{8,0},{12,4},{16,8},{20,12},{24,16},{28,20},{1,25},{... | collective-permute-start | bytes 786440 | tf_op jit(solution)/shard_map/ppermute | solution.py:460
  98.1 30.1 %collective-permute-start.6 = (f32[4,128,128]{2,1,0:T(8,128)}, f32[4,128,128]{2,1,0:T(8,128)}, u32[]{:S(2)}, u32[]{:S(2)}) collective-permute-start(f32[4,128,128]{2,1,0:T(8,128)} %get-tuple-element.30), channel_id=1, source_target_pairs={{0,28},{4,0},{8,4},{12,8},{16,12},{20,16},{24,20},{28,24},{1,29},{... | collective-permute-start | bytes 786440 | tf_op jit(solution)/shard_map/ppermute | solution.py:460
  139.7 56.0 %copy-start.2 = (f32[2,128,4096]{2,1,0:T(8,128)S(1)}, f32[2,128,4096]{2,1,0:T(8,128)}, u32[]{:S(2)}) copy-start(f32[2,128,4096]{2,1,0:T(8,128)} %get-tuple-element.31.wave_ref) | copy-start | bytes 12582916
  139.7 56.0 %copy-start.5 = (f32[2,32,128]{2,1,0:T(8,128)S(1)}, f32[2,32,128]{2,1,0:T(8,128)}, u32[]{:S(2)}) copy-start(f32[2,32,128]{2,1,0:T(8,128)} %get-tuple-element.32.tw_ref) | copy-start | bytes 98308
  200.6 1.3 copy-start.1
Sparse Core Ops, SparseCore 0:
  9.1 44.1 all-gather.1
  202.1 40.1 reduce-scatter.1

commit v5 on v4

--- a/solution.py
+++ b/solution.py
@@ -112,6 +112,10 @@
     return pl.ds(pl.multiple_of(step * BLOCK, BLOCK), BLOCK)
 
 
+def half_rows(step):
+    return pl.ds(pl.multiple_of(step * (BLOCK // 2), BLOCK // 2), BLOCK // 2)
+
+
 def tile(index):
     return slice(index * INNER, (index + 1) * INNER)
 
@@ -125,7 +129,7 @@
 
 
 def rows_kernel(
-    length, place_ref, phase_ref, targets_hbm, out_hbm, wave_hbm, tw_ref, tall_ref, dft_ref, *refs
+    length, place_ref, phase_ref, targets_hbm, out_hbm, first_hbm, second_hbm, tw_ref, tall_ref, dft_ref, *refs
 ):
     sent = refs[:-13]
     high_ref, low_ref, mid_ref, sh_ref, sl_ref, out_ref, wave_ref, row_ref, col_ref, note_ref, stage_ref, sem, send_sem = refs[-13:]
@@ -184,8 +188,11 @@
         send.start()
 
     def save_wave(step):
-        rows = row_block(step)
-        return pltpu.make_async_copy(wave_ref.at[:, rows, :], wave_hbm.at[:, rows, :], sem.at[0])
+        source = [half_rows(2 * step + side) for side in (0, 1)]
+        return [
+            pltpu.make_async_copy(wave_ref.at[:, source[side], :], hbm.at[:, half_rows(step), :], sem.at[0])
+            for side, hbm in enumerate((first_hbm, second_hbm))
+        ]
 
     def save_out(step):
         group = pl.ds(step * 4, 4)
@@ -211,7 +218,8 @@
                 sl_ref[k, rows, tile(side)] = low
 
         dft32(load, store, mid_ref, -1)
-        save_wave(step).start()
+        for save in save_wave(step):
+            save.start()
         return carry
 
     lax.fori_loop(0, INNER // BLOCK, block, 0)
@@ -231,7 +239,8 @@
         return carry
 
     lax.fori_loop(0, OUTER // 4, multiply, 0)
-    pltpu.make_async_copy(wave_ref, wave_hbm, sem.at[0]).wait()
+    for hbm in (first_hbm, second_hbm):
+        pltpu.make_async_copy(wave_ref.at[:, pl.ds(0, INNER // 2), :], hbm, sem.at[0]).wait()
     pltpu.make_async_copy(out_ref, out_hbm, sem.at[1]).wait()
     for send in sends:
         send.wait()
@@ -240,8 +249,8 @@
 def columns_kernel(
     scale, layer_ref, tw_ref, there_ref, in_hbm, *refs
 ):
-    pieces_hbm, refs = refs[: len(refs) - 11], refs[len(refs) - 11 :]
-    out_ref, there_both, home_both, mid_ref, sh_ref, sl_ref, back_ref, target_ref, in_ref, pieces_ref, sem = refs
+    pieces_hbm, refs = refs[: len(refs) - 12], refs[len(refs) - 12 :]
+    first_ref, second_ref, there_both, home_both, mid_ref, sh_ref, sl_ref, back_ref, target_ref, in_ref, pieces_ref, sem = refs
     layers = len(pieces_hbm)
     run = INNER // layers
 
@@ -317,7 +326,8 @@
 
         def store(k, value):
             for side in (0, 1):
-                out_ref[step * 4 + k % 4, side, tile_rows(k // 4), :] = value[side]
+                first_ref[step * 4 + k % 4, side, half_tile(k // 4), :] = value[side][: BLOCK // 2]
+                second_ref[step * 4 + k % 4, side, half_tile(k // 4), :] = value[side][BLOCK // 2 :]
 
         dft32(load, store, mid_ref, 1)
         return carry
@@ -335,6 +345,10 @@
     )
 
 
+def half_tile(index):
+    return slice(index * (BLOCK // 2), (index + 1) * (BLOCK // 2))
+
+
 def tile_rows(index):
     return slice(index * BLOCK, (index + 1) * BLOCK)
 
@@ -342,15 +356,17 @@
 def gradient_kernel(in_ref, wave_ref, tw_ref, dft_ref, out_ref, high_ref, low_ref, mid_ref, back_ref):
     high_ref[...], low_ref[...] = split(transposed(dft_ref))
 
+    rows_here = in_ref.shape[2]
+
     def multiply(step, carry):
         group = pl.ds(step * 4, 4)
-        both = jnp.concatenate([in_ref[group, 0], in_ref[group, 1]], axis=-1).reshape(4 * INNER, 2 * INNER)
+        both = jnp.concatenate([in_ref[group, 0], in_ref[group, 1]], axis=-1).reshape(4 * rows_here, 2 * INNER)
         high, low = split(both)
         out = dot(
             jnp.concatenate([high, low, high], axis=1),
             jnp.concatenate([high_ref[...], high_ref[...], low_ref[...]], axis=0),
         )
-        back_ref[group] = out.reshape(4, INNER, 2 * INNER)
+        back_ref[group] = out.reshape(4, rows_here, 2 * INNER)
         return carry
 
     lax.fori_loop(0, OUTER // 4, multiply, 0)
@@ -369,7 +385,7 @@
         dft32(load, store, mid_ref, 1)
         return carry
 
-    lax.fori_loop(0, INNER // BLOCK, block, 0)
+    lax.fori_loop(0, rows_here // BLOCK, block, 0)
 
 
 def call(kernel, out_shapes, scratch, *args, direct=(), limit=28, held=0):
@@ -423,11 +439,12 @@
     mid = ((OUTER, 2, BLOCK, INNER), F32)
     matrix = ((2 * INNER, 2 * INNER), BF16)
     chunks = (slab_size, 2, layers * share, INNER)
-    spectrum, wave, twiddle, tall_twiddle, there, *sent = call(
+    spectrum, first_wave, second_wave, twiddle, tall_twiddle, there, *sent = call(
         functools.partial(rows_kernel, length),
         [
             chunks,
-            (2, layers * share, length),
+            (2, layers * share // 2, length),
+            (2, layers * share // 2, length),
             (2, OUTER, INNER),
             (2, INNER, OUTER),
             (2 * INNER, 2 * INNER),
@@ -452,7 +469,7 @@
         rows_phase,
         sorted_targets,
         held=1,
-        direct=(0, 1) + tuple(range(5, 4 + layers)),
+        direct=(0, 1, 2) + tuple(range(6, 5 + layers)),
         limit=60,
     )
     own = lax.dynamic_slice(sorted_targets, (layer * group, 0, 0), (group, rows_dev, INNER))
@@ -461,9 +478,9 @@
     ]
     pieces = [piece.reshape(group * rows_dev, INNER) for piece in pieces]
     spectrum = lax.all_to_all(spectrum, SLAB, 0, 0, tiled=True)
-    (spectrum,) = call(
+    halves = call(
         lambda *refs: columns_kernel(4.0 / planes, *refs),
-        [chunks],
+        [(slab_size, 2, layers * share // 2, INNER)] * 2,
         [
             ((2 * INNER, 6 * INNER), BF16),
             ((2 * INNER, 6 * INNER), BF16),
@@ -483,19 +500,35 @@
         *pieces,
         held=1 + layers,
     )
-    spectrum = lax.all_to_all(spectrum, SLAB, 0, 0, tiled=True)
-    (part,) = call(
-        gradient_kernel,
-        [(layers * share, length)],
-        [matrix, matrix, mid, ((OUTER, INNER, 2 * INNER), F32)],
-        spectrum,
-        wave,
-        twiddle,
-        there,
-    )
-    part = lax.psum_scatter(part, "z", scatter_dimension=0, tiled=True)
-    part = jnp.broadcast_to(part[None], (planes, share, length))
-    return lax.all_to_all(part, ("xl", "y"), 0, 0, tiled=True).reshape(rows_dev, length)
+    results = []
+    for half, wave in zip(halves, (first_wave, second_wave)):
+        if results:
+            half, results[0] = lax.optimization_barrier((half, results[0]))
+        half = lax.all_to_all(half, SLAB, 0, 0, tiled=True)
+        (part,) = call(
+            gradient_kernel,
+            [(layers * share // 2, length)],
+            [matrix, matrix, mid, ((OUTER, layers * share // 2, 2 * INNER), F32)],
+            half,
+            wave,
+            twiddle,
+            there,
+        )
+        results.append(part)
+    results[0] = lax.psum_scatter(results[0], "z", scatter_dimension=0, tiled=True)
+    height = share // 2
+    total = lax.dynamic_slice_in_dim(results[1], layer * height, height, 0)
+    for k in range(1, layers):
+        part = lax.dynamic_slice_in_dim(results[1], (layer + k) % layers * height, height, 0)
+        total = total + lax.ppermute(part, "z", [(i, (i + k) % layers) for i in range(layers)])
+    results[1] = total
+    results = [everywhere(part, planes) for part in results]
+    return jnp.stack(results, axis=1).reshape(rows_dev, length)
+
+
+def everywhere(value, copies):
+    value = jnp.broadcast_to(value[None], (copies,) + value.shape)
+    return lax.all_to_all(value, ("xl", "y"), 0, 0, tiled=True)
 
 
 def solution(mesh):

time: 280 us -> 284 us (1.014)
  blocking collectives: 83.6 us -> 52.6 us
  starting transfers between devices: 34.5 us -> 62.6 us
  other arithmetic: 0.59 us -> 4.64 us
  Pallas kernels: 33.3 us -> 37.2 us
  waiting for transfers between devices: 106 us -> 103 us
    reduce_scatter x1, waiting for transfers between devices: 40.3 us -> 0.01 us  [on_device(): lax.psum_scatter(results[0], 'z', scatter_dimension=0, tiled=True)]
    all_to_all x2, blocking collectives: 83.6 us -> 52.6 us  [the longest x1 33.5 us: on_device(): half = lax.all_to_all(half, SLAB, 0, 0, tiled=True)]
    all_to_all x0 -> x2, waiting for transfers between devices: none -> 30.3 us  [the longest x1 25 us: on_device(): half = lax.all_to_all(half, SLAB, 0, 0, tiled=True)]
    ppermute x0 -> x7, starting transfers between devices: none -> 15 us  [on_device(): lax.ppermute(part, 'z', [(i, (i + k) % layers) for i in range(layers)])]
    all_to_all x0 -> x2, starting transfers between devices: none -> 13 us  [the longest x1 6.58 us: on_device(): half = lax.all_to_all(half, SLAB, 0, 0, tiled=True)]
    ppermute x0 -> x7, waiting for transfers between devices: none -> 6.56 us  [on_device(): lax.ppermute(part, 'z', [(i, (i + k) % layers) for i in range(layers)])]
    pallas_call x4 -> x5, Pallas kernels: 33.3 us -> 37.2 us  [call(): pl.pallas_call(kernel, out_shape=[jax.ShapeDtypeStruct(shape, F32) for sh...]
  transfers between devices with their start and end apart: 11 -> 20, of which waited for: 7 -> 9; matrix products, arithmetic and copies ran while one was open for 1% -> 2% of each run, Pallas kernels for 2% -> 3%
where the time goes in v5:
time: 284 us; the launch traced here: 283 us
  waiting for transfers between devices  103 us (36%)
  starting transfers between devices  62.6 us (22%)
  blocking collectives  52.6 us (19%)
  Pallas kernels  37.2 us (13%)
  between operations  14.3 us (5%)
  local copies, waits for them, and re-layouts  8.43 us (3%)
  other arithmetic  4.64 us (2%)
    pallas_call x5, Pallas kernels, call(): pl.pallas_call(kernel, out_shape=[jax.ShapeDtypeStruct(shape, F32) for sh...  37.2 us
    ppermute x7, waiting for transfers between devices, on_device(): lax.ppermute(piece, 'z', [(i, (i + k) % layers) for i in range(layers)])  34.8 us
    all_to_all x1, blocking collectives, on_device(): half = lax.all_to_all(half, SLAB, 0, 0, tiled=True)  33.5 us
    all_to_all x1, waiting for transfers between devices, on_device(): sorted_targets = lax.all_to_all(sorted_targets, SLAB, 0, 0, tiled=True)  26.7 us
    all_to_all x1, waiting for transfers between devices, on_device(): half = lax.all_to_all(half, SLAB, 0, 0, tiled=True)  25 us
    ppermute x7, starting transfers between devices, on_device(): lax.ppermute(piece, 'z', [(i, (i + k) % layers) for i in range(layers)])  19.2 us
    all_to_all x1, blocking collectives, everywhere(): return lax.all_to_all(value, ('xl', 'y'), 0, 0, tiled=True)  19.1 us
    ppermute x7, starting transfers between devices, on_device(): lax.ppermute(part, 'z', [(i, (i + k) % layers) for i in range(layers)])  15 us
  transfers between devices with their start and end apart: 20, of which 9 were waited for; matrix products, arithmetic and copies ran while one was open for 2% of the time, Pallas kernels for 3%

profile of v5, /device:TPU:4, one launch (start us, length us, event | category | flops | bytes accessed | tf_op | source)
XLA Modules:
  0.0 282.9 jit_solution(15345125261713300411)
XLA Ops:
  9.5 4.7 %shard_map.37 = f32[32,136,128]{2,1,0:T(8,128)} custom-call(s32[1]{0:T(128)S(6)} %copy.4.depth_ref, f32[128,4096]{1,0:T(8,128)} %bitcast.19), custom_call_target="tpu_custom_call" | custom-call | tf_op jit(solution)/shard_map/pallas_call | solution.py:392
  14.2 7.6 %all-to-all-start = ((f32[32,136,128]{2,1,0:T(8,128)}), f32[32,136,128]{2,1,0:T(8,128)}, u32[]{:S(2)}, u32[]{:S(2)}) async-start(f32[32,136,128]{2,1,0:T(8,128)} %shard_map.37), calls=%async_computation | async-start | bytes 4456448 | tf_op jit(solution)/shard_map/all_to_all | solution.py:433
  22.5 26.7 %all-to-all-done.targets_hbm = f32[32,136,128]{2,1,0:T(8,128)} async-done(((f32[32,136,128]{2,1,0:T(8,128)}), f32[32,136,128]{2,1,0:T(8,128)}, u32[]{:S(2)}, u32[]{:S(2)}) %all-to-all-start) | async-done | bytes 2228256 | tf_op jit(solution)/shard_map/all_to_all | solution.py:433
  49.2 4.2 %all-gather.2.cloned.1.call-done.phase_ref = f32[128,4096]{1,0:T(8,128)} async-done(((f32[16,4096]{1,0:T(8,128)}), f32[128,4096]{1,0:T(8,128)}) %all-gather.2.cloned.1.call-update) | async-done | bytes 2097168 | tf_op jit(solution)/shard_map/all_gather | solution.py:423
  53.3 12.2 %shard_map.38 = (f32[32,2,128,128]{3,2,1,0:T(8,128)}, f32[2,64,4096]{2,1,0:T(8,128)}, f32[2,64,4096]{2,1,0:T(8,128)}, f32[2,32,128]{2,1,0:T(8,128)}, f32[2,128,3...) custom-call(s32[2]{0:T(128)} %pad_add_fusion.place_ref, ...), custom_call_target="tpu_custom_call" | custom-call | tf_op jit(solution)/shard_map/pallas_call | solution.py:392
  65.6 7.6 %all-to-all-start.1 = ((f32[32,2,128,128]{3,2,1,0:T(8,128)}), f32[32,2,128,128]{3,2,1,0:T(8,128)}, u32[]{:S(2)}, u32[]{:S(2)}) async-start(f32[32,2,128,128]{3,2,1,0:T(8,128)} %get-tuple-element.28), calls=%async_computation.1 | async-start | bytes 8388608 | tf_op jit(solution)/shard_map/all_to_all | solution.py:480
  74.4 2.0 collective-permute-start.1
  76.4 3.6 %collective-permute-start.2 = (f32[4,128,128]{2,1,0:T(8,128)}, f32[4,128,128]{2,1,0:T(8,128)S(1)}, u32[]{:S(2)}, u32[]{:S(2)}) collective-permute-start(f32[4,128,128]{2,1,0:T(8,128)} %get-tuple-element.31), channel_id=1, source_target_pairs={{0,12},{4,16},{8,20},{12,24},{16,28},{20,0},{24,4},{28,8},{1,13},{... | collective-permute-start | bytes 786440 | tf_op jit(solution)/shard_map/ppermute | solution.py:477
  81.0 4.6 %collective-permute-start.4 = (f32[4,128,128]{2,1,0:T(8,128)}, f32[4,128,128]{2,1,0:T(8,128)}, u32[]{:S(2)}, u32[]{:S(2)}) collective-permute-start(f32[4,128,128]{2,1,0:T(8,128)} %get-tuple-element.33), channel_id=1, source_target_pairs={{0,20},{4,24},{8,28},{12,0},{16,4},{20,8},{24,12},{28,16},{1,21},{... | collective-permute-start | bytes 786440 | tf_op jit(solution)/shard_map/ppermute | solution.py:477
  85.6 3.6 %collective-permute-start.5 = (f32[4,128,128]{2,1,0:T(8,128)}, f32[4,128,128]{2,1,0:T(8,128)}, u32[]{:S(2)}, u32[]{:S(2)}) collective-permute-start(f32[4,128,128]{2,1,0:T(8,128)} %get-tuple-element.34), channel_id=1, source_target_pairs={{0,24},{4,28},{8,0},{12,4},{16,8},{20,12},{24,16},{28,20},{1,25},{... | collective-permute-start | bytes 786440 | tf_op jit(solution)/shard_map/ppermute | solution.py:477
  89.2 8.9 %collective-permute-done.1 = f32[4,128,128]{2,1,0:T(8,128)S(1)} collective-permute-done((f32[4,128,128]{2,1,0:T(8,128)S(1)}, f32[4,128,128]{2,1,0:T(8,128)S(1)}, u32[]{:S(2)}, u32[]{:S(2)}) %collective-permute-start.1) | collective-permute-done | bytes 262176 | tf_op jit(solution)/shard_map/ppermute | solution.py:477
  98.1 3.2 %collective-permute-start.6 = (f32[4,128,128]{2,1,0:T(8,128)}, f32[4,128,128]{2,1,0:T(8,128)}, u32[]{:S(2)}, u32[]{:S(2)}) collective-permute-start(f32[4,128,128]{2,1,0:T(8,128)} %get-tuple-element.35), channel_id=1, source_target_pairs={{0,28},{4,0},{8,4},{12,8},{16,12},{20,16},{24,20},{28,24},{1,29},{... | collective-permute-start | bytes 786440 | tf_op jit(solution)/shard_map/ppermute | solution.py:477
  102.3 15.6 %collective-permute-done.2 = f32[4,128,128]{2,1,0:T(8,128)S(1)} collective-permute-done((f32[4,128,128]{2,1,0:T(8,128)}, f32[4,128,128]{2,1,0:T(8,128)S(1)}, u32[]{:S(2)}, u32[]{:S(2)}) %collective-permute-start.2) | collective-permute-done | bytes 262176 | tf_op jit(solution)/shard_map/ppermute | solution.py:477
  117.8 6.7 %collective-permute-done.5 = f32[4,128,128]{2,1,0:T(8,128)} collective-permute-done((f32[4,128,128]{2,1,0:T(8,128)}, f32[4,128,128]{2,1,0:T(8,128)}, u32[]{:S(2)}, u32[]{:S(2)}) %collective-permute-start.5) | collective-permute-done | bytes 262176 | tf_op jit(solution)/shard_map/ppermute | solution.py:477
  124.6 3.6 %collective-permute-done.6 = f32[4,128,128]{2,1,0:T(8,128)} collective-permute-done((f32[4,128,128]{2,1,0:T(8,128)}, f32[4,128,128]{2,1,0:T(8,128)}, u32[]{:S(2)}, u32[]{:S(2)}) %collective-permute-start.6) | collective-permute-done | bytes 262176 | tf_op jit(solution)/shard_map/ppermute | solution.py:477
  128.2 11.4 %shard_map.39 = (f32[32,2,64,128]{3,2,1,0:T(8,128)S(1)}, f32[32,2,64,128]{3,2,1,0:T(8,128)S(1)}) custom-call(s32[1]{0:T(128)} %bitcast.refs_0_, f32[2,128,32]{2,1,0:T(8,128)S(1)} %copy-done.6, f32[256,256]{1,0:T(8,128)S(1)} %copy-done.1, f32[32,2,128,128]{3,2,1,0:T(8,128)} %all-to-all-done.1.refs_3_, f32[512,128]{1,0:T(8,128)S(1)} %bitcast.14, ...), custom_call_target="tpu_custom_call" | custom-call | tf_op jit(solution)/shard_map/pallas_call | solution.py:392
  139.6 33.5 %all_to_all.30.in_ref = f32[32,2,64,128]{3,2,1,0:T(8,128)S(1)} all-to-all(f32[32,2,64,128]{3,2,1,0:T(8,128)S(1)} %get-tuple-element.37), channel_id=1, replica_groups=mesh['xl'=2,'y'=4,'z'=8,'xh'=2,'c'=2] {'xl','y','xh','c'}, dimensions={0} | all-to-all | bytes 4194304 | tf_op jit(solution)/shard_map/all_to_all | solution.py:507
  173.2 4.1 %shard_map.40 = f32[64,4096]{1,0:T(8,128)} custom-call(f32[32,2,64,128]{3,2,1,0:T(8,128)S(1)} %all_to_all.30.in_ref, f32[2,64,4096]{2,1,0:T(8,128)S(1)} %copy-done.4, f32[2,32,128]{2,1,0:T(8,128)S(1)} %copy-done.5, f32[256,256]{1,0:T(8,128)S(1)} %copy-done.1), custom_call_target="tpu_custom_call" | custom-call | tf_op jit(solution)/shard_map/pallas_call | solution.py:392
  177.3 6.6 %all-to-all-start.4 = ((f32[32,2,64,128]{3,2,1,0:T(8,128)}), f32[32,2,64,128]{3,2,1,0:T(8,128)}, u32[]{:S(2)}, u32[]{:S(2)}) async-start(f32[32,2,64,128]{3,2,1,0:T(8,128)} %copy-done.3), calls=%async_computation.5 | async-start | bytes 4194304 | tf_op jit(solution)/shard_map/all_to_all | solution.py:507
  184.7 25.0 %all-to-all-done.4.in_ref = f32[32,2,64,128]{3,2,1,0:T(8,128)} async-done(((f32[32,2,64,128]{3,2,1,0:T(8,128)}), f32[32,2,64,128]{3,2,1,0:T(8,128)}, u32[]{:S(2)}, u32[]{:S(2)}) %all-to-all-start.4) | async-done | bytes 2097184 | tf_op jit(solution)/shard_map/all_to_all | solution.py:507
  211.4 4.7 %shard_map.41 = f32[64,4096]{1,0:T(8,128)S(1)} custom-call(f32[32,2,64,128]{3,2,1,0:T(8,128)} %all-to-all-done.4.in_ref, f32[2,64,4096]{2,1,0:T(8,128)S(1)} %copy-done.2, f32[2,32,128]{2,1,0:T(8,128)S(1)} %copy-done.5, f32[256,256]{1,0:T(8,128)S(1)} %copy-done.1), custom_call_target="tpu_custom_call" | custom-call | tf_op jit(solution)/shard_map/pallas_call | solution.py:392
  216.9 3.1 %collective-permute-start.7 = (f32[8,4096]{1,0:T(8,128)S(1)}, f32[8,4096]{1,0:T(8,128)S(1)}, u32[]{:S(2)}, u32[]{:S(2)}) collective-permute-start(f32[8,4096]{1,0:T(8,128)S(1)} %get-tuple-element.43), channel_id=1, source_target_pairs={{0,4},{4,8},{8,12},{12,16},{16,20},{20,24},{24,28},{28,0},{1,5},{5... | collective-permute-start | bytes 393224 | tf_op jit(solution)/shard_map/ppermute | solution.py:523
  221.0 4.4 %collective-permute-start.11 = (f32[8,4096]{1,0:T(8,128)}, f32[8,4096]{1,0:T(8,128)}, u32[]{:S(2)}, u32[]{:S(2)}) collective-permute-start(f32[8,4096]{1,0:T(8,128)} %get-tuple-element.46), channel_id=1, source_target_pairs={{0,20},{4,24},{8,28},{12,0},{16,4},{20,8},{24,12},{28,16},{1,21},{... | collective-permute-start | bytes 393224 | tf_op jit(solution)/shard_map/ppermute | solution.py:523
  225.4 2.1 collective-permute-start.10
  227.5 2.0 collective-permute-start.9
  230.2 2.4 collective-permute-start.8
  232.6 1.9 broadcast_in_dim.7
  234.6 6.5 %all-to-all-start.3 = ((f32[8,8,4096]{2,1,0:T(8,128)}), f32[8,8,4096]{2,1,0:T(8,128)}, u32[]{:S(2)}, u32[]{:S(2)}) async-start(f32[8,8,4096]{2,1,0:T(8,128)} %broadcast_in_dim.7), calls=%async_computation.4 | async-start | bytes 2097152 | tf_op jit(solution)/shard_map/all_to_all | solution.py:531
  241.1 6.5 %collective-permute-done.9 = f32[8,4096]{1,0:T(8,128)} collective-permute-done((f32[8,4096]{1,0:T(8,128)S(1)}, f32[8,4096]{1,0:T(8,128)}, u32[]{:S(2)}, u32[]{:S(2)}) %collective-permute-start.9) | collective-permute-done | bytes 131104 | tf_op jit(solution)/shard_map/ppermute | solution.py:523
  248.9 5.3 %all-to-all-done.3 = f32[8,8,4096]{2,1,0:T(8,128)} async-done(((f32[8,8,4096]{2,1,0:T(8,128)}), f32[8,8,4096]{2,1,0:T(8,128)}, u32[]{:S(2)}, u32[]{:S(2)}) %all-to-all-start.3) | async-done | bytes 1048608 | tf_op jit(solution)/shard_map/all_to_all | solution.py:531
  254.3 19.1 %all_to_all.31 = f32[8,8,4096]{2,1,0:T(8,128)S(1)} all-to-all(f32[8,8,4096]{2,1,0:T(8,128)S(1)} %broadcast_in_dim.8), channel_id=1, replica_groups=mesh['xl'=2,'y'=4,'z'=8,'xh'=2,'c'=2] {'xl','y'}, dimensions={0} | all-to-all | bytes 2097152 | tf_op jit(solution)/shard_map/all_to_all | solution.py:531
  273.3 2.7 pad_maximum_fusion
  (45 shorter events, 12.2 us)
Async XLA Ops:
  6.5 1.6 copy-start
  6.5 46.8 %all-gather.2.cloned.1.call-start = ((), (), s32[]{:S(2)}) async-start(), calls=%async_computation.7 | async-start | bytes 2359296 | tf_op jit(solution)/shard_map/all_gather | solution.py:423
  14.2 34.9 %all-to-all-start = ((f32[32,136,128]{2,1,0:T(8,128)}), f32[32,136,128]{2,1,0:T(8,128)}, u32[]{:S(2)}, u32[]{:S(2)}) async-start(f32[32,136,128]{2,1,0:T(8,128)} %shard_map.37), calls=%async_computation | async-start | bytes 4456448 | tf_op jit(solution)/shard_map/all_to_all | solution.py:433
  65.5 8.8 %copy-start.9 = (f32[4,128,128]{2,1,0:T(8,128)S(1)}, f32[4,128,128]{2,1,0:T(8,128)}, u32[]{:S(2)}) copy-start(f32[4,128,128]{2,1,0:T(8,128)} %get-tuple-element.30) | copy-start | bytes 786436
  65.6 62.6 %copy-start.1 = (f32[256,256]{1,0:T(8,128)S(1)}, f32[256,256]{1,0:T(8,128)}, u32[]{:S(2)}) copy-start(f32[256,256]{1,0:T(8,128)} %get-tuple-element.27.refs_2_.dft_ref) | copy-start | bytes 786436
  65.6 62.6 %copy-start.6 = (f32[2,128,32]{2,1,0:T(8,128)S(1)}, f32[2,128,32]{2,1,0:T(8,128)}, u32[]{:S(2)}) copy-start(f32[2,128,32]{2,1,0:T(8,128)} %get-tuple-element.26.refs_1_) | copy-start | bytes 98308
  65.6 62.6 %all-to-all-start.1 = ((f32[32,2,128,128]{3,2,1,0:T(8,128)}), f32[32,2,128,128]{3,2,1,0:T(8,128)}, u32[]{:S(2)}, u32[]{:S(2)}) async-start(f32[32,2,128,128]{3,2,1,0:T(8,128)} %get-tuple-element.28), calls=%async_computation.1 | async-start | bytes 8388608 | tf_op jit(solution)/shard_map/all_to_all | solution.py:480
  73.2 12.4 %collective-permute-start = (f32[4,128,128]{2,1,0:T(8,128)}, f32[4,128,128]{2,1,0:T(8,128)S(1)}, u32[]{:S(2)}, u32[]{:S(2)}) collective-permute-start(f32[4,128,128]{2,1,0:T(8,128)} %get-tuple-element.29), channel_id=1, source_target_pairs={{0,4},{4,8},{8,12},{12,16},{16,20},{20,24},{24,28},{28,0},{1,5},{5... | collective-permute-start | bytes 786440 | tf_op jit(solution)/shard_map/ppermute | solution.py:477
  74.4 23.7 %collective-permute-start.1 = (f32[4,128,128]{2,1,0:T(8,128)S(1)}, f32[4,128,128]{2,1,0:T(8,128)S(1)}, u32[]{:S(2)}, u32[]{:S(2)}) collective-permute-start(f32[4,128,128]{2,1,0:T(8,128)S(1)} %copy-done.9), channel_id=1, source_target_pairs={{0,8},{4,12},{8,16},{12,20},{16,24},{20,28},{24,0},{28,4},{1,9},{5... | collective-permute-start | bytes 786440 | tf_op jit(solution)/shard_map/ppermute | solution.py:477
  76.4 41.4 %collective-permute-start.2 = (f32[4,128,128]{2,1,0:T(8,128)}, f32[4,128,128]{2,1,0:T(8,128)S(1)}, u32[]{:S(2)}, u32[]{:S(2)}) collective-permute-start(f32[4,128,128]{2,1,0:T(8,128)} %get-tuple-element.31), channel_id=1, source_target_pairs={{0,12},{4,16},{8,20},{12,24},{16,28},{20,0},{24,4},{28,8},{1,13},{... | collective-permute-start | bytes 786440 | tf_op jit(solution)/shard_map/ppermute | solution.py:477
  80.1 37.7 %collective-permute-start.3 = (f32[4,128,128]{2,1,0:T(8,128)}, f32[4,128,128]{2,1,0:T(8,128)}, u32[]{:S(2)}, u32[]{:S(2)}) collective-permute-start(f32[4,128,128]{2,1,0:T(8,128)} %get-tuple-element.32), channel_id=1, source_target_pairs={{0,16},{4,20},{8,24},{12,28},{16,0},{20,4},{24,8},{28,12},{1,17},{... | collective-permute-start | bytes 786440 | tf_op jit(solution)/shard_map/ppermute | solution.py:477
  81.0 36.9 %collective-permute-start.4 = (f32[4,128,128]{2,1,0:T(8,128)}, f32[4,128,128]{2,1,0:T(8,128)}, u32[]{:S(2)}, u32[]{:S(2)}) collective-permute-start(f32[4,128,128]{2,1,0:T(8,128)} %get-tuple-element.33), channel_id=1, source_target_pairs={{0,20},{4,24},{8,28},{12,0},{16,4},{20,8},{24,12},{28,16},{1,21},{... | collective-permute-start | bytes 786440 | tf_op jit(solution)/shard_map/ppermute | solution.py:477
  85.6 39.0 %collective-permute-start.5 = (f32[4,128,128]{2,1,0:T(8,128)}, f32[4,128,128]{2,1,0:T(8,128)}, u32[]{:S(2)}, u32[]{:S(2)}) collective-permute-start(f32[4,128,128]{2,1,0:T(8,128)} %get-tuple-element.34), channel_id=1, source_target_pairs={{0,24},{4,28},{8,0},{12,4},{16,8},{20,12},{24,16},{28,20},{1,25},{... | collective-permute-start | bytes 786440 | tf_op jit(solution)/shard_map/ppermute | solution.py:477
  98.1 30.1 %collective-permute-start.6 = (f32[4,128,128]{2,1,0:T(8,128)}, f32[4,128,128]{2,1,0:T(8,128)}, u32[]{:S(2)}, u32[]{:S(2)}) collective-permute-start(f32[4,128,128]{2,1,0:T(8,128)} %get-tuple-element.35), channel_id=1, source_target_pairs={{0,28},{4,0},{8,4},{12,8},{16,12},{20,16},{24,20},{28,24},{1,29},{... | collective-permute-start | bytes 786440 | tf_op jit(solution)/shard_map/ppermute | solution.py:477
  139.6 33.6 %copy-start.3 = (f32[32,2,64,128]{3,2,1,0:T(8,128)}, f32[32,2,64,128]{3,2,1,0:T(8,128)S(1)}, u32[]{:S(2)}) copy-start(f32[32,2,64,128]{3,2,1,0:T(8,128)S(1)} %get-tuple-element.41) | copy-start | bytes 6291460
  139.6 33.6 %copy-start.4 = (f32[2,64,4096]{2,1,0:T(8,128)S(1)}, f32[2,64,4096]{2,1,0:T(8,128)}, u32[]{:S(2)}) copy-start(f32[2,64,4096]{2,1,0:T(8,128)} %get-tuple-element.38.wave_ref) | copy-start | bytes 6291460
  139.6 33.5 %copy-start.5 = (f32[2,32,128]{2,1,0:T(8,128)S(1)}, f32[2,32,128]{2,1,0:T(8,128)}, u32[]{:S(2)}) copy-start(f32[2,32,128]{2,1,0:T(8,128)} %get-tuple-element.39.tw_ref) | copy-start | bytes 98308
  177.3 32.5 %all-to-all-start.4 = ((f32[32,2,64,128]{3,2,1,0:T(8,128)}), f32[32,2,64,128]{3,2,1,0:T(8,128)}, u32[]{:S(2)}, u32[]{:S(2)}) async-start(f32[32,2,64,128]{3,2,1,0:T(8,128)} %copy-done.3), calls=%async_computation.5 | async-start | bytes 4194304 | tf_op jit(solution)/shard_map/all_to_all | solution.py:507
  183.9 48.8 %reduce-scatter.2.cloned.1.call-start = ((), (), s32[]{:S(2)}) async-start(), calls=%async_computation.8 | async-start | bytes 1179648 | tf_op jit(solution)/shard_map/reduce_scatter | solution.py:518
  209.7 1.6 copy-start.2
  216.9 10.6 %collective-permute-start.7 = (f32[8,4096]{1,0:T(8,128)S(1)}, f32[8,4096]{1,0:T(8,128)S(1)}, u32[]{:S(2)}, u32[]{:S(2)}) collective-permute-start(f32[8,4096]{1,0:T(8,128)S(1)} %get-tuple-element.43), channel_id=1, source_target_pairs={{0,4},{4,8},{8,12},{12,16},{16,20},{20,24},{24,28},{28,0},{1,5},{5... | collective-permute-start | bytes 393224 | tf_op jit(solution)/shard_map/ppermute | solution.py:523
  220.1 9.5 %collective-permute-start.13 = (f32[8,4096]{1,0:T(8,128)S(1)}, f32[8,4096]{1,0:T(8,128)S(1)}, u32[]{:S(2)}, u32[]{:S(2)}) collective-permute-start(f32[8,4096]{1,0:T(8,128)S(1)} %get-tuple-element.44), channel_id=1, source_target_pairs={{0,28},{4,0},{8,4},{12,8},{16,12},{20,16},{24,20},{28,24},{1,29},{... | collective-permute-start | bytes 393224 | tf_op jit(solution)/shard_map/ppermute | solution.py:523
  220.2 20.9 %collective-permute-start.12 = (f32[8,4096]{1,0:T(8,128)}, f32[8,4096]{1,0:T(8,128)}, u32[]{:S(2)}, u32[]{:S(2)}) collective-permute-start(f32[8,4096]{1,0:T(8,128)} %get-tuple-element.45), channel_id=1, source_target_pairs={{0,24},{4,28},{8,0},{12,4},{16,8},{20,12},{24,16},{28,20},{1,25},{... | collective-permute-start | bytes 393224 | tf_op jit(solution)/shard_map/ppermute | solution.py:523
  221.0 20.0 %collective-permute-start.11 = (f32[8,4096]{1,0:T(8,128)}, f32[8,4096]{1,0:T(8,128)}, u32[]{:S(2)}, u32[]{:S(2)}) collective-permute-start(f32[8,4096]{1,0:T(8,128)} %get-tuple-element.46), channel_id=1, source_target_pairs={{0,20},{4,24},{8,28},{12,0},{16,4},{20,8},{24,12},{28,16},{1,21},{... | collective-permute-start | bytes 393224 | tf_op jit(solution)/shard_map/ppermute | solution.py:523
  225.4 15.6 %collective-permute-start.10 = (f32[8,4096]{1,0:T(8,128)}, f32[8,4096]{1,0:T(8,128)}, u32[]{:S(2)}, u32[]{:S(2)}) collective-permute-start(f32[8,4096]{1,0:T(8,128)} %get-tuple-element.47), channel_id=1, source_target_pairs={{0,16},{4,20},{8,24},{12,28},{16,0},{20,4},{24,8},{28,12},{1,17},{... | collective-permute-start | bytes 393224 | tf_op jit(solution)/shard_map/ppermute | solution.py:523
  227.5 2.0 copy-start.7
  227.5 20.1 %collective-permute-start.9 = (f32[8,4096]{1,0:T(8,128)S(1)}, f32[8,4096]{1,0:T(8,128)}, u32[]{:S(2)}, u32[]{:S(2)}) collective-permute-start(f32[8,4096]{1,0:T(8,128)S(1)} %get-tuple-element.48), channel_id=1, source_target_pairs={{0,12},{4,16},{8,20},{12,24},{16,28},{20,0},{24,4},{28,8},{1,13},{... | collective-permute-start | bytes 393224 | tf_op jit(solution)/shard_map/ppermute | solution.py:523
  229.5 0.7 copy-start.8
  230.2 17.4 %collective-permute-start.8 = (f32[8,4096]{1,0:T(8,128)S(1)}, f32[8,4096]{1,0:T(8,128)}, u32[]{:S(2)}, u32[]{:S(2)}) collective-permute-start(f32[8,4096]{1,0:T(8,128)S(1)} %get-tuple-element.49), channel_id=1, source_target_pairs={{0,8},{4,12},{8,16},{12,20},{16,24},{20,28},{24,0},{28,4},{1,9},{5... | collective-permute-start | bytes 393224 | tf_op jit(solution)/shard_map/ppermute | solution.py:523
  234.6 19.6 %all-to-all-start.3 = ((f32[8,8,4096]{2,1,0:T(8,128)}), f32[8,8,4096]{2,1,0:T(8,128)}, u32[]{:S(2)}, u32[]{:S(2)}) async-start(f32[8,8,4096]{2,1,0:T(8,128)} %broadcast_in_dim.7), calls=%async_computation.4 | async-start | bytes 2097152 | tf_op jit(solution)/shard_map/all_to_all | solution.py:531
Sparse Core Ops, SparseCore 0:
  9.1 44.1 all-gather.1
  187.2 38.5 reduce-scatter.1

commit v6 on v5

--- a/solution.py
+++ b/solution.py
@@ -120,6 +120,14 @@
     return slice(index * INNER, (index + 1) * INNER)
 
 
+def share_kernel(place_ref, phase_hbm, out_ref, sem):
+    share = out_ref.shape[0]
+    rows = pl.ds(pl.multiple_of(place_ref[0] * share, share), share)
+    copy = pltpu.make_async_copy(phase_hbm.at[rows], out_ref, sem)
+    copy.start()
+    copy.wait()
+
+
 def sort_kernel(depth_ref, target_ref, out_ref, turned_ref):
     for k in range(OUTER):
         turned_ref[tile(k), :] = target_ref[:, tile(k)].T
@@ -418,7 +426,15 @@
     place = lax.axis_index("xl") * lax.axis_size("y") + lax.axis_index("y")
     slab_size = math.prod(lax.axis_size(axis) for axis in SLAB)
     share = rows_dev // planes
-    mine = lax.dynamic_slice_in_dim(phase, place * share, share, 0)
+    (mine,) = call(
+        share_kernel,
+        [(share, length)],
+        [pltpu.SemaphoreType.DMA(())],
+        place.astype(jnp.int32)[None],
+        phase,
+        held=1,
+        limit=60,
+    )
     mine, targets = lax.optimization_barrier((mine, targets))
     rows_phase = lax.all_gather(mine, "z", axis=0, tiled=True)
 
@@ -502,8 +518,6 @@
     )
     results = []
     for half, wave in zip(halves, (first_wave, second_wave)):
-        if results:
-            half, results[0] = lax.optimization_barrier((half, results[0]))
         half = lax.all_to_all(half, SLAB, 0, 0, tiled=True)
         (part,) = call(
             gradient_kernel,
@@ -514,14 +528,7 @@
             twiddle,
             there,
         )
-        results.append(part)
-    results[0] = lax.psum_scatter(results[0], "z", scatter_dimension=0, tiled=True)
-    height = share // 2
-    total = lax.dynamic_slice_in_dim(results[1], layer * height, height, 0)
-    for k in range(1, layers):
-        part = lax.dynamic_slice_in_dim(results[1], (layer + k) % layers * height, height, 0)
-        total = total + lax.ppermute(part, "z", [(i, (i + k) % layers) for i in range(layers)])
-    results[1] = total
+        results.append(lax.psum_scatter(part, "z", scatter_dimension=0, tiled=True))
     results = [everywhere(part, planes) for part in results]
     return jnp.stack(results, axis=1).reshape(rows_dev, length)
 

time: 284 us -> 285 us (level)
  blocking collectives: 52.6 us -> 81.6 us
  starting transfers between devices: 62.6 us -> 40.1 us
  waiting for transfers between devices: 103 us -> 97.3 us
    reduce_scatter x1 -> x2, waiting for transfers between devices: 0.01 us -> 33.9 us  [on_device(): results.append(lax.psum_scatter(part, 'z', scatter_dimension=0, tiled=True))]
    all_to_all x1 -> x2, blocking collectives: 33.5 us -> 65.5 us  [on_device(): half = lax.all_to_all(half, SLAB, 0, 0, tiled=True)]
    all_to_all x1 -> x0, waiting for transfers between devices: 25 us -> none  [on_device(): half = lax.all_to_all(half, SLAB, 0, 0, tiled=True)]
    ppermute x7 -> x0, starting transfers between devices: 15 us -> none  [on_device(): lax.ppermute(part, 'z', [(i, (i + k) % layers) for i in range(layers)])]
    all_to_all x1 -> x0, starting transfers between devices: 6.58 us -> none  [on_device(): half = lax.all_to_all(half, SLAB, 0, 0, tiled=True)]
    ppermute x7 -> x0, waiting for transfers between devices: 6.56 us -> none  [on_device(): lax.ppermute(part, 'z', [(i, (i + k) % layers) for i in range(layers)])]
    all_to_all x1, waiting for transfers between devices: 5.29 us -> 0.01 us  [everywhere(): return lax.all_to_all(value, ('xl', 'y'), 0, 0, tiled=True)]
    ppermute x7, waiting for transfers between devices: 34.8 us -> 31.7 us  [on_device(): lax.ppermute(piece, 'z', [(i, (i + k) % layers) for i in range(layers)])]
  transfers between devices with their start and end apart: 20 -> 13, of which waited for: 9 -> 8; matrix products, arithmetic and copies ran while one was open for 2% -> 1% of each run, Pallas kernels for 3% -> 3%
where the time goes in v6:
time: 285 us; the launch traced here: 284 us
  waiting for transfers between devices  97.3 us (34%)
  blocking collectives  81.6 us (29%)
  starting transfers between devices  40.1 us (14%)
  Pallas kernels  38.3 us (13%)
  between operations  13.9 us (5%)
  local copies, waits for them, and re-layouts  10.5 us (4%)
    all_to_all x2, blocking collectives, on_device(): half = lax.all_to_all(half, SLAB, 0, 0, tiled=True)  65.5 us
    pallas_call x6, Pallas kernels, call(): pl.pallas_call(kernel, out_shape=[jax.ShapeDtypeStruct(shape, F32) for sh...  38.3 us
    reduce_scatter x2, waiting for transfers between devices, on_device(): results.append(lax.psum_scatter(part, 'z', scatter_dimension=0, tiled=True))  33.9 us
    ppermute x7, waiting for transfers between devices, on_device(): lax.ppermute(piece, 'z', [(i, (i + k) % layers) for i in range(layers)])  31.7 us
    all_to_all x1, waiting for transfers between devices, on_device(): sorted_targets = lax.all_to_all(sorted_targets, SLAB, 0, 0, tiled=True)  26.6 us
    ppermute x7, starting transfers between devices, on_device(): lax.ppermute(piece, 'z', [(i, (i + k) % layers) for i in range(layers)])  20.1 us
    all_to_all x1, blocking collectives, everywhere(): return lax.all_to_all(value, ('xl', 'y'), 0, 0, tiled=True)  16.1 us
    all_to_all x1, starting transfers between devices, on_device(): sorted_targets = lax.all_to_all(sorted_targets, SLAB, 0, 0, tiled=True)  7.59 us
  transfers between devices with their start and end apart: 13, of which 8 were waited for; matrix products, arithmetic and copies ran while one was open for 1% of the time, Pallas kernels for 3%

profile of v6, /device:TPU:4, one launch (start us, length us, event | category | flops | bytes accessed | tf_op | source)
XLA Modules:
  0.0 283.8 jit_solution(8505511489442117187)
XLA Ops:
  6.5 1.7 shard_map.37
  8.9 4.7 %shard_map.38 = f32[32,136,128]{2,1,0:T(8,128)} custom-call(s32[1]{0:T(128)S(6)} %copy.4.depth_ref, f32[128,4096]{1,0:T(8,128)} %bitcast.25), custom_call_target="tpu_custom_call" | custom-call | tf_op jit(solution)/shard_map/pallas_call | solution.py:400
  13.6 7.6 %all-to-all-start = ((f32[32,136,128]{2,1,0:T(8,128)}), f32[32,136,128]{2,1,0:T(8,128)S(1)}, u32[]{:S(2)}, u32[]{:S(2)}) async-start(f32[32,136,128]{2,1,0:T(8,128)} %shard_map.38), calls=%async_computation | async-start | bytes 4456448 | tf_op jit(solution)/shard_map/all_to_all | solution.py:449
  21.8 26.6 %all-to-all-done.targets_hbm = f32[32,136,128]{2,1,0:T(8,128)S(1)} async-done(((f32[32,136,128]{2,1,0:T(8,128)}), f32[32,136,128]{2,1,0:T(8,128)S(1)}, u32[]{:S(2)}, u32[]{:S(2)}) %all-to-all-start) | async-done | bytes 2228256 | tf_op jit(solution)/shard_map/all_to_all | solution.py:449
  48.4 5.0 %all-gather.2.cloned.1.call-done.phase_ref = f32[128,4096]{1,0:T(8,128)} async-done(((f32[16,4096]{1,0:T(8,128)}), f32[128,4096]{1,0:T(8,128)}) %all-gather.2.cloned.1.call-update) | async-done | bytes 2097168 | tf_op jit(solution)/shard_map/all_gather | solution.py:439
  53.5 12.2 %shard_map.39 = (f32[32,2,128,128]{3,2,1,0:T(8,128)}, f32[2,64,4096]{2,1,0:T(8,128)}, f32[2,64,4096]{2,1,0:T(8,128)}, f32[2,32,128]{2,1,0:T(8,128)}, f32[2,128,3...) custom-call(s32[2]{0:T(128)} %pad_add_fusion.place_ref, ...), custom_call_target="tpu_custom_call" | custom-call | tf_op jit(solution)/shard_map/pallas_call | solution.py:400
  65.8 7.5 %all-to-all-start.1 = ((f32[32,2,128,128]{3,2,1,0:T(8,128)}), f32[32,2,128,128]{3,2,1,0:T(8,128)}, u32[]{:S(2)}, u32[]{:S(2)}) async-start(f32[32,2,128,128]{3,2,1,0:T(8,128)} %get-tuple-element.26), calls=%async_computation.1 | async-start | bytes 8388608 | tf_op jit(solution)/shard_map/all_to_all | solution.py:496
  73.3 1.3 collective-permute-start
  74.6 2.2 collective-permute-start.1
  76.8 4.0 %collective-permute-start.2 = (f32[4,128,128]{2,1,0:T(8,128)}, f32[4,128,128]{2,1,0:T(8,128)S(1)}, u32[]{:S(2)}, u32[]{:S(2)}) collective-permute-start(f32[4,128,128]{2,1,0:T(8,128)} %get-tuple-element.29), channel_id=1, source_target_pairs={{0,12},{4,16},{8,20},{12,24},{16,28},{20,0},{24,4},{28,8},{1,13},{... | collective-permute-start | bytes 786440 | tf_op jit(solution)/shard_map/ppermute | solution.py:493
  81.4 4.9 %collective-permute-start.4 = (f32[4,128,128]{2,1,0:T(8,128)S(1)}, f32[4,128,128]{2,1,0:T(8,128)S(1)}, u32[]{:S(2)}, u32[]{:S(2)}) collective-permute-start(f32[4,128,128]{2,1,0:T(8,128)S(1)} %copy-done.16), channel_id=1, source_target_pairs={{0,20},{4,24},{8,28},{12,0},{16,4},{20,8},{24,12},{28,16},{1,21},{... | collective-permute-start | bytes 786440 | tf_op jit(solution)/shard_map/ppermute | solution.py:493
  86.3 4.3 %collective-permute-start.5 = (f32[4,128,128]{2,1,0:T(8,128)S(1)}, f32[4,128,128]{2,1,0:T(8,128)S(1)}, u32[]{:S(2)}, u32[]{:S(2)}) collective-permute-start(f32[4,128,128]{2,1,0:T(8,128)S(1)} %copy-done.15), channel_id=1, source_target_pairs={{0,24},{4,28},{8,0},{12,4},{16,8},{20,12},{24,16},{28,20},{1,25},{... | collective-permute-start | bytes 786440 | tf_op jit(solution)/shard_map/ppermute | solution.py:493
  90.6 7.9 %collective-permute-done.1 = f32[4,128,128]{2,1,0:T(8,128)S(1)} collective-permute-done((f32[4,128,128]{2,1,0:T(8,128)S(1)}, f32[4,128,128]{2,1,0:T(8,128)S(1)}, u32[]{:S(2)}, u32[]{:S(2)}) %collective-permute-start.1) | collective-permute-done | bytes 262176 | tf_op jit(solution)/shard_map/ppermute | solution.py:493
  98.5 2.8 collective-permute-start.6
  101.3 1.0 constant_dynamic-slice_fusion
  102.2 15.7 %collective-permute-done.2 = f32[4,128,128]{2,1,0:T(8,128)S(1)} collective-permute-done((f32[4,128,128]{2,1,0:T(8,128)}, f32[4,128,128]{2,1,0:T(8,128)S(1)}, u32[]{:S(2)}, u32[]{:S(2)}) %collective-permute-start.2) | collective-permute-done | bytes 262176 | tf_op jit(solution)/shard_map/ppermute | solution.py:493
  119.4 5.6 %collective-permute-done.5 = f32[4,128,128]{2,1,0:T(8,128)S(1)} collective-permute-done((f32[4,128,128]{2,1,0:T(8,128)S(1)}, f32[4,128,128]{2,1,0:T(8,128)S(1)}, u32[]{:S(2)}, u32[]{:S(2)}) %collective-permute-start.5) | collective-permute-done | bytes 262176 | tf_op jit(solution)/shard_map/ppermute | solution.py:493
  125.6 2.5 collective-permute-done.6
  129.9 0.9 copy-done.6
  130.8 0.9 copy-done.8
  131.8 0.9 copy-done.10
  132.7 11.4 %shard_map.40 = (f32[32,2,64,128]{3,2,1,0:T(8,128)S(1)}, f32[32,2,64,128]{3,2,1,0:T(8,128)S(1)}) custom-call(s32[1]{0:T(128)} %bitcast.refs_0_, f32[2,128,32]{2,1,0:T(8,128)S(1)} %copy-done.12, f32[256,256]{1,0:T(8,128)S(1)} %copy-done, f32[32,2,128,128]{3,2,1,0:T(8,128)} %all-to-all-done.1.refs_3_, f32[512,128]{1,0:T(8,128)S(1)} %bitcast.15, ...), custom_call_target="tpu_custom_call" | custom-call | tf_op jit(solution)/shard_map/pallas_call | solution.py:400
  144.1 33.4 %all_to_all.30.in_ref = f32[32,2,64,128]{3,2,1,0:T(8,128)S(1)} all-to-all(f32[32,2,64,128]{3,2,1,0:T(8,128)S(1)} %get-tuple-element.37), channel_id=1, replica_groups=mesh['xl'=2,'y'=4,'z'=8,'xh'=2,'c'=2] {'xl','y','xh','c'}, dimensions={0} | all-to-all | bytes 4194304 | tf_op jit(solution)/shard_map/all_to_all | solution.py:521
  177.5 4.1 %shard_map.42 = f32[64,4096]{1,0:T(8,128)} custom-call(f32[32,2,64,128]{3,2,1,0:T(8,128)S(1)} %all_to_all.30.in_ref, f32[2,64,4096]{2,1,0:T(8,128)S(1)} %copy-done.2, f32[2,32,128]{2,1,0:T(8,128)S(1)} %copy-done.11, f32[256,256]{1,0:T(8,128)S(1)} %copy-done), custom_call_target="tpu_custom_call" | custom-call | tf_op jit(solution)/shard_map/pallas_call | solution.py:400
  181.7 32.1 %all_to_all.31.in_ref = f32[32,2,64,128]{3,2,1,0:T(8,128)S(1)} all-to-all(f32[32,2,64,128]{3,2,1,0:T(8,128)S(1)} %get-tuple-element.34), channel_id=1, replica_groups=mesh['xl'=2,'y'=4,'z'=8,'xh'=2,'c'=2] {'xl','y','xh','c'}, dimensions={0} | all-to-all | bytes 4194304 | tf_op jit(solution)/shard_map/all_to_all | solution.py:521
  213.8 4.1 %shard_map.41 = f32[64,4096]{1,0:T(8,128)} custom-call(f32[32,2,64,128]{3,2,1,0:T(8,128)S(1)} %all_to_all.31.in_ref, f32[2,64,4096]{2,1,0:T(8,128)S(1)} %copy-done.1, f32[2,32,128]{2,1,0:T(8,128)S(1)} %copy-done.11, f32[256,256]{1,0:T(8,128)S(1)} %copy-done), custom_call_target="tpu_custom_call" | custom-call | tf_op jit(solution)/shard_map/pallas_call | solution.py:400
  218.8 1.9 broadcast_in_dim.21
  220.7 4.9 %all-to-all-start.5 = ((f32[8,8,4096]{2,1,0:T(8,128)}), f32[8,8,4096]{2,1,0:T(8,128)S(1)}, u32[]{:S(2)}, u32[]{:S(2)}) async-start(f32[8,8,4096]{2,1,0:T(8,128)} %broadcast_in_dim.21), calls=%async_computation.7 | async-start | bytes 2097152 | tf_op jit(solution)/shard_map/all_to_all | solution.py:538
  225.6 33.1 %reduce-scatter.3.cloned.1.call-done = f32[8,4096]{1,0:T(8,128)} async-done(((f32[64,4096]{1,0:T(8,128)}), f32[8,4096]{1,0:T(8,128)}) %reduce-scatter.3.cloned.1.call-update) | async-done | bytes 131088 | tf_op jit(solution)/shard_map/reduce_scatter | solution.py:531
  258.7 1.0 broadcast_in_dim.20
  259.7 16.1 %all_to_all.32 = f32[8,8,4096]{2,1,0:T(8,128)S(1)} all-to-all(f32[8,8,4096]{2,1,0:T(8,128)S(1)} %broadcast_in_dim.20), channel_id=1, replica_groups=mesh['xl'=2,'y'=4,'z'=8,'xh'=2,'c'=2] {'xl','y'}, dimensions={0} | all-to-all | bytes 2097152 | tf_op jit(solution)/shard_map/all_to_all | solution.py:538
  275.8 1.5 pad_maximum_fusion
  (51 shorter events, 5.9 us)
Async XLA Ops:
  6.5 46.9 %all-gather.2.cloned.1.call-start = ((), (), s32[]{:S(2)}) async-start(), calls=%async_computation.8 | async-start | bytes 2359296 | tf_op jit(solution)/shard_map/all_gather | solution.py:439
  13.6 34.8 %all-to-all-start = ((f32[32,136,128]{2,1,0:T(8,128)}), f32[32,136,128]{2,1,0:T(8,128)S(1)}, u32[]{:S(2)}, u32[]{:S(2)}) async-start(f32[32,136,128]{2,1,0:T(8,128)} %shard_map.38), calls=%async_computation | async-start | bytes 4456448 | tf_op jit(solution)/shard_map/all_to_all | solution.py:449
  48.4 5.0 %copy-start.13 = (f32[32,136,128]{2,1,0:T(8,128)}, f32[32,136,128]{2,1,0:T(8,128)S(1)}, u32[]{:S(2)}) copy-start(f32[32,136,128]{2,1,0:T(8,128)S(1)} %all-to-all-done.targets_hbm) | copy-start | bytes 6684676
  65.7 7.6 %copy-start.19 = (f32[4,128,128]{2,1,0:T(8,128)S(1)}, f32[4,128,128]{2,1,0:T(8,128)}, u32[]{:S(2)}) copy-start(f32[4,128,128]{2,1,0:T(8,128)} %get-tuple-element.27) | copy-start | bytes 786436
  65.7 8.9 %copy-start.18 = (f32[4,128,128]{2,1,0:T(8,128)S(1)}, f32[4,128,128]{2,1,0:T(8,128)}, u32[]{:S(2)}) copy-start(f32[4,128,128]{2,1,0:T(8,128)} %get-tuple-element.28) | copy-start | bytes 786436
  65.7 15.1 %copy-start.17 = (f32[4,128,128]{2,1,0:T(8,128)S(1)}, f32[4,128,128]{2,1,0:T(8,128)}, u32[]{:S(2)}) copy-start(f32[4,128,128]{2,1,0:T(8,128)} %get-tuple-element.30) | copy-start | bytes 786436
  65.7 15.7 %copy-start.16 = (f32[4,128,128]{2,1,0:T(8,128)S(1)}, f32[4,128,128]{2,1,0:T(8,128)}, u32[]{:S(2)}) copy-start(f32[4,128,128]{2,1,0:T(8,128)} %get-tuple-element.31) | copy-start | bytes 786436
  65.7 20.6 %copy-start.15 = (f32[4,128,128]{2,1,0:T(8,128)S(1)}, f32[4,128,128]{2,1,0:T(8,128)}, u32[]{:S(2)}) copy-start(f32[4,128,128]{2,1,0:T(8,128)} %get-tuple-element.32) | copy-start | bytes 786436
  65.7 32.7 %copy-start.14 = (f32[4,128,128]{2,1,0:T(8,128)S(1)}, f32[4,128,128]{2,1,0:T(8,128)}, u32[]{:S(2)}) copy-start(f32[4,128,128]{2,1,0:T(8,128)} %get-tuple-element.33) | copy-start | bytes 786436
  65.8 63.1 %copy-start = (f32[256,256]{1,0:T(8,128)S(1)}, f32[256,256]{1,0:T(8,128)}, u32[]{:S(2)}) copy-start(f32[256,256]{1,0:T(8,128)} %get-tuple-element.25.refs_2_.dft_ref) | copy-start | bytes 786436
  65.8 63.1 %copy-start.12 = (f32[2,128,32]{2,1,0:T(8,128)S(1)}, f32[2,128,32]{2,1,0:T(8,128)}, u32[]{:S(2)}) copy-start(f32[2,128,32]{2,1,0:T(8,128)} %get-tuple-element.24.refs_1_) | copy-start | bytes 98308
  65.8 63.1 %all-to-all-start.1 = ((f32[32,2,128,128]{3,2,1,0:T(8,128)}), f32[32,2,128,128]{3,2,1,0:T(8,128)}, u32[]{:S(2)}, u32[]{:S(2)}) async-start(f32[32,2,128,128]{3,2,1,0:T(8,128)} %get-tuple-element.26), calls=%async_computation.1 | async-start | bytes 8388608 | tf_op jit(solution)/shard_map/all_to_all | solution.py:496
  73.2 145.6 %reduce-scatter.5.cloned.1.call-start = ((), (), s32[]{:S(2)}) async-start(), calls=%async_computation.10 | async-start | bytes 1179648 | tf_op jit(solution)/shard_map/reduce_scatter | solution.py:531
  73.3 13.0 %collective-permute-start = (f32[4,128,128]{2,1,0:T(8,128)S(1)}, f32[4,128,128]{2,1,0:T(8,128)S(1)}, u32[]{:S(2)}, u32[]{:S(2)}) collective-permute-start(f32[4,128,128]{2,1,0:T(8,128)S(1)} %copy-done.19), channel_id=1, source_target_pairs={{0,4},{4,8},{8,12},{12,16},{16,20},{20,24},{24,28},{28,0},{1,5},{5... | collective-permute-start | bytes 786440 | tf_op jit(solution)/shard_map/ppermute | solution.py:493
  74.6 23.9 %collective-permute-start.1 = (f32[4,128,128]{2,1,0:T(8,128)S(1)}, f32[4,128,128]{2,1,0:T(8,128)S(1)}, u32[]{:S(2)}, u32[]{:S(2)}) collective-permute-start(f32[4,128,128]{2,1,0:T(8,128)S(1)} %copy-done.18), channel_id=1, source_target_pairs={{0,8},{4,12},{8,16},{12,20},{16,24},{20,28},{24,0},{28,4},{1,9},{5... | collective-permute-start | bytes 786440 | tf_op jit(solution)/shard_map/ppermute | solution.py:493
  76.8 41.1 %collective-permute-start.2 = (f32[4,128,128]{2,1,0:T(8,128)}, f32[4,128,128]{2,1,0:T(8,128)S(1)}, u32[]{:S(2)}, u32[]{:S(2)}) collective-permute-start(f32[4,128,128]{2,1,0:T(8,128)} %get-tuple-element.29), channel_id=1, source_target_pairs={{0,12},{4,16},{8,20},{12,24},{16,28},{20,0},{24,4},{28,8},{1,13},{... | collective-permute-start | bytes 786440 | tf_op jit(solution)/shard_map/ppermute | solution.py:493
  80.8 37.1 %collective-permute-start.3 = (f32[4,128,128]{2,1,0:T(8,128)S(1)}, f32[4,128,128]{2,1,0:T(8,128)S(1)}, u32[]{:S(2)}, u32[]{:S(2)}) collective-permute-start(f32[4,128,128]{2,1,0:T(8,128)S(1)} %copy-done.17), channel_id=1, source_target_pairs={{0,16},{4,20},{8,24},{12,28},{16,0},{20,4},{24,8},{28,12},{1,17},{... | collective-permute-start | bytes 786440 | tf_op jit(solution)/shard_map/ppermute | solution.py:493
  81.4 37.3 %collective-permute-start.4 = (f32[4,128,128]{2,1,0:T(8,128)S(1)}, f32[4,128,128]{2,1,0:T(8,128)S(1)}, u32[]{:S(2)}, u32[]{:S(2)}) collective-permute-start(f32[4,128,128]{2,1,0:T(8,128)S(1)} %copy-done.16), channel_id=1, source_target_pairs={{0,20},{4,24},{8,28},{12,0},{16,4},{20,8},{24,12},{28,16},{1,21},{... | collective-permute-start | bytes 786440 | tf_op jit(solution)/shard_map/ppermute | solution.py:493
  86.3 38.6 %collective-permute-start.5 = (f32[4,128,128]{2,1,0:T(8,128)S(1)}, f32[4,128,128]{2,1,0:T(8,128)S(1)}, u32[]{:S(2)}, u32[]{:S(2)}) collective-permute-start(f32[4,128,128]{2,1,0:T(8,128)S(1)} %copy-done.15), channel_id=1, source_target_pairs={{0,24},{4,28},{8,0},{12,4},{16,8},{20,12},{24,16},{28,20},{1,25},{... | collective-permute-start | bytes 786440 | tf_op jit(solution)/shard_map/ppermute | solution.py:493
  98.5 29.7 %collective-permute-start.6 = (f32[4,128,128]{2,1,0:T(8,128)S(1)}, f32[4,128,128]{2,1,0:T(8,128)S(1)}, u32[]{:S(2)}, u32[]{:S(2)}) collective-permute-start(f32[4,128,128]{2,1,0:T(8,128)S(1)} %copy-done.14), channel_id=1, source_target_pairs={{0,28},{4,0},{8,4},{12,8},{16,12},{20,16},{24,20},{28,24},{1,29},{... | collective-permute-start | bytes 786440 | tf_op jit(solution)/shard_map/ppermute | solution.py:493
  117.9 0.7 copy-start.3
  118.6 0.7 copy-start.5
  124.9 0.7 copy-start.7
  128.9 1.0 copy-start.4
  129.9 0.9 copy-start.6
  130.8 0.9 copy-start.8
  131.8 0.9 copy-start.10
  144.1 33.4 %copy-start.2 = (f32[2,64,4096]{2,1,0:T(8,128)S(1)}, f32[2,64,4096]{2,1,0:T(8,128)}, u32[]{:S(2)}) copy-start(f32[2,64,4096]{2,1,0:T(8,128)} %get-tuple-element.38.wave_ref) | copy-start | bytes 6291460
  144.1 33.4 %copy-start.11 = (f32[2,32,128]{2,1,0:T(8,128)S(1)}, f32[2,32,128]{2,1,0:T(8,128)}, u32[]{:S(2)}) copy-start(f32[2,32,128]{2,1,0:T(8,128)} %get-tuple-element.36.tw_ref) | copy-start | bytes 98308
  181.7 77.0 %reduce-scatter.3.cloned.1.call-start = ((), (), s32[]{:S(2)}) async-start(), calls=%async_computation.9 | async-start | bytes 1179648 | tf_op jit(solution)/shard_map/reduce_scatter | solution.py:531
  181.7 32.1 %copy-start.1 = (f32[2,64,4096]{2,1,0:T(8,128)S(1)}, f32[2,64,4096]{2,1,0:T(8,128)}, u32[]{:S(2)}) copy-start(f32[2,64,4096]{2,1,0:T(8,128)} %get-tuple-element.35.wave_ref) | copy-start | bytes 6291460
  220.7 38.0 %all-to-all-start.5 = ((f32[8,8,4096]{2,1,0:T(8,128)}), f32[8,8,4096]{2,1,0:T(8,128)S(1)}, u32[]{:S(2)}, u32[]{:S(2)}) async-start(f32[8,8,4096]{2,1,0:T(8,128)} %broadcast_in_dim.21), calls=%async_computation.7 | async-start | bytes 2097152 | tf_op jit(solution)/shard_map/all_to_all | solution.py:538
  (1 other events, 0.7 us)
Sparse Core Ops, SparseCore 0:
  9.1 44.2 all-gather.1
  181.8 36.9 reduce-scatter.4
  221.3 37.3 reduce-scatter.2

commit v7 on v5

--- a/solution.py
+++ b/solution.py
@@ -502,8 +502,6 @@
     )
     results = []
     for half, wave in zip(halves, (first_wave, second_wave)):
-        if results:
-            half, results[0] = lax.optimization_barrier((half, results[0]))
         half = lax.all_to_all(half, SLAB, 0, 0, tiled=True)
         (part,) = call(
             gradient_kernel,
@@ -514,14 +512,7 @@
             twiddle,
             there,
         )
-        results.append(part)
-    results[0] = lax.psum_scatter(results[0], "z", scatter_dimension=0, tiled=True)
-    height = share // 2
-    total = lax.dynamic_slice_in_dim(results[1], layer * height, height, 0)
-    for k in range(1, layers):
-        part = lax.dynamic_slice_in_dim(results[1], (layer + k) % layers * height, height, 0)
-        total = total + lax.ppermute(part, "z", [(i, (i + k) % layers) for i in range(layers)])
-    results[1] = total
+        results.append(lax.psum_scatter(part, "z", scatter_dimension=0, tiled=True))
     results = [everywhere(part, planes) for part in results]
     return jnp.stack(results, axis=1).reshape(rows_dev, length)
 

time: 284 us -> 280 us (0.986)
  blocking collectives: 52.6 us -> 82 us
  starting transfers between devices: 62.6 us -> 39.4 us
  waiting for transfers between devices: 103 us -> 99.1 us
    reduce_scatter x1 -> x2, waiting for transfers between devices: 0.01 us -> 33.3 us  [on_device(): results.append(lax.psum_scatter(part, 'z', scatter_dimension=0, tiled=True))]
    all_to_all x1 -> x2, blocking collectives: 33.5 us -> 65.8 us  [on_device(): half = lax.all_to_all(half, SLAB, 0, 0, tiled=True)]
    all_to_all x1 -> x0, waiting for transfers between devices: 25 us -> none  [on_device(): half = lax.all_to_all(half, SLAB, 0, 0, tiled=True)]
    ppermute x7 -> x0, starting transfers between devices: 15 us -> none  [on_device(): lax.ppermute(part, 'z', [(i, (i + k) % layers) for i in range(layers)])]
    all_to_all x1 -> x0, starting transfers between devices: 6.58 us -> none  [on_device(): half = lax.all_to_all(half, SLAB, 0, 0, tiled=True)]
    ppermute x7 -> x0, waiting for transfers between devices: 6.56 us -> none  [on_device(): lax.ppermute(part, 'z', [(i, (i + k) % layers) for i in range(layers)])]
    all_to_all x1, waiting for transfers between devices: 5.29 us -> 0.01 us  [everywhere(): return lax.all_to_all(value, ('xl', 'y'), 0, 0, tiled=True)]
    all_to_all x1, blocking collectives: 19.1 us -> 16.1 us  [everywhere(): return lax.all_to_all(value, ('xl', 'y'), 0, 0, tiled=True)]
  transfers between devices with their start and end apart: 20 -> 13, of which waited for: 9 -> 8; matrix products, arithmetic and copies ran while one was open for 2% -> 1% of each run, Pallas kernels for 3% -> 3%
where the time goes in v7:
time: 280 us; the launch traced here: 279 us
  waiting for transfers between devices  99.1 us (35%)
  blocking collectives  82 us (29%)
  starting transfers between devices  39.4 us (14%)
  Pallas kernels  36.6 us (13%)
  between operations  13.9 us (5%)
  local copies, waits for them, and re-layouts  6.22 us (2%)
    all_to_all x2, blocking collectives, on_device(): half = lax.all_to_all(half, SLAB, 0, 0, tiled=True)  65.8 us
    pallas_call x5, Pallas kernels, call(): pl.pallas_call(kernel, out_shape=[jax.ShapeDtypeStruct(shape, F32) for sh...  36.6 us
    ppermute x7, waiting for transfers between devices, on_device(): lax.ppermute(piece, 'z', [(i, (i + k) % layers) for i in range(layers)])  34.8 us
    reduce_scatter x2, waiting for transfers between devices, on_device(): results.append(lax.psum_scatter(part, 'z', scatter_dimension=0, tiled=True))  33.3 us
    all_to_all x1, waiting for transfers between devices, on_device(): sorted_targets = lax.all_to_all(sorted_targets, SLAB, 0, 0, tiled=True)  26.7 us
    ppermute x7, starting transfers between devices, on_device(): lax.ppermute(piece, 'z', [(i, (i + k) % layers) for i in range(layers)])  19.1 us
    all_to_all x1, blocking collectives, everywhere(): return lax.all_to_all(value, ('xl', 'y'), 0, 0, tiled=True)  16.1 us
    all_to_all x1, starting transfers between devices, on_device(): sorted_targets = lax.all_to_all(sorted_targets, SLAB, 0, 0, tiled=True)  7.64 us
  transfers between devices with their start and end apart: 13, of which 8 were waited for; matrix products, arithmetic and copies ran while one was open for 1% of the time, Pallas kernels for 3%

profile of v7, /device:TPU:4, one launch (start us, length us, event | category | flops | bytes accessed | tf_op | source)
XLA Modules:
  0.0 279.2 jit_solution(823663946054815935)
XLA Ops:
  6.5 1.6 copy-done
  8.1 0.7 constant_dynamic-slice_fusion.1
  9.5 4.7 %shard_map.37 = f32[32,136,128]{2,1,0:T(8,128)} custom-call(s32[1]{0:T(128)S(6)} %copy.4.depth_ref, f32[128,4096]{1,0:T(8,128)} %bitcast.20), custom_call_target="tpu_custom_call" | custom-call | tf_op jit(solution)/shard_map/pallas_call | solution.py:392
  14.2 7.6 %all-to-all-start = ((f32[32,136,128]{2,1,0:T(8,128)}), f32[32,136,128]{2,1,0:T(8,128)}, u32[]{:S(2)}, u32[]{:S(2)}) async-start(f32[32,136,128]{2,1,0:T(8,128)} %shard_map.37), calls=%async_computation | async-start | bytes 4456448 | tf_op jit(solution)/shard_map/all_to_all | solution.py:433
  21.9 0.6 pad_add_fusion.place_ref
  22.5 26.7 %all-to-all-done.targets_hbm = f32[32,136,128]{2,1,0:T(8,128)} async-done(((f32[32,136,128]{2,1,0:T(8,128)}), f32[32,136,128]{2,1,0:T(8,128)}, u32[]{:S(2)}, u32[]{:S(2)}) %all-to-all-start) | async-done | bytes 2228256 | tf_op jit(solution)/shard_map/all_to_all | solution.py:433
  49.2 4.1 %all-gather.2.cloned.1.call-done.phase_ref = f32[128,4096]{1,0:T(8,128)} async-done(((f32[16,4096]{1,0:T(8,128)}), f32[128,4096]{1,0:T(8,128)}) %all-gather.2.cloned.1.call-update) | async-done | bytes 2097168 | tf_op jit(solution)/shard_map/all_gather | solution.py:423
  53.3 12.2 %shard_map.38 = (f32[32,2,128,128]{3,2,1,0:T(8,128)}, f32[2,64,4096]{2,1,0:T(8,128)}, f32[2,64,4096]{2,1,0:T(8,128)}, f32[2,32,128]{2,1,0:T(8,128)}, f32[2,128,3...) custom-call(s32[2]{0:T(128)} %pad_add_fusion.place_ref, ...), custom_call_target="tpu_custom_call" | custom-call | tf_op jit(solution)/shard_map/pallas_call | solution.py:392
  65.5 7.6 %all-to-all-start.1 = ((f32[32,2,128,128]{3,2,1,0:T(8,128)}), f32[32,2,128,128]{3,2,1,0:T(8,128)}, u32[]{:S(2)}, u32[]{:S(2)}) async-start(f32[32,2,128,128]{3,2,1,0:T(8,128)} %get-tuple-element.26), calls=%async_computation.1 | async-start | bytes 8388608 | tf_op jit(solution)/shard_map/all_to_all | solution.py:480
  73.2 1.2 collective-permute-start
  74.4 2.0 collective-permute-start.1
  76.5 3.7 %collective-permute-start.2 = (f32[4,128,128]{2,1,0:T(8,128)}, f32[4,128,128]{2,1,0:T(8,128)S(1)}, u32[]{:S(2)}, u32[]{:S(2)}) collective-permute-start(f32[4,128,128]{2,1,0:T(8,128)} %get-tuple-element.29), channel_id=1, source_target_pairs={{0,12},{4,16},{8,20},{12,24},{16,28},{20,0},{24,4},{28,8},{1,13},{... | collective-permute-start | bytes 786440 | tf_op jit(solution)/shard_map/ppermute | solution.py:477
  80.1 0.9 collective-permute-start.3
  81.0 4.6 %collective-permute-start.4 = (f32[4,128,128]{2,1,0:T(8,128)}, f32[4,128,128]{2,1,0:T(8,128)}, u32[]{:S(2)}, u32[]{:S(2)}) collective-permute-start(f32[4,128,128]{2,1,0:T(8,128)} %get-tuple-element.31), channel_id=1, source_target_pairs={{0,20},{4,24},{8,28},{12,0},{16,4},{20,8},{24,12},{28,16},{1,21},{... | collective-permute-start | bytes 786440 | tf_op jit(solution)/shard_map/ppermute | solution.py:477
  85.6 3.6 %collective-permute-start.5 = (f32[4,128,128]{2,1,0:T(8,128)}, f32[4,128,128]{2,1,0:T(8,128)}, u32[]{:S(2)}, u32[]{:S(2)}) collective-permute-start(f32[4,128,128]{2,1,0:T(8,128)} %get-tuple-element.32), channel_id=1, source_target_pairs={{0,24},{4,28},{8,0},{12,4},{16,8},{20,12},{24,16},{28,20},{1,25},{... | collective-permute-start | bytes 786440 | tf_op jit(solution)/shard_map/ppermute | solution.py:477
  89.2 8.9 %collective-permute-done.1 = f32[4,128,128]{2,1,0:T(8,128)S(1)} collective-permute-done((f32[4,128,128]{2,1,0:T(8,128)S(1)}, f32[4,128,128]{2,1,0:T(8,128)S(1)}, u32[]{:S(2)}, u32[]{:S(2)}) %collective-permute-start.1) | collective-permute-done | bytes 262176 | tf_op jit(solution)/shard_map/ppermute | solution.py:477
  98.1 3.2 %collective-permute-start.6 = (f32[4,128,128]{2,1,0:T(8,128)}, f32[4,128,128]{2,1,0:T(8,128)}, u32[]{:S(2)}, u32[]{:S(2)}) collective-permute-start(f32[4,128,128]{2,1,0:T(8,128)} %get-tuple-element.33), channel_id=1, source_target_pairs={{0,28},{4,0},{8,4},{12,8},{16,12},{20,16},{24,20},{28,24},{1,29},{... | collective-permute-start | bytes 786440 | tf_op jit(solution)/shard_map/ppermute | solution.py:477
  101.3 1.0 constant_dynamic-slice_fusion
  102.3 15.6 %collective-permute-done.2 = f32[4,128,128]{2,1,0:T(8,128)S(1)} collective-permute-done((f32[4,128,128]{2,1,0:T(8,128)}, f32[4,128,128]{2,1,0:T(8,128)S(1)}, u32[]{:S(2)}, u32[]{:S(2)}) %collective-permute-start.2) | collective-permute-done | bytes 262176 | tf_op jit(solution)/shard_map/ppermute | solution.py:477
  117.8 6.8 %collective-permute-done.5 = f32[4,128,128]{2,1,0:T(8,128)} collective-permute-done((f32[4,128,128]{2,1,0:T(8,128)}, f32[4,128,128]{2,1,0:T(8,128)}, u32[]{:S(2)}, u32[]{:S(2)}) %collective-permute-start.5) | collective-permute-done | bytes 262176 | tf_op jit(solution)/shard_map/ppermute | solution.py:477
  124.6 3.6 %collective-permute-done.6 = f32[4,128,128]{2,1,0:T(8,128)} collective-permute-done((f32[4,128,128]{2,1,0:T(8,128)}, f32[4,128,128]{2,1,0:T(8,128)}, u32[]{:S(2)}, u32[]{:S(2)}) %collective-permute-start.6) | collective-permute-done | bytes 262176 | tf_op jit(solution)/shard_map/ppermute | solution.py:477
  128.2 11.4 %shard_map.39 = (f32[32,2,64,128]{3,2,1,0:T(8,128)S(1)}, f32[32,2,64,128]{3,2,1,0:T(8,128)S(1)}) custom-call(s32[1]{0:T(128)} %bitcast.refs_0_, f32[2,128,32]{2,1,0:T(8,128)S(1)} %copy-done.6, f32[256,256]{1,0:T(8,128)S(1)} %copy-done.1, f32[32,2,128,128]{3,2,1,0:T(8,128)} %all-to-all-done.1.refs_3_, f32[512,128]{1,0:T(8,128)S(1)} %bitcast.14, ...), custom_call_target="tpu_custom_call" | custom-call | tf_op jit(solution)/shard_map/pallas_call | solution.py:392
  139.6 33.5 %all_to_all.30.in_ref = f32[32,2,64,128]{3,2,1,0:T(8,128)S(1)} all-to-all(f32[32,2,64,128]{3,2,1,0:T(8,128)S(1)} %get-tuple-element.37), channel_id=1, replica_groups=mesh['xl'=2,'y'=4,'z'=8,'xh'=2,'c'=2] {'xl','y','xh','c'}, dimensions={0} | all-to-all | bytes 4194304 | tf_op jit(solution)/shard_map/all_to_all | solution.py:505
  173.2 4.1 %shard_map.41 = f32[64,4096]{1,0:T(8,128)} custom-call(f32[32,2,64,128]{3,2,1,0:T(8,128)S(1)} %all_to_all.30.in_ref, f32[2,64,4096]{2,1,0:T(8,128)S(1)} %copy-done.3, f32[2,32,128]{2,1,0:T(8,128)S(1)} %copy-done.5, f32[256,256]{1,0:T(8,128)S(1)} %copy-done.1), custom_call_target="tpu_custom_call" | custom-call | tf_op jit(solution)/shard_map/pallas_call | solution.py:392
  177.4 32.3 %all_to_all.31.in_ref = f32[32,2,64,128]{3,2,1,0:T(8,128)S(1)} all-to-all(f32[32,2,64,128]{3,2,1,0:T(8,128)} %copy-done.4), channel_id=1, replica_groups=mesh['xl'=2,'y'=4,'z'=8,'xh'=2,'c'=2] {'xl','y','xh','c'}, dimensions={0} | all-to-all | bytes 4194304 | tf_op jit(solution)/shard_map/all_to_all | solution.py:505
  209.7 4.2 %shard_map.40 = f32[64,4096]{1,0:T(8,128)} custom-call(f32[32,2,64,128]{3,2,1,0:T(8,128)S(1)} %all_to_all.31.in_ref, f32[2,64,4096]{2,1,0:T(8,128)S(1)} %copy-done.2, f32[2,32,128]{2,1,0:T(8,128)S(1)} %copy-done.5, f32[256,256]{1,0:T(8,128)S(1)} %copy-done.1), custom_call_target="tpu_custom_call" | custom-call | tf_op jit(solution)/shard_map/pallas_call | solution.py:392
  214.1 1.9 broadcast_in_dim.8
  216.0 4.9 %all-to-all-start.5 = ((f32[8,8,4096]{2,1,0:T(8,128)}), f32[8,8,4096]{2,1,0:T(8,128)S(1)}, u32[]{:S(2)}, u32[]{:S(2)}) async-start(f32[8,8,4096]{2,1,0:T(8,128)} %broadcast_in_dim.8), calls=%async_computation.7 | async-start | bytes 2097152 | tf_op jit(solution)/shard_map/all_to_all | solution.py:522
  221.0 33.1 %reduce-scatter.3.cloned.1.call-done = f32[8,4096]{1,0:T(8,128)} async-done(((f32[64,4096]{1,0:T(8,128)}), f32[8,4096]{1,0:T(8,128)}) %reduce-scatter.3.cloned.1.call-update) | async-done | bytes 131088 | tf_op jit(solution)/shard_map/reduce_scatter | solution.py:515
  254.1 1.0 broadcast_in_dim.7
  255.1 16.1 %all_to_all.32 = f32[8,8,4096]{2,1,0:T(8,128)S(1)} all-to-all(f32[8,8,4096]{2,1,0:T(8,128)S(1)} %broadcast_in_dim.7), channel_id=1, replica_groups=mesh['xl'=2,'y'=4,'z'=8,'xh'=2,'c'=2] {'xl','y'}, dimensions={0} | all-to-all | bytes 2097152 | tf_op jit(solution)/shard_map/all_to_all | solution.py:522
  271.2 1.5 pad_maximum_fusion
  (27 shorter events, 0.4 us)
Async XLA Ops:
  6.5 1.6 copy-start
  6.5 46.8 %all-gather.2.cloned.1.call-start = ((), (), s32[]{:S(2)}) async-start(), calls=%async_computation.8 | async-start | bytes 2359296 | tf_op jit(solution)/shard_map/all_gather | solution.py:423
  14.2 34.9 %all-to-all-start = ((f32[32,136,128]{2,1,0:T(8,128)}), f32[32,136,128]{2,1,0:T(8,128)}, u32[]{:S(2)}, u32[]{:S(2)}) async-start(f32[32,136,128]{2,1,0:T(8,128)} %shard_map.37), calls=%async_computation | async-start | bytes 4456448 | tf_op jit(solution)/shard_map/all_to_all | solution.py:433
  65.5 8.9 %copy-start.7 = (f32[4,128,128]{2,1,0:T(8,128)S(1)}, f32[4,128,128]{2,1,0:T(8,128)}, u32[]{:S(2)}) copy-start(f32[4,128,128]{2,1,0:T(8,128)} %get-tuple-element.28) | copy-start | bytes 786436
  65.5 62.7 %copy-start.1 = (f32[256,256]{1,0:T(8,128)S(1)}, f32[256,256]{1,0:T(8,128)}, u32[]{:S(2)}) copy-start(f32[256,256]{1,0:T(8,128)} %get-tuple-element.25.refs_2_.dft_ref) | copy-start | bytes 786436
  65.5 62.6 %copy-start.6 = (f32[2,128,32]{2,1,0:T(8,128)S(1)}, f32[2,128,32]{2,1,0:T(8,128)}, u32[]{:S(2)}) copy-start(f32[2,128,32]{2,1,0:T(8,128)} %get-tuple-element.24.refs_1_) | copy-start | bytes 98308
  65.5 62.6 %all-to-all-start.1 = ((f32[32,2,128,128]{3,2,1,0:T(8,128)}), f32[32,2,128,128]{3,2,1,0:T(8,128)}, u32[]{:S(2)}, u32[]{:S(2)}) async-start(f32[32,2,128,128]{3,2,1,0:T(8,128)} %get-tuple-element.26), calls=%async_computation.1 | async-start | bytes 8388608 | tf_op jit(solution)/shard_map/all_to_all | solution.py:480
  73.2 140.9 %reduce-scatter.5.cloned.1.call-start = ((), (), s32[]{:S(2)}) async-start(), calls=%async_computation.10 | async-start | bytes 1179648 | tf_op jit(solution)/shard_map/reduce_scatter | solution.py:515
  73.2 12.4 %collective-permute-start = (f32[4,128,128]{2,1,0:T(8,128)}, f32[4,128,128]{2,1,0:T(8,128)S(1)}, u32[]{:S(2)}, u32[]{:S(2)}) collective-permute-start(f32[4,128,128]{2,1,0:T(8,128)} %get-tuple-element.27), channel_id=1, source_target_pairs={{0,4},{4,8},{8,12},{12,16},{16,20},{20,24},{24,28},{28,0},{1,5},{5... | collective-permute-start | bytes 786440 | tf_op jit(solution)/shard_map/ppermute | solution.py:477
  74.4 23.7 %collective-permute-start.1 = (f32[4,128,128]{2,1,0:T(8,128)S(1)}, f32[4,128,128]{2,1,0:T(8,128)S(1)}, u32[]{:S(2)}, u32[]{:S(2)}) collective-permute-start(f32[4,128,128]{2,1,0:T(8,128)S(1)} %copy-done.7), channel_id=1, source_target_pairs={{0,8},{4,12},{8,16},{12,20},{16,24},{20,28},{24,0},{28,4},{1,9},{5... | collective-permute-start | bytes 786440 | tf_op jit(solution)/shard_map/ppermute | solution.py:477
  76.5 41.4 %collective-permute-start.2 = (f32[4,128,128]{2,1,0:T(8,128)}, f32[4,128,128]{2,1,0:T(8,128)S(1)}, u32[]{:S(2)}, u32[]{:S(2)}) collective-permute-start(f32[4,128,128]{2,1,0:T(8,128)} %get-tuple-element.29), channel_id=1, source_target_pairs={{0,12},{4,16},{8,20},{12,24},{16,28},{20,0},{24,4},{28,8},{1,13},{... | collective-permute-start | bytes 786440 | tf_op jit(solution)/shard_map/ppermute | solution.py:477
  80.1 37.7 %collective-permute-start.3 = (f32[4,128,128]{2,1,0:T(8,128)}, f32[4,128,128]{2,1,0:T(8,128)}, u32[]{:S(2)}, u32[]{:S(2)}) collective-permute-start(f32[4,128,128]{2,1,0:T(8,128)} %get-tuple-element.30), channel_id=1, source_target_pairs={{0,16},{4,20},{8,24},{12,28},{16,0},{20,4},{24,8},{28,12},{1,17},{... | collective-permute-start | bytes 786440 | tf_op jit(solution)/shard_map/ppermute | solution.py:477
  81.0 36.8 %collective-permute-start.4 = (f32[4,128,128]{2,1,0:T(8,128)}, f32[4,128,128]{2,1,0:T(8,128)}, u32[]{:S(2)}, u32[]{:S(2)}) collective-permute-start(f32[4,128,128]{2,1,0:T(8,128)} %get-tuple-element.31), channel_id=1, source_target_pairs={{0,20},{4,24},{8,28},{12,0},{16,4},{20,8},{24,12},{28,16},{1,21},{... | collective-permute-start | bytes 786440 | tf_op jit(solution)/shard_map/ppermute | solution.py:477
  85.6 39.0 %collective-permute-start.5 = (f32[4,128,128]{2,1,0:T(8,128)}, f32[4,128,128]{2,1,0:T(8,128)}, u32[]{:S(2)}, u32[]{:S(2)}) collective-permute-start(f32[4,128,128]{2,1,0:T(8,128)} %get-tuple-element.32), channel_id=1, source_target_pairs={{0,24},{4,28},{8,0},{12,4},{16,8},{20,12},{24,16},{28,20},{1,25},{... | collective-permute-start | bytes 786440 | tf_op jit(solution)/shard_map/ppermute | solution.py:477
  98.1 30.1 %collective-permute-start.6 = (f32[4,128,128]{2,1,0:T(8,128)}, f32[4,128,128]{2,1,0:T(8,128)}, u32[]{:S(2)}, u32[]{:S(2)}) collective-permute-start(f32[4,128,128]{2,1,0:T(8,128)} %get-tuple-element.33), channel_id=1, source_target_pairs={{0,28},{4,0},{8,4},{12,8},{16,12},{20,16},{24,20},{28,24},{1,29},{... | collective-permute-start | bytes 786440 | tf_op jit(solution)/shard_map/ppermute | solution.py:477
  139.6 33.6 %copy-start.4 = (f32[32,2,64,128]{3,2,1,0:T(8,128)}, f32[32,2,64,128]{3,2,1,0:T(8,128)S(1)}, u32[]{:S(2)}) copy-start(f32[32,2,64,128]{3,2,1,0:T(8,128)S(1)} %get-tuple-element.34) | copy-start | bytes 6291460
  139.6 33.6 %copy-start.3 = (f32[2,64,4096]{2,1,0:T(8,128)S(1)}, f32[2,64,4096]{2,1,0:T(8,128)}, u32[]{:S(2)}) copy-start(f32[2,64,4096]{2,1,0:T(8,128)} %get-tuple-element.38.wave_ref) | copy-start | bytes 6291460
  139.6 33.5 %copy-start.5 = (f32[2,32,128]{2,1,0:T(8,128)S(1)}, f32[2,32,128]{2,1,0:T(8,128)}, u32[]{:S(2)}) copy-start(f32[2,32,128]{2,1,0:T(8,128)} %get-tuple-element.36.tw_ref) | copy-start | bytes 98308
  177.3 76.8 %reduce-scatter.3.cloned.1.call-start = ((), (), s32[]{:S(2)}) async-start(), calls=%async_computation.9 | async-start | bytes 1179648 | tf_op jit(solution)/shard_map/reduce_scatter | solution.py:515
  177.4 32.3 %copy-start.2 = (f32[2,64,4096]{2,1,0:T(8,128)S(1)}, f32[2,64,4096]{2,1,0:T(8,128)}, u32[]{:S(2)}) copy-start(f32[2,64,4096]{2,1,0:T(8,128)} %get-tuple-element.35.wave_ref) | copy-start | bytes 6291460
  216.0 38.0 %all-to-all-start.5 = ((f32[8,8,4096]{2,1,0:T(8,128)}), f32[8,8,4096]{2,1,0:T(8,128)S(1)}, u32[]{:S(2)}, u32[]{:S(2)}) async-start(f32[8,8,4096]{2,1,0:T(8,128)} %broadcast_in_dim.8), calls=%async_computation.7 | async-start | bytes 2097152 | tf_op jit(solution)/shard_map/all_to_all | solution.py:522
Sparse Core Ops, SparseCore 0:
  9.1 44.1 all-gather.1
  177.4 36.6 reduce-scatter.4
  216.6 37.3 reduce-scatter.2

commit v8 on v4

--- a/solution.py
+++ b/solution.py
@@ -179,10 +179,6 @@
     inside = local & (BLOCK - 1)
     row_ref[...] = chirp((local - inside) * (length // layers // BLOCK) + place_ref[1] + inside)
 
-    stage.wait()
-    for send in sends:
-        send.start()
-
     def save_wave(step):
         rows = row_block(step)
         return pltpu.make_async_copy(wave_ref.at[:, rows, :], wave_hbm.at[:, rows, :], sem.at[0])
@@ -215,6 +211,9 @@
         return carry
 
     lax.fori_loop(0, INNER // BLOCK, block, 0)
+    stage.wait()
+    for send in sends:
+        send.start()
 
     def multiply(step, carry):
         group = pl.ds(step * 4, 4)

time: 280 us -> 279 us (level)
  no operation moved by 1% of the time
where the time goes in v8:
time: 279 us; the launch traced here: 278 us
  waiting for transfers between devices  106 us (38%)
  blocking collectives  83.5 us (30%)
  starting transfers between devices  34.6 us (12%)
  Pallas kernels  32.6 us (12%)
  between operations  14.2 us (5%)
  local copies, waits for them, and re-layouts  7.08 us (3%)
    all_to_all x1, blocking collectives, on_device(): spectrum = lax.all_to_all(spectrum, SLAB, 0, 0, tiled=True)  56 us
    reduce_scatter x1, waiting for transfers between devices, on_device(): part = lax.psum_scatter(part, 'z', scatter_dimension=0, tiled=True)  40.2 us
    ppermute x7, waiting for transfers between devices, on_device(): lax.ppermute(piece, 'z', [(i, (i + k) % layers) for i in range(layers)])  34.7 us
    pallas_call x4, Pallas kernels, call(): pl.pallas_call(kernel, out_shape=[jax.ShapeDtypeStruct(shape, F32) for sh...  32.6 us
    all_to_all x1, blocking collectives, on_device(): lax.all_to_all(part, ('xl', 'y'), 0, 0, tiled=True)  27.5 us
    all_to_all x1, waiting for transfers between devices, on_device(): sorted_targets = lax.all_to_all(sorted_targets, SLAB, 0, 0, tiled=True)  26.7 us
    ppermute x7, starting transfers between devices, on_device(): lax.ppermute(piece, 'z', [(i, (i + k) % layers) for i in range(layers)])  19.2 us
    all_to_all x1, starting transfers between devices, on_device(): sorted_targets = lax.all_to_all(sorted_targets, SLAB, 0, 0, tiled=True)  7.64 us
  transfers between devices with their start and end apart: 11, of which 7 were waited for; matrix products, arithmetic and copies ran while one was open for 1% of the time, Pallas kernels for 2%

profile of v8, /device:TPU:4, one launch (start us, length us, event | category | flops | bytes accessed | tf_op | source)
XLA Modules:
  0.0 278.3 jit_solution(217872283605220134)
XLA Ops:
  6.5 1.6 copy-done
  8.1 0.7 constant_dynamic-slice_fusion.1
  8.8 0.0 all-gather.2.cloned.1.call-update
  9.5 4.7 %shard_map.37 = f32[32,136,128]{2,1,0:T(8,128)} custom-call(s32[1]{0:T(128)S(6)} %copy.5.depth_ref, f32[128,4096]{1,0:T(8,128)} %bitcast.17), custom_call_target="tpu_custom_call" | custom-call | tf_op jit(solution)/shard_map/pallas_call | solution.py:375
  14.2 7.6 %all-to-all-start = ((f32[32,136,128]{2,1,0:T(8,128)}), f32[32,136,128]{2,1,0:T(8,128)}, u32[]{:S(2)}, u32[]{:S(2)}) async-start(f32[32,136,128]{2,1,0:T(8,128)} %shard_map.37), calls=%async_computation | async-start | bytes 4456448 | tf_op jit(solution)/shard_map/all_to_all | solution.py:416
  21.9 0.6 pad_add_fusion.place_ref
  22.5 26.7 %all-to-all-done.targets_hbm = f32[32,136,128]{2,1,0:T(8,128)} async-done(((f32[32,136,128]{2,1,0:T(8,128)}), f32[32,136,128]{2,1,0:T(8,128)}, u32[]{:S(2)}, u32[]{:S(2)}) %all-to-all-start) | async-done | bytes 2228256 | tf_op jit(solution)/shard_map/all_to_all | solution.py:416
  49.2 4.1 %all-gather.2.cloned.1.call-done.phase_ref = f32[128,4096]{1,0:T(8,128)} async-done(((f32[16,4096]{1,0:T(8,128)}), f32[128,4096]{1,0:T(8,128)}) %all-gather.2.cloned.1.call-update) | async-done | bytes 2097168 | tf_op jit(solution)/shard_map/all_gather | solution.py:406
  53.3 11.5 %shard_map.38 = (f32[32,2,128,128]{3,2,1,0:T(8,128)}, f32[2,128,4096]{2,1,0:T(8,128)}, f32[2,32,128]{2,1,0:T(8,128)}, f32[2,128,32]{2,1,0:T(8,128)}, f32[256,256...) custom-call(s32[2]{0:T(128)} %pad_add_fusion.place_ref, ...), custom_call_target="tpu_custom_call" | custom-call | tf_op jit(solution)/shard_map/pallas_call | solution.py:375
  64.9 7.6 %all-to-all-start.1 = ((f32[32,2,128,128]{3,2,1,0:T(8,128)}), f32[32,2,128,128]{3,2,1,0:T(8,128)}, u32[]{:S(2)}, u32[]{:S(2)}) async-start(f32[32,2,128,128]{3,2,1,0:T(8,128)} %get-tuple-element.23), calls=%async_computation.1 | async-start | bytes 8388608 | tf_op jit(solution)/shard_map/all_to_all | solution.py:462
  72.6 0.0 reduce-scatter.2.cloned.1.call-start
  72.6 1.1 collective-permute-start
  73.8 2.1 collective-permute-start.1
  75.8 3.7 %collective-permute-start.2 = (f32[4,128,128]{2,1,0:T(8,128)}, f32[4,128,128]{2,1,0:T(8,128)S(1)}, u32[]{:S(2)}, u32[]{:S(2)}) collective-permute-start(f32[4,128,128]{2,1,0:T(8,128)} %get-tuple-element.26), channel_id=1, source_target_pairs={{0,12},{4,16},{8,20},{12,24},{16,28},{20,0},{24,4},{28,8},{1,13},{... | collective-permute-start | bytes 786440 | tf_op jit(solution)/shard_map/ppermute | solution.py:459
  79.5 0.9 collective-permute-start.3
  80.4 4.6 %collective-permute-start.4 = (f32[4,128,128]{2,1,0:T(8,128)}, f32[4,128,128]{2,1,0:T(8,128)}, u32[]{:S(2)}, u32[]{:S(2)}) collective-permute-start(f32[4,128,128]{2,1,0:T(8,128)} %get-tuple-element.28), channel_id=1, source_target_pairs={{0,20},{4,24},{8,28},{12,0},{16,4},{20,8},{24,12},{28,16},{1,21},{... | collective-permute-start | bytes 786440 | tf_op jit(solution)/shard_map/ppermute | solution.py:459
  85.0 3.6 %collective-permute-start.5 = (f32[4,128,128]{2,1,0:T(8,128)}, f32[4,128,128]{2,1,0:T(8,128)}, u32[]{:S(2)}, u32[]{:S(2)}) collective-permute-start(f32[4,128,128]{2,1,0:T(8,128)} %get-tuple-element.29), channel_id=1, source_target_pairs={{0,24},{4,28},{8,0},{12,4},{16,8},{20,12},{24,16},{28,20},{1,25},{... | collective-permute-start | bytes 786440 | tf_op jit(solution)/shard_map/ppermute | solution.py:459
  88.6 8.8 %collective-permute-done.1 = f32[4,128,128]{2,1,0:T(8,128)S(1)} collective-permute-done((f32[4,128,128]{2,1,0:T(8,128)S(1)}, f32[4,128,128]{2,1,0:T(8,128)S(1)}, u32[]{:S(2)}, u32[]{:S(2)}) %collective-permute-start.1) | collective-permute-done | bytes 262176 | tf_op jit(solution)/shard_map/ppermute | solution.py:459
  97.4 3.3 %collective-permute-start.6 = (f32[4,128,128]{2,1,0:T(8,128)}, f32[4,128,128]{2,1,0:T(8,128)}, u32[]{:S(2)}, u32[]{:S(2)}) collective-permute-start(f32[4,128,128]{2,1,0:T(8,128)} %get-tuple-element.30), channel_id=1, source_target_pairs={{0,28},{4,0},{8,4},{12,8},{16,12},{20,16},{24,20},{28,24},{1,29},{... | collective-permute-start | bytes 786440 | tf_op jit(solution)/shard_map/ppermute | solution.py:459
  100.7 1.0 constant_dynamic-slice_fusion
  101.7 15.6 %collective-permute-done.2 = f32[4,128,128]{2,1,0:T(8,128)S(1)} collective-permute-done((f32[4,128,128]{2,1,0:T(8,128)}, f32[4,128,128]{2,1,0:T(8,128)S(1)}, u32[]{:S(2)}, u32[]{:S(2)}) %collective-permute-start.2) | collective-permute-done | bytes 262176 | tf_op jit(solution)/shard_map/ppermute | solution.py:459
  117.2 6.7 %collective-permute-done.5 = f32[4,128,128]{2,1,0:T(8,128)} collective-permute-done((f32[4,128,128]{2,1,0:T(8,128)}, f32[4,128,128]{2,1,0:T(8,128)}, u32[]{:S(2)}, u32[]{:S(2)}) %collective-permute-start.5) | collective-permute-done | bytes 262176 | tf_op jit(solution)/shard_map/ppermute | solution.py:459
  124.0 3.6 %collective-permute-done.6 = f32[4,128,128]{2,1,0:T(8,128)} collective-permute-done((f32[4,128,128]{2,1,0:T(8,128)}, f32[4,128,128]{2,1,0:T(8,128)}, u32[]{:S(2)}, u32[]{:S(2)}) %collective-permute-start.6) | collective-permute-done | bytes 262176 | tf_op jit(solution)/shard_map/ppermute | solution.py:459
  127.6 11.5 %shard_map.39 = f32[32,2,128,128]{3,2,1,0:T(8,128)S(1)} custom-call(s32[1]{0:T(128)} %bitcast.refs_0_, f32[2,128,32]{2,1,0:T(8,128)S(1)} %copy-done.4, f32[256,256]{1,0:T(8,128)S(1)} %copy-done.3, f32[32,2,128,128]{3,2,1,0:T(8,128)} %all-to-all-done.1.refs_3_, f32[512,128]{1,0:T(8,128)S(1)} %bitcast.12, f32[512,128]{1,0:T(8,128)S(1)} %bitcast.13, ...), custom_call_target="tpu_custom_call" | custom-call | tf_op jit(solution)/shard_map/pallas_call | solution.py:375
  139.0 56.0 %all_to_all.20.in_ref = f32[32,2,128,128]{3,2,1,0:T(8,128)S(1)} all-to-all(f32[32,2,128,128]{3,2,1,0:T(8,128)S(1)} %shard_map.39), channel_id=1, replica_groups=mesh['xl'=2,'y'=4,'z'=8,'xh'=2,'c'=2] {'xl','y','xh','c'}, dimensions={0} | all-to-all | bytes 8388608 | tf_op jit(solution)/shard_map/all_to_all | solution.py:485
  195.1 4.9 %shard_map.40 = f32[128,4096]{1,0:T(8,128)S(1)} custom-call(f32[32,2,128,128]{3,2,1,0:T(8,128)S(1)} %all_to_all.20.in_ref, f32[2,128,4096]{2,1,0:T(8,128)S(1)} %copy-done.2, f32[2,32,128]{2,1,0:T(8,128)S(1)} %copy-done.5, f32[256,256]{1,0:T(8,128)S(1)} %copy-done.3), custom_call_target="tpu_custom_call" | custom-call | tf_op jit(solution)/shard_map/pallas_call | solution.py:375
  200.0 1.3 copy-done.1
  201.3 0.0 reduce-scatter.2.cloned.1.call-update
  201.3 40.2 %reduce-scatter.2.cloned.1.call-done = f32[16,4096]{1,0:T(8,128)} async-done(((f32[128,4096]{1,0:T(8,128)}), f32[16,4096]{1,0:T(8,128)}) %reduce-scatter.2.cloned.1.call-update) | async-done | bytes 262160 | tf_op jit(solution)/shard_map/reduce_scatter | solution.py:495
  241.5 1.1 broadcast_in_dim.10
  242.7 27.5 %all_to_all.21 = f32[8,16,4096]{2,1,0:T(8,128)S(1)} all-to-all(f32[8,16,4096]{2,1,0:T(8,128)S(1)} %broadcast_in_dim.10), channel_id=1, replica_groups=mesh['xl'=2,'y'=4,'z'=8,'xh'=2,'c'=2] {'xl','y'}, dimensions={0} | all-to-all | bytes 4194304 | tf_op jit(solution)/shard_map/all_to_all | solution.py:497
  270.2 1.3 copy.6
  (17 shorter events, 0.0 us)
Async XLA Ops:
  6.5 1.6 copy-start
  6.5 46.8 %all-gather.2.cloned.1.call-start = ((), (), s32[]{:S(2)}) async-start(), calls=%async_computation.5 | async-start | bytes 2359296 | tf_op jit(solution)/shard_map/all_gather | solution.py:406
  14.2 34.9 %all-to-all-start = ((f32[32,136,128]{2,1,0:T(8,128)}), f32[32,136,128]{2,1,0:T(8,128)}, u32[]{:S(2)}, u32[]{:S(2)}) async-start(f32[32,136,128]{2,1,0:T(8,128)} %shard_map.37), calls=%async_computation | async-start | bytes 4456448 | tf_op jit(solution)/shard_map/all_to_all | solution.py:416
  64.9 8.9 %copy-start.6 = (f32[4,128,128]{2,1,0:T(8,128)S(1)}, f32[4,128,128]{2,1,0:T(8,128)}, u32[]{:S(2)}) copy-start(f32[4,128,128]{2,1,0:T(8,128)} %get-tuple-element.25) | copy-start | bytes 786436
  64.9 62.7 %copy-start.3 = (f32[256,256]{1,0:T(8,128)S(1)}, f32[256,256]{1,0:T(8,128)}, u32[]{:S(2)}) copy-start(f32[256,256]{1,0:T(8,128)} %get-tuple-element.22.refs_2_.dft_ref) | copy-start | bytes 786436
  64.9 62.6 %copy-start.4 = (f32[2,128,32]{2,1,0:T(8,128)S(1)}, f32[2,128,32]{2,1,0:T(8,128)}, u32[]{:S(2)}) copy-start(f32[2,128,32]{2,1,0:T(8,128)} %get-tuple-element.21.refs_1_) | copy-start | bytes 98308
  64.9 62.6 %all-to-all-start.1 = ((f32[32,2,128,128]{3,2,1,0:T(8,128)}), f32[32,2,128,128]{3,2,1,0:T(8,128)}, u32[]{:S(2)}, u32[]{:S(2)}) async-start(f32[32,2,128,128]{3,2,1,0:T(8,128)} %get-tuple-element.23), calls=%async_computation.1 | async-start | bytes 8388608 | tf_op jit(solution)/shard_map/all_to_all | solution.py:462
  72.6 169.0 %reduce-scatter.2.cloned.1.call-start = ((), (), s32[]{:S(2)}) async-start(), calls=%async_computation.6 | async-start | bytes 2359296 | tf_op jit(solution)/shard_map/reduce_scatter | solution.py:495
  72.6 12.4 %collective-permute-start = (f32[4,128,128]{2,1,0:T(8,128)}, f32[4,128,128]{2,1,0:T(8,128)S(1)}, u32[]{:S(2)}, u32[]{:S(2)}) collective-permute-start(f32[4,128,128]{2,1,0:T(8,128)} %get-tuple-element.24), channel_id=1, source_target_pairs={{0,4},{4,8},{8,12},{12,16},{16,20},{20,24},{24,28},{28,0},{1,5},{5... | collective-permute-start | bytes 786440 | tf_op jit(solution)/shard_map/ppermute | solution.py:459
  73.8 23.7 %collective-permute-start.1 = (f32[4,128,128]{2,1,0:T(8,128)S(1)}, f32[4,128,128]{2,1,0:T(8,128)S(1)}, u32[]{:S(2)}, u32[]{:S(2)}) collective-permute-start(f32[4,128,128]{2,1,0:T(8,128)S(1)} %copy-done.6), channel_id=1, source_target_pairs={{0,8},{4,12},{8,16},{12,20},{16,24},{20,28},{24,0},{28,4},{1,9},{5... | collective-permute-start | bytes 786440 | tf_op jit(solution)/shard_map/ppermute | solution.py:459
  75.8 41.4 %collective-permute-start.2 = (f32[4,128,128]{2,1,0:T(8,128)}, f32[4,128,128]{2,1,0:T(8,128)S(1)}, u32[]{:S(2)}, u32[]{:S(2)}) collective-permute-start(f32[4,128,128]{2,1,0:T(8,128)} %get-tuple-element.26), channel_id=1, source_target_pairs={{0,12},{4,16},{8,20},{12,24},{16,28},{20,0},{24,4},{28,8},{1,13},{... | collective-permute-start | bytes 786440 | tf_op jit(solution)/shard_map/ppermute | solution.py:459
  79.5 37.7 %collective-permute-start.3 = (f32[4,128,128]{2,1,0:T(8,128)}, f32[4,128,128]{2,1,0:T(8,128)}, u32[]{:S(2)}, u32[]{:S(2)}) collective-permute-start(f32[4,128,128]{2,1,0:T(8,128)} %get-tuple-element.27), channel_id=1, source_target_pairs={{0,16},{4,20},{8,24},{12,28},{16,0},{20,4},{24,8},{28,12},{1,17},{... | collective-permute-start | bytes 786440 | tf_op jit(solution)/shard_map/ppermute | solution.py:459
  80.4 36.9 %collective-permute-start.4 = (f32[4,128,128]{2,1,0:T(8,128)}, f32[4,128,128]{2,1,0:T(8,128)}, u32[]{:S(2)}, u32[]{:S(2)}) collective-permute-start(f32[4,128,128]{2,1,0:T(8,128)} %get-tuple-element.28), channel_id=1, source_target_pairs={{0,20},{4,24},{8,28},{12,0},{16,4},{20,8},{24,12},{28,16},{1,21},{... | collective-permute-start | bytes 786440 | tf_op jit(solution)/shard_map/ppermute | solution.py:459
  85.0 39.0 %collective-permute-start.5 = (f32[4,128,128]{2,1,0:T(8,128)}, f32[4,128,128]{2,1,0:T(8,128)}, u32[]{:S(2)}, u32[]{:S(2)}) collective-permute-start(f32[4,128,128]{2,1,0:T(8,128)} %get-tuple-element.29), channel_id=1, source_target_pairs={{0,24},{4,28},{8,0},{12,4},{16,8},{20,12},{24,16},{28,20},{1,25},{... | collective-permute-start | bytes 786440 | tf_op jit(solution)/shard_map/ppermute | solution.py:459
  97.4 30.1 %collective-permute-start.6 = (f32[4,128,128]{2,1,0:T(8,128)}, f32[4,128,128]{2,1,0:T(8,128)}, u32[]{:S(2)}, u32[]{:S(2)}) collective-permute-start(f32[4,128,128]{2,1,0:T(8,128)} %get-tuple-element.30), channel_id=1, source_target_pairs={{0,28},{4,0},{8,4},{12,8},{16,12},{20,16},{24,20},{28,24},{1,29},{... | collective-permute-start | bytes 786440 | tf_op jit(solution)/shard_map/ppermute | solution.py:459
  139.0 56.0 %copy-start.2 = (f32[2,128,4096]{2,1,0:T(8,128)S(1)}, f32[2,128,4096]{2,1,0:T(8,128)}, u32[]{:S(2)}) copy-start(f32[2,128,4096]{2,1,0:T(8,128)} %get-tuple-element.31.wave_ref) | copy-start | bytes 12582916
  139.0 56.0 %copy-start.5 = (f32[2,32,128]{2,1,0:T(8,128)S(1)}, f32[2,32,128]{2,1,0:T(8,128)}, u32[]{:S(2)}) copy-start(f32[2,32,128]{2,1,0:T(8,128)} %get-tuple-element.32.tw_ref) | copy-start | bytes 98308
  200.0 1.3 copy-start.1
Sparse Core Ops, SparseCore 0:
  9.1 44.1 all-gather.1
  201.5 40.0 reduce-scatter.1

commit v9 on v8

--- a/solution.py
+++ b/solution.py
@@ -342,17 +342,17 @@
     high_ref[...], low_ref[...] = split(transposed(dft_ref))
 
     def multiply(step, carry):
-        group = pl.ds(step * 4, 4)
-        both = jnp.concatenate([in_ref[group, 0], in_ref[group, 1]], axis=-1).reshape(4 * INNER, 2 * INNER)
+        group = pl.ds(step * 8, 8)
+        both = jnp.concatenate([in_ref[group, 0], in_ref[group, 1]], axis=-1).reshape(8 * INNER, 2 * INNER)
         high, low = split(both)
         out = dot(
             jnp.concatenate([high, low, high], axis=1),
             jnp.concatenate([high_ref[...], high_ref[...], low_ref[...]], axis=0),
         )
-        back_ref[group] = out.reshape(4, INNER, 2 * INNER)
-        return carry
-
-    lax.fori_loop(0, OUTER // 4, multiply, 0)
+        back_ref[group] = out.reshape(8, INNER, 2 * INNER)
+        return carry
+
+    lax.fori_loop(0, OUTER // 8, multiply, 0)
 
     def block(step, carry):
         rows = row_block(step)

time: 279 us -> 278 us (level)
  no operation moved by 1% of the time
where the time goes in v9:
time: 278 us
  waiting for transfers between devices  106 us (38%)
  blocking collectives  83.8 us (30%)
  starting transfers between devices  34.6 us (12%)
  Pallas kernels  32 us (12%)
  between operations  14.2 us (5%)
  local copies, waits for them, and re-layouts  7.08 us (3%)
    all_to_all x1, blocking collectives, on_device(): spectrum = lax.all_to_all(spectrum, SLAB, 0, 0, tiled=True)  56 us
    reduce_scatter x1, waiting for transfers between devices, on_device(): part = lax.psum_scatter(part, 'z', scatter_dimension=0, tiled=True)  40.2 us
    ppermute x7, waiting for transfers between devices, on_device(): lax.ppermute(piece, 'z', [(i, (i + k) % layers) for i in range(layers)])  34.7 us
    pallas_call x4, Pallas kernels, call(): pl.pallas_call(kernel, out_shape=[jax.ShapeDtypeStruct(shape, F32) for sh...  32 us
    all_to_all x1, blocking collectives, on_device(): lax.all_to_all(part, ('xl', 'y'), 0, 0, tiled=True)  27.8 us
    all_to_all x1, waiting for transfers between devices, on_device(): sorted_targets = lax.all_to_all(sorted_targets, SLAB, 0, 0, tiled=True)  26.7 us
    ppermute x7, starting transfers between devices, on_device(): lax.ppermute(piece, 'z', [(i, (i + k) % layers) for i in range(layers)])  19.2 us
    all_to_all x1, starting transfers between devices, on_device(): sorted_targets = lax.all_to_all(sorted_targets, SLAB, 0, 0, tiled=True)  7.64 us
  transfers between devices with their start and end apart: 11, of which 7 were waited for; matrix products, arithmetic and copies ran while one was open for 1% of the time, Pallas kernels for 2%

profile of v9, /device:TPU:4, one launch (start us, length us, event | category | flops | bytes accessed | tf_op | source)
XLA Modules:
  0.0 278.0 jit_solution(16425658617486143828)
XLA Ops:
  6.5 1.6 copy-done
  8.1 0.7 constant_dynamic-slice_fusion.1
  8.8 0.0 all-gather.2.cloned.1.call-update
  9.5 4.7 %shard_map.37 = f32[32,136,128]{2,1,0:T(8,128)} custom-call(s32[1]{0:T(128)S(6)} %copy.5.depth_ref, f32[128,4096]{1,0:T(8,128)} %bitcast.17), custom_call_target="tpu_custom_call" | custom-call | tf_op jit(solution)/shard_map/pallas_call | solution.py:375
  14.2 7.6 %all-to-all-start = ((f32[32,136,128]{2,1,0:T(8,128)}), f32[32,136,128]{2,1,0:T(8,128)}, u32[]{:S(2)}, u32[]{:S(2)}) async-start(f32[32,136,128]{2,1,0:T(8,128)} %shard_map.37), calls=%async_computation | async-start | bytes 4456448 | tf_op jit(solution)/shard_map/all_to_all | solution.py:416
  21.9 0.6 pad_add_fusion.place_ref
  22.5 26.7 %all-to-all-done.targets_hbm = f32[32,136,128]{2,1,0:T(8,128)} async-done(((f32[32,136,128]{2,1,0:T(8,128)}), f32[32,136,128]{2,1,0:T(8,128)}, u32[]{:S(2)}, u32[]{:S(2)}) %all-to-all-start) | async-done | bytes 2228256 | tf_op jit(solution)/shard_map/all_to_all | solution.py:416
  49.2 4.1 %all-gather.2.cloned.1.call-done.phase_ref = f32[128,4096]{1,0:T(8,128)} async-done(((f32[16,4096]{1,0:T(8,128)}), f32[128,4096]{1,0:T(8,128)}) %all-gather.2.cloned.1.call-update) | async-done | bytes 2097168 | tf_op jit(solution)/shard_map/all_gather | solution.py:406
  53.3 11.5 %shard_map.38 = (f32[32,2,128,128]{3,2,1,0:T(8,128)}, f32[2,128,4096]{2,1,0:T(8,128)}, f32[2,32,128]{2,1,0:T(8,128)}, f32[2,128,32]{2,1,0:T(8,128)}, f32[256,256...) custom-call(s32[2]{0:T(128)} %pad_add_fusion.place_ref, ...), custom_call_target="tpu_custom_call" | custom-call | tf_op jit(solution)/shard_map/pallas_call | solution.py:375
  64.9 7.6 %all-to-all-start.1 = ((f32[32,2,128,128]{3,2,1,0:T(8,128)}), f32[32,2,128,128]{3,2,1,0:T(8,128)}, u32[]{:S(2)}, u32[]{:S(2)}) async-start(f32[32,2,128,128]{3,2,1,0:T(8,128)} %get-tuple-element.23), calls=%async_computation.1 | async-start | bytes 8388608 | tf_op jit(solution)/shard_map/all_to_all | solution.py:462
  72.6 0.0 reduce-scatter.2.cloned.1.call-start
  72.6 1.1 collective-permute-start
  73.8 2.1 collective-permute-start.1
  75.8 3.7 %collective-permute-start.2 = (f32[4,128,128]{2,1,0:T(8,128)}, f32[4,128,128]{2,1,0:T(8,128)S(1)}, u32[]{:S(2)}, u32[]{:S(2)}) collective-permute-start(f32[4,128,128]{2,1,0:T(8,128)} %get-tuple-element.26), channel_id=1, source_target_pairs={{0,12},{4,16},{8,20},{12,24},{16,28},{20,0},{24,4},{28,8},{1,13},{... | collective-permute-start | bytes 786440 | tf_op jit(solution)/shard_map/ppermute | solution.py:459
  79.5 0.9 collective-permute-start.3
  80.4 4.6 %collective-permute-start.4 = (f32[4,128,128]{2,1,0:T(8,128)}, f32[4,128,128]{2,1,0:T(8,128)}, u32[]{:S(2)}, u32[]{:S(2)}) collective-permute-start(f32[4,128,128]{2,1,0:T(8,128)} %get-tuple-element.28), channel_id=1, source_target_pairs={{0,20},{4,24},{8,28},{12,0},{16,4},{20,8},{24,12},{28,16},{1,21},{... | collective-permute-start | bytes 786440 | tf_op jit(solution)/shard_map/ppermute | solution.py:459
  85.0 3.6 %collective-permute-start.5 = (f32[4,128,128]{2,1,0:T(8,128)}, f32[4,128,128]{2,1,0:T(8,128)}, u32[]{:S(2)}, u32[]{:S(2)}) collective-permute-start(f32[4,128,128]{2,1,0:T(8,128)} %get-tuple-element.29), channel_id=1, source_target_pairs={{0,24},{4,28},{8,0},{12,4},{16,8},{20,12},{24,16},{28,20},{1,25},{... | collective-permute-start | bytes 786440 | tf_op jit(solution)/shard_map/ppermute | solution.py:459
  88.6 8.8 %collective-permute-done.1 = f32[4,128,128]{2,1,0:T(8,128)S(1)} collective-permute-done((f32[4,128,128]{2,1,0:T(8,128)S(1)}, f32[4,128,128]{2,1,0:T(8,128)S(1)}, u32[]{:S(2)}, u32[]{:S(2)}) %collective-permute-start.1) | collective-permute-done | bytes 262176 | tf_op jit(solution)/shard_map/ppermute | solution.py:459
  97.4 3.3 %collective-permute-start.6 = (f32[4,128,128]{2,1,0:T(8,128)}, f32[4,128,128]{2,1,0:T(8,128)}, u32[]{:S(2)}, u32[]{:S(2)}) collective-permute-start(f32[4,128,128]{2,1,0:T(8,128)} %get-tuple-element.30), channel_id=1, source_target_pairs={{0,28},{4,0},{8,4},{12,8},{16,12},{20,16},{24,20},{28,24},{1,29},{... | collective-permute-start | bytes 786440 | tf_op jit(solution)/shard_map/ppermute | solution.py:459
  100.7 1.0 constant_dynamic-slice_fusion
  101.7 15.6 %collective-permute-done.2 = f32[4,128,128]{2,1,0:T(8,128)S(1)} collective-permute-done((f32[4,128,128]{2,1,0:T(8,128)}, f32[4,128,128]{2,1,0:T(8,128)S(1)}, u32[]{:S(2)}, u32[]{:S(2)}) %collective-permute-start.2) | collective-permute-done | bytes 262176 | tf_op jit(solution)/shard_map/ppermute | solution.py:459
  117.2 6.7 %collective-permute-done.5 = f32[4,128,128]{2,1,0:T(8,128)} collective-permute-done((f32[4,128,128]{2,1,0:T(8,128)}, f32[4,128,128]{2,1,0:T(8,128)}, u32[]{:S(2)}, u32[]{:S(2)}) %collective-permute-start.5) | collective-permute-done | bytes 262176 | tf_op jit(solution)/shard_map/ppermute | solution.py:459
  124.0 3.6 %collective-permute-done.6 = f32[4,128,128]{2,1,0:T(8,128)} collective-permute-done((f32[4,128,128]{2,1,0:T(8,128)}, f32[4,128,128]{2,1,0:T(8,128)}, u32[]{:S(2)}, u32[]{:S(2)}) %collective-permute-start.6) | collective-permute-done | bytes 262176 | tf_op jit(solution)/shard_map/ppermute | solution.py:459
  127.6 11.5 %shard_map.39 = f32[32,2,128,128]{3,2,1,0:T(8,128)S(1)} custom-call(s32[1]{0:T(128)} %bitcast.refs_0_, f32[2,128,32]{2,1,0:T(8,128)S(1)} %copy-done.4, f32[256,256]{1,0:T(8,128)S(1)} %copy-done.3, f32[32,2,128,128]{3,2,1,0:T(8,128)} %all-to-all-done.1.refs_3_, f32[512,128]{1,0:T(8,128)S(1)} %bitcast.12, f32[512,128]{1,0:T(8,128)S(1)} %bitcast.13, ...), custom_call_target="tpu_custom_call" | custom-call | tf_op jit(solution)/shard_map/pallas_call | solution.py:375
  139.0 56.0 %all_to_all.20.in_ref = f32[32,2,128,128]{3,2,1,0:T(8,128)S(1)} all-to-all(f32[32,2,128,128]{3,2,1,0:T(8,128)S(1)} %shard_map.39), channel_id=1, replica_groups=mesh['xl'=2,'y'=4,'z'=8,'xh'=2,'c'=2] {'xl','y','xh','c'}, dimensions={0} | all-to-all | bytes 8388608 | tf_op jit(solution)/shard_map/all_to_all | solution.py:485
  195.1 4.3 %shard_map.40 = f32[128,4096]{1,0:T(8,128)S(1)} custom-call(f32[32,2,128,128]{3,2,1,0:T(8,128)S(1)} %all_to_all.20.in_ref, f32[2,128,4096]{2,1,0:T(8,128)S(1)} %copy-done.2, f32[2,32,128]{2,1,0:T(8,128)S(1)} %copy-done.5, f32[256,256]{1,0:T(8,128)S(1)} %copy-done.3), custom_call_target="tpu_custom_call" | custom-call | tf_op jit(solution)/shard_map/pallas_call | solution.py:375
  199.4 1.3 copy-done.1
  200.7 0.0 reduce-scatter.2.cloned.1.call-update
  200.7 40.2 %reduce-scatter.2.cloned.1.call-done = f32[16,4096]{1,0:T(8,128)} async-done(((f32[128,4096]{1,0:T(8,128)}), f32[16,4096]{1,0:T(8,128)}) %reduce-scatter.2.cloned.1.call-update) | async-done | bytes 262160 | tf_op jit(solution)/shard_map/reduce_scatter | solution.py:495
  240.9 1.1 broadcast_in_dim.10
  242.0 27.8 %all_to_all.21 = f32[8,16,4096]{2,1,0:T(8,128)S(1)} all-to-all(f32[8,16,4096]{2,1,0:T(8,128)S(1)} %broadcast_in_dim.10), channel_id=1, replica_groups=mesh['xl'=2,'y'=4,'z'=8,'xh'=2,'c'=2] {'xl','y'}, dimensions={0} | all-to-all | bytes 4194304 | tf_op jit(solution)/shard_map/all_to_all | solution.py:497
  269.9 1.3 copy.6
  (17 shorter events, 0.0 us)
Async XLA Ops:
  6.5 1.6 copy-start
  6.5 46.8 %all-gather.2.cloned.1.call-start = ((), (), s32[]{:S(2)}) async-start(), calls=%async_computation.5 | async-start | bytes 2359296 | tf_op jit(solution)/shard_map/all_gather | solution.py:406
  14.2 34.9 %all-to-all-start = ((f32[32,136,128]{2,1,0:T(8,128)}), f32[32,136,128]{2,1,0:T(8,128)}, u32[]{:S(2)}, u32[]{:S(2)}) async-start(f32[32,136,128]{2,1,0:T(8,128)} %shard_map.37), calls=%async_computation | async-start | bytes 4456448 | tf_op jit(solution)/shard_map/all_to_all | solution.py:416
  64.9 8.9 %copy-start.6 = (f32[4,128,128]{2,1,0:T(8,128)S(1)}, f32[4,128,128]{2,1,0:T(8,128)}, u32[]{:S(2)}) copy-start(f32[4,128,128]{2,1,0:T(8,128)} %get-tuple-element.25) | copy-start | bytes 786436
  64.9 62.7 %copy-start.3 = (f32[256,256]{1,0:T(8,128)S(1)}, f32[256,256]{1,0:T(8,128)}, u32[]{:S(2)}) copy-start(f32[256,256]{1,0:T(8,128)} %get-tuple-element.22.refs_2_.dft_ref) | copy-start | bytes 786436
  64.9 62.6 %copy-start.4 = (f32[2,128,32]{2,1,0:T(8,128)S(1)}, f32[2,128,32]{2,1,0:T(8,128)}, u32[]{:S(2)}) copy-start(f32[2,128,32]{2,1,0:T(8,128)} %get-tuple-element.21.refs_1_) | copy-start | bytes 98308
  64.9 62.6 %all-to-all-start.1 = ((f32[32,2,128,128]{3,2,1,0:T(8,128)}), f32[32,2,128,128]{3,2,1,0:T(8,128)}, u32[]{:S(2)}, u32[]{:S(2)}) async-start(f32[32,2,128,128]{3,2,1,0:T(8,128)} %get-tuple-element.23), calls=%async_computation.1 | async-start | bytes 8388608 | tf_op jit(solution)/shard_map/all_to_all | solution.py:462
  72.6 168.3 %reduce-scatter.2.cloned.1.call-start = ((), (), s32[]{:S(2)}) async-start(), calls=%async_computation.6 | async-start | bytes 2359296 | tf_op jit(solution)/shard_map/reduce_scatter | solution.py:495
  72.6 12.4 %collective-permute-start = (f32[4,128,128]{2,1,0:T(8,128)}, f32[4,128,128]{2,1,0:T(8,128)S(1)}, u32[]{:S(2)}, u32[]{:S(2)}) collective-permute-start(f32[4,128,128]{2,1,0:T(8,128)} %get-tuple-element.24), channel_id=1, source_target_pairs={{0,4},{4,8},{8,12},{12,16},{16,20},{20,24},{24,28},{28,0},{1,5},{5... | collective-permute-start | bytes 786440 | tf_op jit(solution)/shard_map/ppermute | solution.py:459
  73.8 23.7 %collective-permute-start.1 = (f32[4,128,128]{2,1,0:T(8,128)S(1)}, f32[4,128,128]{2,1,0:T(8,128)S(1)}, u32[]{:S(2)}, u32[]{:S(2)}) collective-permute-start(f32[4,128,128]{2,1,0:T(8,128)S(1)} %copy-done.6), channel_id=1, source_target_pairs={{0,8},{4,12},{8,16},{12,20},{16,24},{20,28},{24,0},{28,4},{1,9},{5... | collective-permute-start | bytes 786440 | tf_op jit(solution)/shard_map/ppermute | solution.py:459
  75.8 41.4 %collective-permute-start.2 = (f32[4,128,128]{2,1,0:T(8,128)}, f32[4,128,128]{2,1,0:T(8,128)S(1)}, u32[]{:S(2)}, u32[]{:S(2)}) collective-permute-start(f32[4,128,128]{2,1,0:T(8,128)} %get-tuple-element.26), channel_id=1, source_target_pairs={{0,12},{4,16},{8,20},{12,24},{16,28},{20,0},{24,4},{28,8},{1,13},{... | collective-permute-start | bytes 786440 | tf_op jit(solution)/shard_map/ppermute | solution.py:459
  79.5 37.7 %collective-permute-start.3 = (f32[4,128,128]{2,1,0:T(8,128)}, f32[4,128,128]{2,1,0:T(8,128)}, u32[]{:S(2)}, u32[]{:S(2)}) collective-permute-start(f32[4,128,128]{2,1,0:T(8,128)} %get-tuple-element.27), channel_id=1, source_target_pairs={{0,16},{4,20},{8,24},{12,28},{16,0},{20,4},{24,8},{28,12},{1,17},{... | collective-permute-start | bytes 786440 | tf_op jit(solution)/shard_map/ppermute | solution.py:459
  80.4 36.9 %collective-permute-start.4 = (f32[4,128,128]{2,1,0:T(8,128)}, f32[4,128,128]{2,1,0:T(8,128)}, u32[]{:S(2)}, u32[]{:S(2)}) collective-permute-start(f32[4,128,128]{2,1,0:T(8,128)} %get-tuple-element.28), channel_id=1, source_target_pairs={{0,20},{4,24},{8,28},{12,0},{16,4},{20,8},{24,12},{28,16},{1,21},{... | collective-permute-start | bytes 786440 | tf_op jit(solution)/shard_map/ppermute | solution.py:459
  85.0 39.0 %collective-permute-start.5 = (f32[4,128,128]{2,1,0:T(8,128)}, f32[4,128,128]{2,1,0:T(8,128)}, u32[]{:S(2)}, u32[]{:S(2)}) collective-permute-start(f32[4,128,128]{2,1,0:T(8,128)} %get-tuple-element.29), channel_id=1, source_target_pairs={{0,24},{4,28},{8,0},{12,4},{16,8},{20,12},{24,16},{28,20},{1,25},{... | collective-permute-start | bytes 786440 | tf_op jit(solution)/shard_map/ppermute | solution.py:459
  97.4 30.1 %collective-permute-start.6 = (f32[4,128,128]{2,1,0:T(8,128)}, f32[4,128,128]{2,1,0:T(8,128)}, u32[]{:S(2)}, u32[]{:S(2)}) collective-permute-start(f32[4,128,128]{2,1,0:T(8,128)} %get-tuple-element.30), channel_id=1, source_target_pairs={{0,28},{4,0},{8,4},{12,8},{16,12},{20,16},{24,20},{28,24},{1,29},{... | collective-permute-start | bytes 786440 | tf_op jit(solution)/shard_map/ppermute | solution.py:459
  139.0 56.0 %copy-start.2 = (f32[2,128,4096]{2,1,0:T(8,128)S(1)}, f32[2,128,4096]{2,1,0:T(8,128)}, u32[]{:S(2)}) copy-start(f32[2,128,4096]{2,1,0:T(8,128)} %get-tuple-element.31.wave_ref) | copy-start | bytes 12582916
  139.0 56.0 %copy-start.5 = (f32[2,32,128]{2,1,0:T(8,128)S(1)}, f32[2,32,128]{2,1,0:T(8,128)}, u32[]{:S(2)}) copy-start(f32[2,32,128]{2,1,0:T(8,128)} %get-tuple-element.32.tw_ref) | copy-start | bytes 98308
  199.3 1.3 copy-start.1
Sparse Core Ops, SparseCore 0:
  9.1 44.1 all-gather.1
  200.8 40.0 reduce-scatter.1
